TPU v7x, 32 devices: a whole 2x2x4 slice. The times are simulated.
32 devices in a mesh: fsdp: 8 (over y, x, core), head: 4 (over z).
Axes of the slice: x: 2, y: 2, z: 4, core: 2. Of those that a mesh axis runs over, the one named last changes fastest.
Arguments:
- tokens: bfloat16 [2, 8192, 1024], P(None, ('fsdp', 'head')), may hold values from -6 to 6
- cotangent: bfloat16 [2, 8192, 1024], P(None, ('fsdp', 'head')), may hold values from -6 to 6
- lengths: int32 [2, 8], replicated, may hold values from 1 to 4096, 8192 in all within a row
- decay_rate: float32 [8], replicated, may hold values from 7.324219e-05 to 0.03
- query_weight: bfloat16 [1024, 1024], P('fsdp'), may hold values from -0.1875 to 0.1875
- key_weight: bfloat16 [1024, 1024], P('fsdp'), may hold values from -0.1875 to 0.1875
- value_weight: bfloat16 [1024, 1024], P('fsdp'), may hold values from -0.1875 to 0.1875
- gate_weight: bfloat16 [1024, 1024], P('fsdp'), may hold values from -0.1875 to 0.1875
- out_weight: bfloat16 [1024, 1024], P('fsdp'), may hold values from -0.1875 to 0.1875
- first_weight: bfloat16 [1024, 2816], P('fsdp'), may hold values from -0.1875 to 0.1875
- second_weight: bfloat16 [1024, 2816], P('fsdp'), may hold values from -0.1875 to 0.1875
- down_weight: bfloat16 [2816, 1024], P(None, 'fsdp'), may hold values from -0.109375 to 0.109375
Outputs:
- mixed: bfloat16 [2, 8192, 1024], P(None, ('fsdp', 'head'))
- grad_tokens: bfloat16 [2, 8192, 1024], P(None, ('fsdp', 'head'))
- grad_query: float32 [1024, 1024], P(('fsdp', 'head'))
- grad_key: float32 [1024, 1024], P(('fsdp', 'head'))
- grad_value: float32 [1024, 1024], P(('fsdp', 'head'))
- grad_gate: float32 [1024, 1024], P(('fsdp', 'head'))
- grad_out: float32 [1024, 1024], P(('fsdp', 'head'))
- grad_first: float32 [1024, 2816], P(('fsdp', 'head'))
- grad_second: float32 [1024, 2816], P(('fsdp', 'head'))
- grad_down: float32 [2816, 1024], P(None, ('fsdp', 'head'))
Inputs may be any that keep to these rules, and one draw needn't show every extreme that they name: Each row holds 8 sequence lengths that sum to 8192; the largest is exactly 4096.
All inputs are finite; a program needn't handle non-finite values.
Results may differ from a plain program's by a relative error of at most 0.017.
Values may be sent and summed in bfloat16 or wider, within the bound.
A program may use at most 256 MiB of HBM per device.

v0:
```python
import math

import jax
import jax.numpy as jnp
from jax import lax
from jax.sharding import PartitionSpec as P

H = 8
DH = 128
BLOCK = 512


EPSILON = 1e-06
PRECISE = lax.Precision.HIGHEST


def prefix(shard, axis, join, neutral, backward):
    count = lax.axis_size(axis)
    place = lax.axis_index(axis)
    ahead = count - 1 - place if backward else place
    gathered = jax.tree.map(
        lambda a, kind: lax.all_gather(a.astype(kind), axis), shard, (jnp.bfloat16, jnp.bfloat16)
    )
    state = jax.tree.map(lambda a, e: jnp.zeros_like(a) + jnp.asarray(e, a.dtype), shard, neutral)

    def one(hop, state):
        source = count - 1 - hop if backward else hop
        return join(
            state,
            jax.tree.map(
                lambda a, own: lax.dynamic_index_in_dim(a, source, 0, False).astype(own.dtype),
                gathered,
                shard,
            ),
        )

    return lax.fori_loop(0, ahead, one, state)


def norm_parts(values):
    inv_scale = lax.rsqrt(jnp.mean(values * values, axis=-1, keepdims=True) + EPSILON)
    return (values * inv_scale, inv_scale)


def norm_back(gradient, normed, inv_scale):
    return inv_scale * (gradient - normed * jnp.mean(gradient * normed, axis=-1, keepdims=True))


def rotate_pairs(values, cosine, sine_vals):
    half_size = values.shape[-1] // 2
    first_half = values[..., :half_size]
    second_half = values[..., half_size:]
    return jnp.concatenate(
        [
            first_half * cosine - second_half * sine_vals,
            first_half * sine_vals + second_half * cosine,
        ],
        axis=-1,
    )


def rotation_tables(positions, head_size):
    half_size = head_size // 2
    shifts = jnp.arange(half_size, dtype=jnp.int32) * 10 // half_size
    speeds = jnp.right_shift(jnp.full((half_size,), 651, jnp.int32), shifts) + 1
    phases = positions[:, None] * speeds[None, :] % 4096
    angles = phases.astype(jnp.float32) * (2.0 * math.pi / 4096.0)
    return (jnp.cos(angles)[:, None, :], jnp.sin(angles)[:, None, :])


def segment_ids(seq_lengths, positions):
    seq_ends = jnp.cumsum(seq_lengths)
    return jnp.sum((seq_ends[None, :] <= positions[:, None]).astype(jnp.int32), axis=1)


def silu_slope(values):
    sigmoid_v = jax.nn.sigmoid(values)
    return sigmoid_v * (1.0 + values * (1.0 - sigmoid_v))


def dot_rows(left_arr, right_arr):
    return lax.dot_general(
        left_arr, right_arr, (((0,), (0,)), ((), ())), preferred_element_type=jnp.float32
    )


def dot_cols(left_arr, right_arr):
    return lax.dot_general(
        left_arr, right_arr, (((1,), (1,)), ((), ())), preferred_element_type=jnp.float32
    )


def combine_maps(earlier_map, later_map):
    return (
        earlier_map[0] * later_map[0],
        later_map[0][:, None, None] * earlier_map[1] + later_map[1],
    )


def block_mask(seg_blk, decay_here):
    row_count = seg_blk.shape[0]
    offsets = jnp.arange(row_count, dtype=jnp.float32)
    distance = offsets[:, None] - offsets[None, :]
    visible = (seg_blk[:, None] == seg_blk[None, :]) & (distance >= 0.0)
    return jnp.where(
        visible[None], jnp.exp(-decay_here[:, None, None] * jnp.maximum(distance, 0.0)[None]), 0.0
    )


def edge_terms(seg_blk, seg_before, decay_here):
    row_count = seg_blk.shape[0]
    offsets = jnp.arange(row_count, dtype=jnp.float32)
    entering = jnp.where(
        (seg_blk == seg_before)[:, None],
        jnp.exp(-decay_here[None, :] * (offsets[:, None] + 1.0)),
        0.0,
    )
    leaving = jnp.where(
        (seg_blk == seg_blk[row_count - 1])[:, None],
        jnp.exp(-decay_here[None, :] * (row_count - 1.0 - offsets)[:, None]),
        0.0,
    )
    through = jnp.where(seg_blk[row_count - 1] == seg_before, jnp.exp(-decay_here * row_count), 0.0)
    return (entering, leaving, through)


def block_befores(seg_group, seg_before, block_len):
    return jnp.concatenate(
        [jnp.reshape(seg_before, (1,)), seg_group[block_len - 1 :: block_len][:-1]]
    )


def local_forward(queries, keys_h, values_h, seg_group, seg_before, decay_here, block_len):
    group_len, head_count, head_size = queries.shape
    num_blocks = group_len // block_len

    def step_fn(carried, pieces):
        query_blk, key_blk, value_blk, seg_blk, before_blk = pieces
        within = block_mask(seg_blk, decay_here)
        entering, leaving, through = edge_terms(seg_blk, before_blk, decay_here)
        scores = (
            jnp.einsum("shd,thd->hst", query_blk, key_blk, preferred_element_type=jnp.float32)
            * within
        )
        query_wide = query_blk.astype(jnp.float32)
        key_wide = key_blk.astype(jnp.float32)
        value_wide = value_blk.astype(jnp.float32)
        result = jnp.einsum("hst,thd->shd", scores, value_wide, precision=PRECISE)
        result = result + entering[:, :, None] * jnp.einsum(
            "shd,hde->she", query_wide, carried, precision=PRECISE
        )
        updated = through[:, None, None] * carried + jnp.einsum(
            "thd,the->hde", key_wide * leaving[:, :, None], value_wide, precision=PRECISE
        )
        return (updated, (result, carried))

    zero_state = jnp.zeros((head_count, head_size, head_size), jnp.float32)
    final_state, (results, states_in) = lax.scan(
        step_fn,
        zero_state,
        (
            queries.reshape(num_blocks, block_len, head_count, head_size),
            keys_h.reshape(num_blocks, block_len, head_count, head_size),
            values_h.reshape(num_blocks, block_len, head_count, head_size),
            seg_group.reshape(num_blocks, block_len),
            block_befores(seg_group, seg_before, block_len),
        ),
    )
    return (results.reshape(group_len, head_count, head_size), states_in, final_state)


def local_backward(
    queries, keys_h, values_h, grad_heads, seg_group, seg_before, decay_here, block_len, states_in
):
    group_len, head_count, head_size = queries.shape
    num_blocks = group_len // block_len

    def step_fn(grad_state, pieces):
        query_blk, key_blk, value_blk, grad_blk, seg_blk, before_blk, state_blk = pieces
        within = block_mask(seg_blk, decay_here)
        entering, leaving, through = edge_terms(seg_blk, before_blk, decay_here)
        grad_scores = (
            jnp.einsum("shd,thd->hst", grad_blk, value_blk, preferred_element_type=jnp.float32)
            * within
        )
        scores = (
            jnp.einsum("shd,thd->hst", query_blk, key_blk, preferred_element_type=jnp.float32)
            * within
        )
        query_wide = query_blk.astype(jnp.float32)
        key_wide = key_blk.astype(jnp.float32)
        value_wide = value_blk.astype(jnp.float32)
        grad_wide = grad_blk.astype(jnp.float32)
        grad_query = jnp.einsum("hst,thd->shd", grad_scores, key_wide, precision=PRECISE)
        grad_query = grad_query + entering[:, :, None] * jnp.einsum(
            "she,hde->shd", grad_wide, state_blk, precision=PRECISE
        )
        grad_key = jnp.einsum("hst,shd->thd", grad_scores, query_wide, precision=PRECISE)
        grad_key = grad_key + leaving[:, :, None] * jnp.einsum(
            "the,hde->thd", value_wide, grad_state, precision=PRECISE
        )
        grad_value = jnp.einsum("hst,she->the", scores, grad_wide, precision=PRECISE)
        grad_value = grad_value + leaving[:, :, None] * jnp.einsum(
            "thd,hde->the", key_wide, grad_state, precision=PRECISE
        )
        earlier_grad = through[:, None, None] * grad_state + jnp.einsum(
            "shd,she->hde", query_wide * entering[:, :, None], grad_wide, precision=PRECISE
        )
        return (earlier_grad, (grad_query, grad_key, grad_value))

    zero_state = jnp.zeros((head_count, head_size, head_size), jnp.float32)
    final_grad, (grad_q, grad_k, grad_v) = lax.scan(
        step_fn,
        zero_state,
        (
            queries.reshape(num_blocks, block_len, head_count, head_size),
            keys_h.reshape(num_blocks, block_len, head_count, head_size),
            values_h.reshape(num_blocks, block_len, head_count, head_size),
            grad_heads.reshape(num_blocks, block_len, head_count, head_size),
            seg_group.reshape(num_blocks, block_len),
            block_befores(seg_group, seg_before, block_len),
            states_in,
        ),
        reverse=True,
    )
    shape_out = (group_len, head_count, head_size)
    return (grad_q.reshape(shape_out), grad_k.reshape(shape_out), grad_v.reshape(shape_out))


def local(
    tokens,
    cotangent,
    lengths,
    decay_rate,
    query_weight,
    key_weight,
    value_weight,
    gate_weight,
    out_weight,
    first_weight,
    second_weight,
    down_weight,
):
    n_group = lax.axis_size("head")
    micro_count, tok_count, model_width = tokens.shape
    heads_here = H // n_group
    group_len = tok_count * n_group
    block_len = min(BLOCK, group_len)
    fsdp_index = lax.axis_index("fsdp")
    head_index = lax.axis_index("head")
    seq_base = (fsdp_index * n_group + head_index) * tok_count
    group_base = fsdp_index * group_len
    decay_here = lax.dynamic_slice_in_dim(decay_rate, head_index * heads_here, heads_here)
    cosine, sine_vals = rotation_tables(seq_base + jnp.arange(tok_count, dtype=jnp.int32), DH)
    group_pos = group_base + jnp.arange(group_len, dtype=jnp.int32)

    def gather_all():
        return (
            lax.all_gather(query_weight, "fsdp", axis=0, tiled=True),
            lax.all_gather(key_weight, "fsdp", axis=0, tiled=True),
            lax.all_gather(value_weight, "fsdp", axis=0, tiled=True),
            lax.all_gather(gate_weight, "fsdp", axis=0, tiled=True),
            lax.all_gather(out_weight, "fsdp", axis=0, tiled=True),
            lax.all_gather(first_weight, "fsdp", axis=0, tiled=True),
            lax.all_gather(second_weight, "fsdp", axis=0, tiled=True),
            lax.all_gather(down_weight, "fsdp", axis=1, tiled=True),
        )

    mixed_list = []
    input_grads = []
    grad_totals = None
    for micro_step in range(micro_count):
        full_weights = gather_all()
        (
            query_full,
            key_full,
            value_full,
            gate_full,
            out_full,
            first_full,
            second_full,
            down_full,
        ) = full_weights
        inputs = tokens[micro_step].astype(jnp.float32)
        normed_in, scale_in = norm_parts(inputs)
        act_in = normed_in.astype(jnp.bfloat16)
        query_pre = jnp.dot(act_in, query_full, preferred_element_type=jnp.float32)
        key_pre = jnp.dot(act_in, key_full, preferred_element_type=jnp.float32)
        value_low = jnp.dot(act_in, value_full, preferred_element_type=jnp.float32).astype(
            jnp.bfloat16
        )
        gate_vals = jnp.dot(act_in, gate_full, preferred_element_type=jnp.float32)
        query_low = (
            rotate_pairs(jax.nn.silu(query_pre).reshape(tok_count, H, DH), cosine, sine_vals)
            .reshape(tok_count, model_width)
            .astype(jnp.bfloat16)
        )
        key_low = (
            rotate_pairs(jax.nn.silu(key_pre).reshape(tok_count, H, DH), cosine, sine_vals)
            .reshape(tok_count, model_width)
            .astype(jnp.bfloat16)
        )
        query_heads, key_heads, value_heads = (
            lax.all_to_all(query_low, "head", split_axis=1, concat_axis=0, tiled=True),
            lax.all_to_all(key_low, "head", split_axis=1, concat_axis=0, tiled=True),
            lax.all_to_all(value_low, "head", split_axis=1, concat_axis=0, tiled=True),
        )
        query_hb = query_heads.reshape(group_len, heads_here, DH)
        key_hb = key_heads.reshape(group_len, heads_here, DH)
        value_hb = value_heads.reshape(group_len, heads_here, DH)
        seg_group = segment_ids(lengths[micro_step], group_pos)
        seg_before = segment_ids(lengths[micro_step], jnp.reshape(group_base - 1, (1,)))[0]
        entering_g, leaving_g, through_g = edge_terms(seg_group, seg_before, decay_here)
        local_out, states_in, local_end = local_forward(
            query_hb, key_hb, value_hb, seg_group, seg_before, decay_here, block_len
        )
        chain_in = prefix(
            (through_g, local_end),
            "fsdp",
            combine_maps,
            (jnp.ones_like(through_g), jnp.zeros_like(local_end)),
            False,
        )[1]
        attended = local_out + entering_g[:, :, None] * jnp.einsum(
            "shd,hde->she", query_hb.astype(jnp.float32), chain_in, precision=PRECISE
        )
        att_tokens = lax.all_to_all(
            attended.reshape(group_len, heads_here * DH).astype(jnp.bfloat16),
            "head",
            split_axis=0,
            concat_axis=1,
            tiled=True,
        )
        normed_att, scale_att = norm_parts(att_tokens.astype(jnp.float32))
        gated = (normed_att * gate_vals).astype(jnp.bfloat16)
        hidden = inputs + jnp.dot(gated, out_full, preferred_element_type=jnp.float32)
        normed_mid, scale_mid = norm_parts(hidden)
        act_mid = normed_mid.astype(jnp.bfloat16)
        first_pre = jnp.dot(act_mid, first_full, preferred_element_type=jnp.float32)
        second_pre = jnp.dot(act_mid, second_full, preferred_element_type=jnp.float32)
        product = (first_pre * second_pre).astype(jnp.bfloat16)
        result = hidden + jnp.dot(product, down_full, preferred_element_type=jnp.float32)
        mixed_list.append(result.astype(jnp.bfloat16))
        full_weights = gather_all()
        (
            query_full,
            key_full,
            value_full,
            gate_full,
            out_full,
            first_full,
            second_full,
            down_full,
        ) = full_weights
        grad_low = cotangent[micro_step]
        grad_res = grad_low.astype(jnp.float32)
        grad_down = dot_rows(product, grad_low)
        grad_prod = dot_cols(grad_low, down_full)
        grad_first_pre = (grad_prod * second_pre).astype(jnp.bfloat16)
        grad_second_pre = (grad_prod * first_pre).astype(jnp.bfloat16)
        grad_first = dot_rows(act_mid, grad_first_pre)
        grad_second = dot_rows(act_mid, grad_second_pre)
        grad_mid = dot_cols(grad_first_pre, first_full) + dot_cols(grad_second_pre, second_full)
        grad_hidden = grad_res + norm_back(grad_mid, normed_mid, scale_mid)
        grad_hidden_low = grad_hidden.astype(jnp.bfloat16)
        grad_out = dot_rows(gated, grad_hidden_low)
        grad_gated = dot_cols(grad_hidden_low, out_full)
        grad_gate_low = (grad_gated * normed_att).astype(jnp.bfloat16)
        grad_att = norm_back(grad_gated * gate_vals, normed_att, scale_att).astype(jnp.bfloat16)
        grad_hb = lax.all_to_all(grad_att, "head", split_axis=1, concat_axis=0, tiled=True).reshape(
            group_len, heads_here, DH
        )
        grad_wide = grad_hb.astype(jnp.float32)
        query_wide = query_hb.astype(jnp.float32)
        chain_term = jnp.einsum(
            "shd,she->hde", query_wide * entering_g[:, :, None], grad_wide, precision=PRECISE
        )
        grad_end = prefix(
            (through_g, chain_term),
            "fsdp",
            combine_maps,
            (jnp.ones_like(through_g), jnp.zeros_like(chain_term)),
            True,
        )[1]
        grad_q, grad_k, grad_v = local_backward(
            query_hb,
            key_hb,
            value_hb,
            grad_hb,
            seg_group,
            seg_before,
            decay_here,
            block_len,
            states_in,
        )
        grad_q = grad_q + entering_g[:, :, None] * jnp.einsum(
            "she,hde->shd", grad_wide, chain_in, precision=PRECISE
        )
        grad_k = grad_k + leaving_g[:, :, None] * jnp.einsum(
            "the,hde->thd", value_hb.astype(jnp.float32), grad_end, precision=PRECISE
        )
        grad_v = grad_v + leaving_g[:, :, None] * jnp.einsum(
            "thd,hde->the", key_hb.astype(jnp.float32), grad_end, precision=PRECISE
        )
        back_query, back_key, back_value = (
            lax.all_to_all(
                grad_q.reshape(group_len, heads_here * DH).astype(jnp.bfloat16),
                "head",
                split_axis=0,
                concat_axis=1,
                tiled=True,
            ),
            lax.all_to_all(
                grad_k.reshape(group_len, heads_here * DH).astype(jnp.bfloat16),
                "head",
                split_axis=0,
                concat_axis=1,
                tiled=True,
            ),
            lax.all_to_all(
                grad_v.reshape(group_len, heads_here * DH).astype(jnp.bfloat16),
                "head",
                split_axis=0,
                concat_axis=1,
                tiled=True,
            ),
        )
        grad_query_pre = (
            silu_slope(query_pre)
            * rotate_pairs(
                back_query.astype(jnp.float32).reshape(tok_count, H, DH), cosine, -sine_vals
            ).reshape(tok_count, model_width)
        ).astype(jnp.bfloat16)
        grad_key_pre = (
            silu_slope(key_pre)
            * rotate_pairs(
                back_key.astype(jnp.float32).reshape(tok_count, H, DH), cosine, -sine_vals
            ).reshape(tok_count, model_width)
        ).astype(jnp.bfloat16)
        grad_query = dot_rows(act_in, grad_query_pre)
        grad_key = dot_rows(act_in, grad_key_pre)
        grad_value = dot_rows(act_in, back_value)
        grad_gate = dot_rows(act_in, grad_gate_low)
        grad_act = (
            dot_cols(grad_query_pre, query_full)
            + dot_cols(grad_key_pre, key_full)
            + dot_cols(back_value, value_full)
            + dot_cols(grad_gate_low, gate_full)
        )
        input_grads.append(
            (grad_hidden + norm_back(grad_act, normed_in, scale_in)).astype(jnp.bfloat16)
        )
        grad_terms = (
            grad_query,
            grad_key,
            grad_value,
            grad_gate,
            grad_out,
            grad_first,
            grad_second,
            grad_down,
        )
        grad_totals = (
            grad_terms
            if grad_totals is None
            else tuple((total + term for total, term in zip(grad_totals, grad_terms)))
        )
    shares = (
        lax.psum_scatter(grad_totals[0], ("fsdp", "head"), scatter_dimension=0, tiled=True),
        lax.psum_scatter(grad_totals[1], ("fsdp", "head"), scatter_dimension=0, tiled=True),
        lax.psum_scatter(grad_totals[2], ("fsdp", "head"), scatter_dimension=0, tiled=True),
        lax.psum_scatter(grad_totals[3], ("fsdp", "head"), scatter_dimension=0, tiled=True),
        lax.psum_scatter(grad_totals[4], ("fsdp", "head"), scatter_dimension=0, tiled=True),
        lax.psum_scatter(grad_totals[5], ("fsdp", "head"), scatter_dimension=0, tiled=True),
        lax.psum_scatter(grad_totals[6], ("fsdp", "head"), scatter_dimension=0, tiled=True),
        lax.psum_scatter(grad_totals[7], ("fsdp", "head"), scatter_dimension=1, tiled=True),
    )
    return (
        jnp.stack(mixed_list),
        jnp.stack(input_grads),
        shares[0],
        shares[1],
        shares[2],
        shares[3],
        shares[4],
        shares[5],
        shares[6],
        shares[7],
    )


def solution(mesh):
    in_specs = (
        P(None, ("fsdp", "head"), None),
        P(None, ("fsdp", "head"), None),
        P(),
        P(),
        P("fsdp", None),
        P("fsdp", None),
        P("fsdp", None),
        P("fsdp", None),
        P("fsdp", None),
        P("fsdp", None),
        P("fsdp", None),
        P(None, "fsdp"),
    )
    out_specs = (
        P(None, ("fsdp", "head"), None),
        P(None, ("fsdp", "head"), None),
        P(("fsdp", "head"), None),
        P(("fsdp", "head"), None),
        P(("fsdp", "head"), None),
        P(("fsdp", "head"), None),
        P(("fsdp", "head"), None),
        P(("fsdp", "head"), None),
        P(("fsdp", "head"), None),
        P(None, ("fsdp", "head")),
    )
    return jax.shard_map(local, mesh=mesh, in_specs=in_specs, out_specs=out_specs, check_vma=False)
```

profile of v0, /device:TPU:0, one launch (start us, length us, event | category | flops | bytes accessed | tf_op | source)
XLA Modules:
  0.0 1976.7 jit_solution(10994626592373391438)
XLA Ops:
  13.2 27.3 %all-gather.19.cloned.1.call-done = bf16[1024,1024]{1,0:T(8,128)(2,1)} async-done(((bf16[128,1024]{1,0:T(8,128)(2,1)}), bf16[1024,1024]{1,0:T(8,128)(2,1)}) %all-gather.19.cloned.1.call-update) | async-done | bytes 2097168 | tf_op jit(solution)/shard_map/all_gather | solution.py:259
  45.2 25.2 %all-gather.15.cloned.1.call-done = bf16[1024,1024]{1,0:T(8,128)(2,1)} async-done(((bf16[128,1024]{1,0:T(8,128)(2,1)}), bf16[1024,1024]{1,0:T(8,128)(2,1)}) %all-gather.15.cloned.1.call-update) | async-done | bytes 2097168 | tf_op jit(solution)/shard_map/all_gather | solution.py:260
  90.4 4.6 all-to-all-start.4
  103.4 6.5 all-to-all-done.4
  123.2 5.0 all-to-all-done.5
  138.1 8.3 all-to-all-done.6
  151.9 12.8 all-reduce.2
  173.4 5.1 all-to-all-start.1
  180.5 42.3 %while.137 = (s32[]{:T(128)}, f32[2,128,128]{2,1,0:T(8,128)S(1)}, f32[2,512,2,128]{1,0,3,2:T(2,128)}, f32[2,2,128,128]{3,2,1,0:T(8,128)}, s32[2,512]{1,0:T(2,128...) while((s32[]{:T(128)}, f32[2,128,128]{2,1,0:T(8,128)S(1)}, ...), condition=%wide.region_15.16_spmd.clone, body=%wide.region_14.15_spmd.clone.sunk | while | flops 1346017280 | bytes 13798655 | solution.py:158
  191.2 10.4 dynamic_update_slice.111
  212.3 10.4 dynamic_update_slice.111
  222.8 9.9 all-gather.3
  232.7 5.1 all-to-all-start.2
  260.8 42.0 %while.136 = (s32[]{:T(128)}, f32[2,128,128]{2,1,0:T(8,128)S(1)}, f32[2,512,2,128]{1,0,3,2:T(2,128)}, f32[2,2,128,128]{3,2,1,0:T(8,128)S(1)}, s32[2,512]{1,0:T(2...) while((s32[]{:T(128)}, f32[2,128,128]{2,1,0:T(8,128)S(1)}, ...), condition=%wide.region_5.6_spmd.clone, body=%wide.region_4.5_spmd.clone.sunk | while | flops 1346017280 | bytes 13798655 | solution.py:158
  271.4 10.4 dynamic_update_slice.109
  292.4 10.4 dynamic_update_slice.109
  302.8 9.1 all-gather.1
  320.2 5.1 all-to-all-start.3
  327.0 14.1 all-to-all-done.3
  354.2 6.0 fusion.304
  360.2 5.8 fusion.305
  366.0 7.4 multiply_convert_fusion.2
  373.4 5.4 fusion.308
  387.8 5.4 fusion.310
  424.8 20.9 %all-to-all-done.8 = bf16[256,4,256]{2,0,1:T(8,128)(2,1)} async-done(((bf16[256,4,256]{2,0,1:T(8,128)(2,1)}), bf16[256,4,256]{2,0,1:T(8,128)(2,1)}, u32[]{:S(2)}, u32[]{:S(2)}) %all-to-all-start.8) | async-done | bytes 524320 | tf_op jit(solution)/shard_map/all_to_all | solution.py:370
  445.8 4.5 all-to-all-start.12
  458.0 94.2 %while.138 = (s32[]{:T(128)}, f32[2,128,128]{2,1,0:T(8,128)S(1)}, f32[2,512,2,128]{1,0,3,2:T(2,128)}, f32[2,512,2,128]{1,0,3,2:T(2,128)}, f32[2,512,2,128]{1,0,3...) while((s32[]{:T(128)}, f32[2,128,128]{2,1,0:T(8,128)S(1)}, ...), condition=%wide.region_23.24_spmd.clone, body=%wide.region_22.23_spmd.clone.sunk | while | flops 3495598080 | bytes 56011468 | solution.py:212
  476.5 10.4 dynamic_update_slice.112
  488.4 10.3 dynamic_update_slice.113
  499.3 4.9 dynamic_update_slice.114
  523.6 10.4 dynamic_update_slice.112
  535.4 10.3 dynamic_update_slice.113
  546.3 4.9 dynamic_update_slice.114
  554.2 13.0 all-gather.4
  567.3 5.6 while.134
  575.7 5.1 all-to-all-start.10
  586.6 94.8 %while.139 = (s32[]{:T(128)}, f32[2,128,128]{2,1,0:T(8,128)S(1)}, f32[2,512,2,128]{1,0,3,2:T(2,128)}, f32[2,512,2,128]{1,0,3,2:T(2,128)}, f32[2,512,2,128]{1,0,3...) while((s32[]{:T(128)}, f32[2,128,128]{2,1,0:T(8,128)S(1)}, ...), condition=%wide.region_30.31_spmd.clone, body=%wide.region_29.30_spmd.clone.sunk | while | flops 3495598080 | bytes 49719940 | solution.py:212
  605.4 10.3 dynamic_update_slice.115
  617.2 10.3 dynamic_update_slice.116
  628.0 4.9 dynamic_update_slice.117
  652.7 10.3 dynamic_update_slice.115
  664.5 10.3 dynamic_update_slice.116
  675.3 4.9 dynamic_update_slice.117
  687.1 5.3 all-to-all-start.13
  700.0 9.0 all-gather.5
  709.0 4.6 all-to-all-done.13
  713.6 5.3 all-to-all-start.9
  718.9 5.2 while.135
  726.9 6.4 all-to-all-done.9
  741.1 10.9 all-to-all-done.14
  793.2 18.1 all-to-all-done.11
  817.8 20.2 %all-to-all-done.15 = bf16[4,256,256]{1,2,0:T(8,128)(2,1)S(1)} async-done(((bf16[4,256,256]{1,2,0:T(8,128)(2,1)}), bf16[4,256,256]{1,2,0:T(8,128)(2,1)S(1)}, u32[]{:S(2)}, u32[]{:S(2)}) %all-to-all-start.15) | async-done | bytes 524320 | tf_op jit(solution)/shard_map/all_to_all | solution.py:420
  838.0 5.3 convolution_add_fusion.9
  846.5 6.0 convolution_add_fusion.6
  855.7 6.0 convolution_add_fusion.5
  866.1 6.2 convolution_add_fusion.4
  873.5 4.5 fusion.202
  878.0 4.5 fusion.203
  896.8 20.1 %reduce-scatter.9.cloned.1.call-done = f32[32,1024]{1,0:T(8,128)} async-done(((f32[1024,1024]{1,0:T(8,128)}), f32[32,1024]{1,0:T(8,128)}) %reduce-scatter.9.cloned.1.call-update) | async-done | bytes 131088 | tf_op jit(solution)/shard_map/reduce_scatter | solution.py:469
  916.9 149.5 %reduce-scatter.11.cloned.1.call-done = f32[32,1024]{1,0:T(8,128)} async-done(((f32[1024,1024]{1,0:T(8,128)}), f32[32,1024]{1,0:T(8,128)}) %reduce-scatter.11.cloned.1.call-update) | async-done | bytes 131088 | tf_op jit(solution)/shard_map/reduce_scatter | solution.py:470
  1066.4 148.9 %reduce-scatter.13.cloned.1.call-done = f32[32,1024]{1,0:T(8,128)} async-done(((f32[1024,1024]{1,0:T(8,128)}), f32[32,1024]{1,0:T(8,128)}) %reduce-scatter.13.cloned.1.call-update) | async-done | bytes 131088 | tf_op jit(solution)/shard_map/reduce_scatter | solution.py:471
  1215.3 252.2 %reduce-scatter.19.cloned.1.call-done = f32[32,2816]{1,0:T(8,128)} async-done(((f32[1024,2816]{1,0:T(8,128)}), f32[32,2816]{1,0:T(8,128)}) %reduce-scatter.19.cloned.1.call-update) | async-done | bytes 360464 | tf_op jit(solution)/shard_map/reduce_scatter | solution.py:474
  1467.5 251.2 %reduce-scatter.21.cloned.1.call-done = f32[32,2816]{1,0:T(8,128)} async-done(((f32[1024,2816]{1,0:T(8,128)}), f32[32,2816]{1,0:T(8,128)}) %reduce-scatter.21.cloned.1.call-update) | async-done | bytes 360464 | tf_op jit(solution)/shard_map/reduce_scatter | solution.py:475
  1718.7 251.2 %reduce-scatter.23.cloned.1.call-done = f32[2816,32]{0,1:T(8,128)} async-done(((f32[2816,1024]{0,1:T(8,128)}), f32[2816,32]{0,1:T(8,128)}) %reduce-scatter.23.cloned.1.call-update) | async-done | bytes 360464 | tf_op jit(solution)/shard_map/reduce_scatter | solution.py:476
  (819 shorter events, 404.2 us)
Async XLA Ops:
  7.2 33.4 %all-gather.19.cloned.1.call-start = ((), (), s32[]{:S(2)}) async-start(), calls=%async_computation.26 | async-start | bytes 2359296 | tf_op jit(solution)/shard_map/all_gather | solution.py:259
  7.9 62.4 %all-gather.15.cloned.1.call-start = ((), (), s32[]{:S(2)}) async-start(), calls=%async_computation.24 | async-start | bytes 2359296 | tf_op jit(solution)/shard_map/all_gather | solution.py:260
  8.7 91.5 %all-gather.17.cloned.1.call-start = ((), (), s32[]{:S(2)}) async-start(), calls=%async_computation.25 | async-start | bytes 2359296 | tf_op jit(solution)/shard_map/all_gather | solution.py:261
  9.4 334.4 %all-gather.21.cloned.1.call-start = ((), (), s32[]{:S(2)}) async-start(), calls=%async_computation.27 | async-start | bytes 2359296 | tf_op jit(solution)/shard_map/all_gather | solution.py:262
  10.0 337.1 %all-gather.23.cloned.1.call-start = ((), (), s32[]{:S(2)}) async-start(), calls=%async_computation.28 | async-start | bytes 2359296 | tf_op jit(solution)/shard_map/all_gather | solution.py:263
  10.6 343.6 %all-gather.25.cloned.1.call-start = ((), (), s32[]{:S(2)}) async-start(), calls=%async_computation.29 | async-start | bytes 6488064 | tf_op jit(solution)/shard_map/all_gather | solution.py:264
  11.1 349.0 %all-gather.27.cloned.1.call-start = ((), (), s32[]{:S(2)}) async-start(), calls=%async_computation.30 | async-start | bytes 6488064 | tf_op jit(solution)/shard_map/all_gather | solution.py:265
  12.2 87.9 %copy-start.142 = (f32[256]{0:T(256)}, f32[256]{0:T(256)S(1)}, u32[]{:S(2)}) copy-start(f32[256]{0:T(256)S(1)} %add_rsqrt_fusion.2) | copy-start | bytes 3076
  13.2 73.2 %copy-start.130 = (f32[256,64]{0,1:T(8,128)}, f32[256,64]{0,1:T(8,128)S(1)}, u32[]{:S(2)}) copy-start(f32[256,64]{0,1:T(8,128)S(1)} %get-tuple-element.1818) | copy-start | bytes 196612
  90.4 19.5 all-to-all-start.4
  95.0 271.0 %all-gather.29.cloned.1.call-start = ((), (), s32[]{:S(2)}) async-start(), calls=%async_computation.31 | async-start | bytes 6488064 | tf_op jit(solution)/shard_map/all_gather | solution.py:266
  95.7 18.3 copy-start.145
  95.8 24.1 %copy-start.151 = (u32[32]{0:T(128)S(1)}, u32[32]{0:T(128)}, u32[]{:S(2)}) copy-start(u32[32]{0:T(128)} %constant.442) | copy-start | bytes 388
  102.5 29.8 %copy-start.146 = (f32[8]{0:T(128)S(1)}, f32[8]{0:T(128)}, u32[]{:S(2)}) copy-start(f32[8]{0:T(128)} %param.31) | copy-start | bytes 100
  109.9 18.3 all-to-all-start.5
  121.2 45.0 %copy-start.48 = (bf16[1024,1024]{1,0:T(8,128)(2,1)S(1)}, bf16[1024,1024]{1,0:T(8,128)(2,1)}, u32[]{:S(2)}) copy-start(bf16[1024,1024]{1,0:T(8,128)(2,1)} %all-gather.17.cloned.1.call-done) | copy-start | bytes 6291460
  128.2 18.2 all-to-all-start.6
  146.4 27.0 %all-to-all-start = ((bf16[256,4,256]{0,2,1:T(8,128)(2,1)}), bf16[256,4,256]{0,2,1:T(8,128)(2,1)}, u32[]{:S(2)}, u32[]{:S(2)}) async-start(bf16[256,4,256]{0,2,1:T(8,128)(2,1)} %bitcast.839), calls=%async_computation | async-start | bytes 1048576 | tf_op jit(solution)/shard_map/all_to_all | solution.py:305
  166.1 76.1 %copy-start.138 = (f32[1024,2]{0,1:T(2,128)}, f32[1024,2]{0,1:T(2,128)S(1)}, u32[]{:S(2)}) copy-start(f32[1024,2]{0,1:T(2,128)S(1)} %get-tuple-element.1821) | copy-start | bytes 24580
  173.4 59.3 %all-to-all-start.1 = ((bf16[256,4,256]{2,0,1:T(8,128)(2,1)}), bf16[256,4,256]{2,0,1:T(8,128)(2,1)}, u32[]{:S(2)}, u32[]{:S(2)}) async-start(bf16[256,4,256]{2,0,1:T(8,128)(2,1)} %bitcast.610), calls=%async_computation.1 | async-start | bytes 1048576 | tf_op jit(solution)/shard_map/all_to_all | solution.py:306
  222.7 16.0 copy-start.16
  222.7 16.0 copy-start.133
  222.7 16.0 copy-start.148
  222.7 15.0 copy-start.80
  232.7 20.2 %all-to-all-start.2 = ((bf16[256,4,256]{0,2,1:T(8,128)(2,1)}), bf16[256,4,256]{0,2,1:T(8,128)(2,1)}, u32[]{:S(2)}, u32[]{:S(2)}) async-start(bf16[256,4,256]{0,2,1:T(8,128)(2,1)} %bitcast.837), calls=%async_computation.2 | async-start | bytes 1048576 | tf_op jit(solution)/shard_map/all_to_all | solution.py:304
  252.9 67.4 %all-to-all-start.7 = ((bf16[4,256,256]{2,1,0:T(8,128)(2,1)}), bf16[4,256,256]{2,1,0:T(8,128)(2,1)}, u32[]{:S(2)}, u32[]{:S(2)}) async-start(bf16[4,256,256]{2,1,0:T(8,128)(2,1)} %copy.419), calls=%async_computation.7 | async-start | bytes 1048576 | tf_op jit(solution)/shard_map/all_to_all | solution.py:327
  302.8 12.2 copy-start.106
  320.2 20.9 %all-to-all-start.3 = ((bf16[4,256,256]{2,1,0:T(8,128)(2,1)}), bf16[4,256,256]{2,1,0:T(8,128)(2,1)S(1)}, u32[]{:S(2)}, u32[]{:S(2)}) async-start(bf16[4,256,256]{2,1,0:T(8,128)(2,1)} %copy.418), calls=%async_computation.3 | async-start | bytes 1048576 | tf_op jit(solution)/shard_map/all_to_all | solution.py:327
  325.3 571.5 %reduce-scatter.15.cloned.1.call-start = ((), (), s32[]{:S(2)}) async-start(), calls=%async_computation.35 | async-start | bytes 4325376 | tf_op jit(solution)/shard_map/reduce_scatter | solution.py:472
  327.0 16.8 copy-start.25
  327.0 16.8 copy-start.143
  353.1 29.3 %copy-start.33 = (bf16[256,1024]{1,0:T(8,128)(2,1)}, bf16[256,1024]{1,0:T(8,128)(2,1)S(1)}, u32[]{:S(2)}) copy-start(bf16[256,1024]{1,0:T(8,128)(2,1)S(1)} %multiply_convert_fusion.16) | copy-start | bytes 1572868
  366.0 12.8 copy-start.147
  398.2 23.6 %copy-start.23 = (f32[256,1024]{1,0:T(8,128)}, f32[256,1024]{1,0:T(8,128)S(1)}, u32[]{:S(2)}) copy-start(f32[256,1024]{1,0:T(8,128)S(1)} %get-tuple-element.1795) | copy-start | bytes 3145732
  414.4 31.4 %all-to-all-start.8 = ((bf16[256,4,256]{2,0,1:T(8,128)(2,1)}), bf16[256,4,256]{2,0,1:T(8,128)(2,1)}, u32[]{:S(2)}, u32[]{:S(2)}) async-start(bf16[256,4,256]{2,0,1:T(8,128)(2,1)} %bitcast.841), calls=%async_computation.8 | async-start | bytes 1048576 | tf_op jit(solution)/shard_map/all_to_all | solution.py:370
  418.6 478.3 %reduce-scatter.17.cloned.1.call-start = ((), (), s32[]{:S(2)}) async-start(), calls=%async_computation.36 | async-start | bytes 4325376 | tf_op jit(solution)/shard_map/reduce_scatter | solution.py:473
  445.8 130.0 %all-to-all-start.12 = ((bf16[256,4,256]{2,0,1:T(8,128)(2,1)}), bf16[256,4,256]{2,0,1:T(8,128)(2,1)}, u32[]{:S(2)}, u32[]{:S(2)}) async-start(bf16[256,4,256]{2,0,1:T(8,128)(2,1)} %bitcast.607), calls=%async_computation.12 | async-start | bytes 1048576 | tf_op jit(solution)/shard_map/all_to_all | solution.py:370
  474.7 12.3 copy-start.1
  474.7 12.2 copy-start.14
  487.8 17.3 copy-start.18
  487.8 17.3 copy-start.22
  521.7 12.3 copy-start.1
  521.8 12.2 copy-start.14
  534.9 17.3 copy-start.18
  534.9 17.3 copy-start.22
  552.2 20.7 %copy-start.98 = (f32[2,512,2,128]{1,0,3,2:T(2,128)S(1)}, f32[2,512,2,128]{1,0,3,2:T(2,128)}, u32[]{:S(2)}) copy-start(f32[2,512,2,128]{1,0,3,2:T(2,128)} %get-tuple-element.1190) | copy-start | bytes 3145732
  575.7 111.4 %all-to-all-start.10 = ((bf16[4,256,256]{1,2,0:T(8,128)(2,1)}), bf16[4,256,256]{1,2,0:T(8,128)(2,1)}, u32[]{:S(2)}, u32[]{:S(2)}) async-start(bf16[4,256,256]{1,2,0:T(8,128)(2,1)} %copy.368), calls=%async_computation.10 | async-start | bytes 1048576 | tf_op jit(solution)/shard_map/all_to_all | solution.py:413
  603.5 12.2 copy-start.3
  616.6 17.3 copy-start.150
  663.9 17.3 copy-start.150
  687.1 26.5 %all-to-all-start.13 = ((bf16[4,256,256]{2,1,0:T(8,128)(2,1)}), bf16[4,256,256]{2,1,0:T(8,128)(2,1)S(1)}, u32[]{:S(2)}, u32[]{:S(2)}) async-start(bf16[4,256,256]{2,1,0:T(8,128)(2,1)} %copy.423), calls=%async_computation.13 | async-start | bytes 1048576 | tf_op jit(solution)/shard_map/all_to_all | solution.py:406
  700.0 24.2 %copy-start.102 = (f32[2,512,2,128]{1,0,3,2:T(2,128)S(1)}, f32[2,512,2,128]{1,0,3,2:T(2,128)}, u32[]{:S(2)}) copy-start(f32[2,512,2,128]{1,0,3,2:T(2,128)} %get-tuple-element.2724) | copy-start | bytes 3145732
  713.6 19.8 %all-to-all-start.9 = ((bf16[4,256,256]{2,1,0:T(8,128)(2,1)}), bf16[4,256,256]{2,1,0:T(8,128)(2,1)}, u32[]{:S(2)}, u32[]{:S(2)}) async-start(bf16[4,256,256]{2,1,0:T(8,128)(2,1)} %copy.420), calls=%async_computation.9 | async-start | bytes 1048576 | tf_op jit(solution)/shard_map/all_to_all | solution.py:406
  733.4 18.6 all-to-all-start.14
  737.5 179.4 %reduce-scatter.9.cloned.1.call-start = ((), (), s32[]{:S(2)}) async-start(), calls=%async_computation.32 | async-start | bytes 4325376 | tf_op jit(solution)/shard_map/reduce_scatter | solution.py:469
  739.9 13.2 copy-start.131
  739.9 13.2 copy-start.132
  763.4 303.0 %reduce-scatter.11.cloned.1.call-start = ((), (), s32[]{:S(2)}) async-start(), calls=%async_computation.33 | async-start | bytes 4325376 | tf_op jit(solution)/shard_map/reduce_scatter | solution.py:470
  783.6 27.7 %all-to-all-start.11 = ((bf16[4,256,256]{1,2,0:T(8,128)(2,1)}), bf16[4,256,256]{1,2,0:T(8,128)(2,1)S(1)}, u32[]{:S(2)}, u32[]{:S(2)}) async-start(bf16[4,256,256]{1,2,0:T(8,128)(2,1)} %copy.374), calls=%async_computation.11 | async-start | bytes 1048576 | tf_op jit(solution)/shard_map/all_to_all | solution.py:420
  811.3 26.7 %all-to-all-start.15 = ((bf16[4,256,256]{1,2,0:T(8,128)(2,1)}), bf16[4,256,256]{1,2,0:T(8,128)(2,1)S(1)}, u32[]{:S(2)}, u32[]{:S(2)}) async-start(bf16[4,256,256]{1,2,0:T(8,128)(2,1)} %copy.395), calls=%async_computation.15 | async-start | bytes 1048576 | tf_op jit(solution)/shard_map/all_to_all | solution.py:420
  814.8 400.6 %reduce-scatter.13.cloned.1.call-start = ((), (), s32[]{:S(2)}) async-start(), calls=%async_computation.34 | async-start | bytes 4325376 | tf_op jit(solution)/shard_map/reduce_scatter | solution.py:471
  843.4 624.2 %reduce-scatter.19.cloned.1.call-start = ((), (), s32[]{:S(2)}) async-start(), calls=%async_computation.37 | async-start | bytes 11894784 | tf_op jit(solution)/shard_map/reduce_scatter | solution.py:474
  852.6 866.1 %reduce-scatter.21.cloned.1.call-start = ((), (), s32[]{:S(2)}) async-start(), calls=%async_computation.38 | async-start | bytes 11894784 | tf_op jit(solution)/shard_map/reduce_scatter | solution.py:475
  861.7 1108.2 %reduce-scatter.23.cloned.1.call-start = ((), (), s32[]{:S(2)}) async-start(), calls=%async_computation.39 | async-start | bytes 11894784 | tf_op jit(solution)/shard_map/reduce_scatter | solution.py:476
  (150 other events, 632.3 us)
Sparse Core Ops, SparseCore 0:
  9.9 30.5 all-gather.18
  42.4 27.8 all-gather.14
  72.2 27.8 all-gather.16
  101.9 27.8 all-gather.20
  131.6 27.9 all-gather.22
  161.3 43.3 all-gather.24
  206.5 43.3 all-gather.26
  251.8 44.3 all-gather.28
  409.8 158.9 reduce-scatter.14
  571.5 156.0 reduce-scatter.16
  763.6 153.3 reduce-scatter.8
  919.6 146.7 reduce-scatter.10
  1069.3 146.0 reduce-scatter.12
  1218.1 249.4 reduce-scatter.18
  1470.3 248.4 reduce-scatter.20
  1721.5 248.4 reduce-scatter.22
where the time goes:
time: 2000 us; the launch traced here: 1980 us
  waiting for transfers between devices  1250 us (62%)
  local copies, waits for them, and re-layouts  300 us (15%)
  matrix products  199 us (10%)
  starting transfers between devices  73.9 us (4%)
  other arithmetic  65.6 us (3%)
  blocking collectives  53.8 us (3%)
    reduce_scatter x1, waiting for transfers between devices, local(): lax.psum_scatter(grad_totals[5], ('fsdp', 'head'), scatter_dimension=0, t...  252 us
    reduce_scatter x1, waiting for transfers between devices, local(): lax.psum_scatter(grad_totals[7], ('fsdp', 'head'), scatter_dimension=1, t...  251 us
    reduce_scatter x1, waiting for transfers between devices, local(): lax.psum_scatter(grad_totals[6], ('fsdp', 'head'), scatter_dimension=0, t...  251 us
    dynamic_update_slice x32, local copies, waits for them, and re-layouts, local_forward(): lax.scan(step_fn, zero_state, (queries.reshape(num_blocks, block_len, hea...  152 us
    reduce_scatter x1, waiting for transfers between devices, local(): lax.psum_scatter(grad_totals[1], ('fsdp', 'head'), scatter_dimension=0, t...  150 us
    reduce_scatter x1, waiting for transfers between devices, local(): lax.psum_scatter(grad_totals[2], ('fsdp', 'head'), scatter_dimension=0, t...  149 us
    dot_general x16, matrix products, dot_rows(): lax.dot_general(left_arr, right_arr, (((0,), (0,)), ((), ())), preferred_...  47.5 us
    all_gather x4, blocking collectives, prefix(): lax.all_gather(a.astype(kind), axis)  41 us
  transfers between devices with their start and end apart: 32, of which 20 were waited for; matrix products, arithmetic and copies ran while one was open for 25% of the time, Pallas kernels for 0%

commit v1 on v0

v1 whole, which is shorter than its diff:
```python
import math

import jax
import jax.numpy as jnp
from jax import lax
from jax.sharding import PartitionSpec as P

H = 8
DH = 128
EPSILON = 1e-06
AXES = ("fsdp", "head")
F32 = jnp.float32
BF16 = jnp.bfloat16


def norm_parts(values):
    inv_scale = lax.rsqrt(jnp.mean(values * values, axis=-1, keepdims=True) + EPSILON)
    return (values * inv_scale, inv_scale)


def norm_back(gradient, normed, inv_scale):
    return inv_scale * (gradient - normed * jnp.mean(gradient * normed, axis=-1, keepdims=True))


def rotate_pairs(values, cosine, sine_vals):
    half_size = values.shape[-1] // 2
    first_half = values[..., :half_size]
    second_half = values[..., half_size:]
    return jnp.concatenate(
        [
            first_half * cosine - second_half * sine_vals,
            first_half * sine_vals + second_half * cosine,
        ],
        axis=-1,
    )


def rotation_tables(positions, head_size):
    half_size = head_size // 2
    shifts = jnp.arange(half_size, dtype=jnp.int32) * 10 // half_size
    speeds = jnp.right_shift(jnp.full((half_size,), 651, jnp.int32), shifts) + 1
    phases = positions[:, None] * speeds[None, :] % 4096
    angles = phases.astype(F32) * (2.0 * math.pi / 4096.0)
    return (jnp.cos(angles)[:, None, :], jnp.sin(angles)[:, None, :])


def silu_slope(values):
    sigmoid_v = jax.nn.sigmoid(values)
    return sigmoid_v * (1.0 + values * (1.0 - sigmoid_v))


def dot(a, b):
    return jnp.dot(a, b, preferred_element_type=F32)


def dot_rows(a, b):
    return lax.dot_general(a, b, (((0,), (0,)), ((), ())), preferred_element_type=F32)


def dot_cols(a, b):
    return lax.dot_general(a, b, (((1,), (1,)), ((), ())), preferred_element_type=F32)


class Wires:
    def __init__(self):
        self.nf = lax.axis_size("fsdp")
        self.nh = lax.axis_size("head")
        self.fast = self.nf == 8 and self.nh == 4
        self.f = lax.axis_index("fsdp")
        self.h = lax.axis_index("head")

    def swap(self, values, fbits=0, hbits=0):
        pairs = []
        for f in range(self.nf):
            for h in range(self.nh):
                pairs.append((f * self.nh + h, (f ^ fbits) * self.nh + (h ^ hbits)))
        return lax.ppermute(values, AXES, pairs)

    def rel(self, values):
        if not self.fast:
            return values
        width = values.shape[1] // self.nf
        return jnp.concatenate(
            [
                lax.dynamic_slice_in_dim(values, (self.f ^ i) * width, width, 1)
                for i in range(self.nf)
            ],
            axis=1,
        )

    def gather(self, shard):
        if not self.fast:
            return lax.all_gather(shard, "fsdp", axis=0, tiled=True)
        half = shard.shape[1] // 2
        core, x, y = 1, 2, 4
        at_c = self.swap(shard, core)
        at_x = self.swap(shard, x)
        at_y = self.swap(shard, y)
        at_xy = jnp.concatenate(
            [self.swap(at_x[:, :half], y), self.swap(at_y[:, half:], x)], axis=1
        )
        at_cx = self.swap(at_x, core)
        at_cy = self.swap(at_y, core)
        at_cxy = self.swap(at_xy, core)
        return jnp.concatenate([shard, at_c, at_x, at_cx, at_y, at_cy, at_xy, at_cxy], axis=0)

    def reduce(self, grad):
        if not self.fast:
            return lax.psum_scatter(grad, AXES, scatter_dimension=0, tiled=True)
        core, x, y = 1, 2, 4
        rows, n = grad.shape[0] // 8, grad.shape[1]
        low = grad.astype(BF16).reshape(2, 2, 2, rows, n)
        merged = (low[:, :, 0].astype(F32) + self.swap(low[:, :, 1], core).astype(F32)).astype(BF16)
        half = n // 2
        a = merged[:, :, :, :half]
        a = (a[:, 0].astype(F32) + self.swap(a[:, 1], x).astype(F32)).astype(BF16)
        a = (a[0].astype(F32) + self.swap(a[1], y).astype(F32)).astype(BF16)
        b = merged[:, :, :, half:]
        b = (b[0].astype(F32) + self.swap(b[1], y).astype(F32)).astype(BF16)
        b = (b[0].astype(F32) + self.swap(b[1], x).astype(F32)).astype(BF16)
        return jnp.concatenate([self.along(a), self.along(b)], axis=1)

    def along(self, part):
        rows, n = part.shape
        part = part.reshape(2, 2, rows // 4, n)
        low, high = self.h % 2, self.h // 2
        keep = lax.dynamic_index_in_dim(part, low, 1, False)
        send = lax.dynamic_index_in_dim(part, 1 - low, 1, False)
        part = (keep.astype(F32) + self.swap(send, 0, 1).astype(F32)).astype(BF16)
        keep = lax.dynamic_index_in_dim(part, high, 0, False)
        send = lax.dynamic_index_in_dim(part, 1 - high, 0, False)
        return keep.astype(F32) + self.swap(send, 0, 2).astype(F32)

    def to_heads(self, states):
        mb, heads, d, _ = states.shape
        mine = heads // self.nh
        parts = jnp.moveaxis(states.reshape(mb, self.nh, mine, d, d), 1, 0)
        return self.scatter(parts)

    def scatter(self, parts):
        if not self.fast:
            return lax.all_to_all(parts, "head", split_axis=0, concat_axis=0, tiled=True)
        got = [lax.dynamic_index_in_dim(parts, self.h, 0, False)]
        for i in range(1, self.nh):
            got.append(self.swap(lax.dynamic_index_in_dim(parts, self.h ^ i, 0, False), 0, i))
        got = jnp.stack(got)
        order = self.h ^ jnp.arange(self.nh)
        return jnp.take(got, order, axis=0)

    def from_heads(self, parts):
        got = self.scatter(parts)
        nh, mb, mine, d, _ = got.shape
        return jnp.moveaxis(got, 0, 1).reshape(mb, nh * mine, d, d)

    def spread(self, total):
        if not self.fast:
            return lax.all_gather(total, "fsdp")
        core, x, y = 1, 2, 4
        at_c = self.swap(total, core)
        pair = jnp.stack([total, at_c])
        at_x = self.swap(pair, x)
        at_y = self.swap(pair, y)
        at_xy = self.swap(pair, x + y)
        got = jnp.concatenate([pair, at_x, at_y, at_xy])
        return jnp.take(got, self.f ^ jnp.arange(self.nf), axis=0)


def chain(wires, states, ends, decay, chunk, backward):
    nf, nh, f = wires.nf, wires.nh, wires.f
    mb, heads = states.shape[:2]
    mine = heads // nh
    rates = lax.dynamic_slice_in_dim(decay, wires.h * mine, mine)
    places = jnp.arange(nh)
    groups = jnp.arange(nf)
    at_group = lax.dynamic_slice_in_dim(ends, f * nh, nh, axis=1)
    before_group = jnp.where(
        f > 0, lax.dynamic_index_in_dim(ends, jnp.maximum(f * nh - 1, 0), 1, False), 0
    )
    before = jnp.concatenate([before_group[:, None], at_group[:, :-1]], axis=1)
    last = at_group[:, -1]
    group_last = ends.reshape(mb, nf, nh)[:, :, -1]
    group_before = jnp.concatenate([jnp.zeros_like(group_last[:, :1]), group_last[:, :-1]], axis=1)

    def factor(same, gap):
        gap = jnp.maximum(gap, 0)
        return jnp.where(
            same[..., None], jnp.exp(-rates * (chunk * gap).astype(F32)[..., None]), 0.0
        )

    own = wires.to_heads(states.astype(BF16)).astype(F32)
    if backward:
        to_total = factor(before == before_group[:, None], jnp.broadcast_to(places, (mb, nh)))
        group_same = (last[:, None] == group_before) & (groups > f)
        group_gap = jnp.broadcast_to((groups - 1 - f) * nh, (mb, nf))
        to_place = factor(at_group == last[:, None], jnp.broadcast_to(nh - 1 - places, (mb, nh)))
        same = (at_group[:, :, None] == before[:, None, :]) & (places[None, :] > places[:, None])
        gap = jnp.broadcast_to(places[None, :] - 1 - places[:, None], (mb, nh, nh))
    else:
        to_total = factor(at_group == last[:, None], jnp.broadcast_to(nh - 1 - places, (mb, nh)))
        group_same = (before_group[:, None] == group_last) & (groups < f)
        group_gap = jnp.broadcast_to((f - 1 - groups) * nh, (mb, nf))
        to_place = factor(before == before_group[:, None], jnp.broadcast_to(places, (mb, nh)))
        same = (before[:, :, None] == at_group[:, None, :]) & (places[None, :] < places[:, None])
        gap = jnp.broadcast_to(places[:, None] - 1 - places[None, :], (mb, nh, nh))
    total = sum(to_total[:, i, :, None, None] * own[i] for i in range(nh))
    totals = wires.spread(total.astype(BF16)).astype(F32)
    from_group = factor(group_same, group_gap)
    outer = sum(from_group[:, i, :, None, None] * totals[i] for i in range(nf))
    between = factor(same, gap)
    result = [
        to_place[:, i, :, None, None] * outer
        + sum(between[:, i, j, :, None, None] * own[j] for j in range(nh) if i != j)
        for i in range(nh)
    ]
    return wires.from_heads(jnp.stack(result).astype(BF16))


def masks(segs, before, last, decay):
    rows = segs.shape[1]
    offsets = jnp.arange(rows, dtype=F32)
    distance = offsets[:, None] - offsets[None, :]
    visible = (segs[:, :, None] == segs[:, None, :]) & (distance >= 0.0)
    within = jnp.where(
        visible[:, None],
        jnp.exp(-decay[:, None, None] * jnp.maximum(distance, 0.0))[None],
        0.0,
    )
    entering = jnp.where(
        (segs == before[:, None])[:, None, :],
        jnp.exp(-decay[:, None] * (offsets + 1.0))[None],
        0.0,
    )
    leaving = jnp.where(
        (segs == last[:, None])[:, None, :],
        jnp.exp(-decay[:, None] * (rows - 1.0 - offsets))[None],
        0.0,
    )
    return within, entering[..., None], leaving[..., None]


def local(
    tokens,
    cotangent,
    lengths,
    decay_rate,
    query_weight,
    key_weight,
    value_weight,
    gate_weight,
    out_weight,
    first_weight,
    second_weight,
    down_weight,
):
    wires = Wires()
    mb, chunk, width = tokens.shape
    rows = mb * chunk
    place = wires.f * wires.nh + wires.h
    count = wires.nf * wires.nh

    mix_weights = wires.gather(
        jnp.concatenate([query_weight, key_weight, value_weight, gate_weight], axis=1)
    )
    out_full = wires.gather(out_weight)
    gate_up = wires.gather(jnp.concatenate([first_weight, second_weight], axis=1))
    down_t = wires.gather(down_weight.T)
    hidden_size = down_t.shape[1]

    positions = place * chunk + jnp.arange(chunk, dtype=jnp.int32)
    cosine, sine_vals = rotation_tables(positions, DH)
    cosine, sine_vals = jnp.tile(cosine, (mb, 1, 1)), jnp.tile(sine_vals, (mb, 1, 1))
    seq_ends = jnp.cumsum(lengths, axis=1)
    segs = jnp.sum((seq_ends[:, None, :] <= positions[None, :, None]).astype(jnp.int32), axis=2)
    marks = (jnp.arange(count, dtype=jnp.int32) + 1) * chunk - 1
    ends = jnp.sum((seq_ends[:, None, :] <= marks[None, :, None]).astype(jnp.int32), axis=2)
    last = lax.dynamic_index_in_dim(ends, place, 1, False)
    before = jnp.where(
        place > 0, lax.dynamic_index_in_dim(ends, jnp.maximum(place - 1, 0), 1, False), 0
    )
    within, entering, leaving = masks(segs, before, last, decay_rate)

    def heads(values):
        return values.reshape(mb, chunk, H, DH).transpose(0, 2, 1, 3)

    def flat(values):
        return values.transpose(0, 2, 1, 3).reshape(rows, H * DH)

    def mm(spec, a, b):
        return jnp.einsum(spec, a.astype(BF16), b.astype(BF16), preferred_element_type=F32)

    inputs = tokens.reshape(rows, width).astype(F32)
    normed_in, scale_in = norm_parts(inputs)
    act_rel = wires.rel(normed_in.astype(BF16))
    mixed_pre = dot(act_rel, mix_weights)
    query_pre = mixed_pre[:, :width]
    key_pre = mixed_pre[:, width : 2 * width]
    value_low = mixed_pre[:, 2 * width : 3 * width].astype(BF16)
    gate_vals = mixed_pre[:, 3 * width :]

    def turned(values):
        return rotate_pairs(jax.nn.silu(values).reshape(rows, H, DH), cosine, sine_vals).astype(BF16)

    query_h = heads(turned(query_pre))
    key_h = heads(turned(key_pre))
    value_h = heads(value_low)
    local_state = mm("mhtd,mhte->mhde", key_h * leaving, value_h)
    state_in = chain(wires, local_state, ends, decay_rate, chunk, False)
    scores = (mm("mhsd,mhtd->mhst", query_h, key_h) * within).astype(BF16)
    attended = mm("mhst,mhte->mhse", scores, value_h)
    attended = attended + entering * mm("mhsd,mhde->mhse", query_h, state_in)
    attended = flat(attended.astype(BF16))

    normed_att, scale_att = norm_parts(attended.astype(F32))
    gated_rel = wires.rel((normed_att * gate_vals).astype(BF16))
    hidden = inputs + dot(gated_rel, out_full)
    normed_mid, scale_mid = norm_parts(hidden)
    mid_rel = wires.rel(normed_mid.astype(BF16))
    pre = dot(mid_rel, gate_up)
    first_pre, second_pre = pre[:, :hidden_size], pre[:, hidden_size:]
    product = (first_pre * second_pre).astype(BF16)
    mixed = (hidden + wires.rel(dot_cols(product, down_t))).astype(BF16)

    grad_low = cotangent.reshape(rows, width)
    grad_rel = wires.rel(grad_low)
    share_down = wires.reduce(dot_rows(grad_rel, product)).T
    grad_prod = dot(grad_rel, down_t)
    grad_pre = jnp.concatenate(
        [(grad_prod * second_pre).astype(BF16), (grad_prod * first_pre).astype(BF16)], axis=1
    )
    share_up = wires.reduce(dot_rows(mid_rel, grad_pre))
    grad_mid = wires.rel(dot_cols(grad_pre, gate_up))
    grad_hidden = grad_low.astype(F32) + norm_back(grad_mid, normed_mid, scale_mid)
    grad_hidden_low = grad_hidden.astype(BF16)
    share_out = wires.reduce(dot_rows(gated_rel, grad_hidden_low))
    grad_gated = wires.rel(dot_cols(grad_hidden_low, out_full))
    grad_gate_low = (grad_gated * normed_att).astype(BF16)
    grad_att = heads(norm_back(grad_gated * gate_vals, normed_att, scale_att).astype(BF16))

    grad_state = mm("mhsd,mhse->mhde", query_h * entering, grad_att)
    grad_end = chain(wires, grad_state, ends, decay_rate, chunk, True)
    grad_scores = (mm("mhse,mhte->mhst", grad_att, value_h) * within).astype(BF16)
    grad_q = mm("mhst,mhtd->mhsd", grad_scores, key_h)
    grad_q = grad_q + entering * mm("mhse,mhde->mhsd", grad_att, state_in)
    grad_k = mm("mhst,mhsd->mhtd", grad_scores, query_h)
    grad_k = grad_k + leaving * mm("mhte,mhde->mhtd", value_h, grad_end)
    grad_v = mm("mhst,mhse->mhte", scores, grad_att)
    grad_v = grad_v + leaving * mm("mhtd,mhde->mhte", key_h, grad_end)

    def turned_back(values, pre_values):
        back = flat(values.astype(BF16)).astype(F32).reshape(rows, H, DH)
        back = rotate_pairs(back, cosine, -sine_vals).reshape(rows, width)
        return (silu_slope(pre_values) * back).astype(BF16)

    grad_mix = jnp.concatenate(
        [
            turned_back(grad_q, query_pre),
            turned_back(grad_k, key_pre),
            flat(grad_v.astype(BF16)),
            grad_gate_low,
        ],
        axis=1,
    )
    share_mix = wires.reduce(dot_rows(act_rel, grad_mix))
    grad_act = wires.rel(dot_cols(grad_mix, mix_weights))
    grad_tokens = (grad_hidden + norm_back(grad_act, normed_in, scale_in)).astype(BF16)
    return (
        mixed.reshape(mb, chunk, width),
        grad_tokens.reshape(mb, chunk, width),
        share_mix[:, :width],
        share_mix[:, width : 2 * width],
        share_mix[:, 2 * width : 3 * width],
        share_mix[:, 3 * width :],
        share_out,
        share_up[:, :hidden_size],
        share_up[:, hidden_size:],
        share_down,
    )


def solution(mesh):
    rows = P(None, AXES, None)
    in_specs = (rows, rows, P(), P()) + (P("fsdp", None),) * 7 + (P(None, "fsdp"),)
    out_specs = (rows, rows) + (P(AXES, None),) * 7 + (P(None, AXES),)
    return jax.shard_map(local, mesh=mesh, in_specs=in_specs, out_specs=out_specs, check_vma=False)
```

time: 2000 us -> 650 us (0.33)
  waiting for transfers between devices: 1250 us -> 221 us
  local copies, waits for them, and re-layouts: 300 us -> 167 us
  matrix products: 199 us -> 95 us
  blocking collectives: 53.8 us -> 0 us
    reduce_scatter x8 -> x0, waiting for transfers between devices: 1070 us -> none  [the longest x1 252 us: local(): lax.psum_scatter(grad_totals[5], ('fsdp', 'head'), scatter_dimension=0, t...]
    ppermute x0 -> x88, waiting for transfers between devices: none -> 221 us  [swap(): return lax.ppermute(values, AXES, pairs)]
    dynamic_update_slice x32 -> x0, local copies, waits for them, and re-layouts: 152 us -> none  [local_forward(): lax.scan(step_fn, zero_state, (queries.reshape(num_blocks, block_len, hea...]
    all_to_all x16 -> x0, waiting for transfers between devices: 118 us -> none  [the longest x2 38.3 us: local(): lax.all_to_all(grad_v.reshape(group_len, heads_here * DH).astype(jnp.bflo...]
    dot_general x110 -> x24, matrix products: 199 us -> 95 us  [the longest x4 29.5 us: dot(): return jnp.dot(a, b, preferred_element_type=F32)]
    ppermute x0 -> x88, starting transfers between devices: none -> 82.5 us  [swap(): return lax.ppermute(values, AXES, pairs)]
    unnamed x275 -> x393, local copies, waits for them, and re-layouts: 22.9 us -> 97.2 us
    all_to_all x16 -> x0, starting transfers between devices: 72.3 us -> none  [the longest x2 10.6 us: local(): lax.all_to_all(grad_q.reshape(group_len, heads_here * DH).astype(jnp.bflo...]
  transfers between devices with their start and end apart: 32 -> 88, of which waited for: 20 -> 41; matrix products, arithmetic and copies ran while one was open for 25% -> 36% of each run, Pallas kernels for 0% -> 0%
where the time goes in v1:
time: 650 us; the launch traced here: 639 us
  waiting for transfers between devices  221 us (34%)
  local copies, waits for them, and re-layouts  167 us (26%)
  matrix products  95 us (15%)
  starting transfers between devices  82.5 us (13%)
  other arithmetic  70.4 us (11%)
    ppermute x88, waiting for transfers between devices, swap(): return lax.ppermute(values, AXES, pairs)  221 us
    unnamed x393, local copies, waits for them, and re-layouts  97.2 us
    ppermute x88, starting transfers between devices, swap(): return lax.ppermute(values, AXES, pairs)  82.5 us
    dot_general x4, matrix products, dot(): return jnp.dot(a, b, preferred_element_type=F32)  29.5 us
    dot_general x4, matrix products, dot_cols(): lax.dot_general(a, b, (((1,), (1,)), ((), ())), preferred_element_type=F32)  25.5 us
    dot_general x4, matrix products, dot_rows(): lax.dot_general(a, b, (((0,), (0,)), ((), ())), preferred_element_type=F32)  23.3 us
    dot_general x12, matrix products, mm(): jnp.einsum(spec, a.astype(BF16), b.astype(BF16), preferred_element_type=F32)  16.8 us
    slice x4, local copies, waits for them, and re-layouts, reduce(): low[:, :, 0].astype(F32) + self.swap(low[:, :, 1], core).astype(F32)  13.8 us
  transfers between devices with their start and end apart: 88, of which 41 were waited for; matrix products, arithmetic and copies ran while one was open for 36% of the time, Pallas kernels for 0%

profile of v1, /device:TPU:0, one launch (start us, length us, event | category | flops | bytes accessed | tf_op | source)
XLA Modules:
  0.0 639.3 jit_solution(9577214588398271711)
XLA Ops:
  1.2 2.6 collective-permute-start.19
  74.3 8.8 %collective-permute-done.37 = bf16[128,2816]{0,1:T(8,128)(2,1)S(1)} collective-permute-done((bf16[128,2816]{0,1:T(8,128)(2,1)}, bf16[128,2816]{0,1:T(8,128)(2,1)S(1)}, u32[]{:S(2)}, u32[]{:S(2)}) %collective-permute-start.37) | collective-permute-done | bytes 720928 | tf_op jit(solution)/shard_map/ppermute | solution.py:77
  88.0 7.5 %collective-permute-done.1 = bf16[128,4096]{1,0:T(8,128)(2,1)S(1)} collective-permute-done((bf16[128,4096]{1,0:T(8,128)(2,1)S(1)}, bf16[128,4096]{1,0:T(8,128)(2,1)S(1)}, u32[]{:S(2)}, u32[]{:S(2)}) %collective-permute-start.1) | collective-permute-done | bytes 1048608 | tf_op jit(solution)/shard_map/ppermute | solution.py:77
  96.1 9.4 %collective-permute-done.3 = bf16[128,4096]{1,0:T(8,128)(2,1)S(1)} collective-permute-done((bf16[128,4096]{1,0:T(8,128)(2,1)S(1)}, bf16[128,4096]{1,0:T(8,128)(2,1)S(1)}, u32[]{:S(2)}, u32[]{:S(2)}) %collective-permute-start.3) | collective-permute-done | bytes 1048608 | tf_op jit(solution)/shard_map/ppermute | solution.py:77
  106.5 6.3 collective-permute-done.39
  114.4 19.1 %collective-permute-done.40 = bf16[128,1408]{0,1:T(8,128)(2,1)S(1)} collective-permute-done((bf16[128,1408]{0,1:T(8,128)(2,1)S(1)}, bf16[128,1408]{0,1:T(8,128)(2,1)S(1)}, u32[]{:S(2)}, u32[]{:S(2)}) %collective-permute-start.40) | collective-permute-done | bytes 360480 | tf_op jit(solution)/shard_map/ppermute | solution.py:77
  138.7 2.6 constant_dynamic-update-slice_fusion.59
  144.7 2.7 collective-permute-done.29
  149.4 8.0 %collective-permute-done.5 = bf16[128,2048]{1,0:T(8,128)(2,1)S(1)} collective-permute-done((bf16[128,2048]{1,0:T(8,128)(2,1)S(1)}, bf16[128,2048]{1,0:T(8,128)(2,1)S(1)}, u32[]{:S(2)}, u32[]{:S(2)}) %collective-permute-start.5) | collective-permute-done | bytes 524320 | tf_op jit(solution)/shard_map/ppermute | solution.py:77
  161.6 12.8 %collective-permute-done.31 = bf16[128,2816]{1,0:T(8,128)(2,1)S(1)} collective-permute-done((bf16[128,2816]{1,0:T(8,128)(2,1)S(1)}, bf16[128,2816]{1,0:T(8,128)(2,1)S(1)}, u32[]{:S(2)}, u32[]{:S(2)}) %collective-permute-start.31) | collective-permute-done | bytes 720928 | tf_op jit(solution)/shard_map/ppermute | solution.py:77
  177.1 3.2 copy-done.83
  180.4 5.8 fusion.120
  205.7 3.6 collective-permute-start.10
  224.5 2.6 constant_dynamic-update-slice_fusion.58
  227.2 2.6 constant_dynamic-update-slice_fusion.57
  229.7 2.6 constant_dynamic-update-slice_fusion.56
  234.5 2.4 collective-permute-start.14
  237.6 4.0 collective-permute-done.12
  242.3 5.4 collective-permute-done.13
  249.2 3.0 gather_fusion.1
  255.0 3.5 collective-permute-start.17
  260.4 2.8 collective-permute-done.17
  263.2 4.2 collective-permute-done.16
  268.2 2.6 gather_fusion.2
  272.6 2.5 multiply_reduce_fusion.3
  275.0 3.1 copy.197
  278.2 2.8 multiply_convert_fusion.6
  284.4 3.0 constant_dynamic-update-slice_fusion.54
  287.4 13.2 %fusion.121 = f32[512,5632]{1,0:T(8,128)} fusion(bf16[512,1024]{1,0:T(8,128)(2,1)S(1)} %constant_dynamic-update-slice_fusion.44, bf16[1024,5632]{1,0:T(8,128)(2,1)} %constant_dynamic-update-slice_fusion.54), kind=kOutput, calls=%fused_computation.599 | convolution fusion | flops 5905580032 | bytes 24117248 | tf_op jit(solution)/shard_map/dot_general | solution.py:53
  300.6 9.1 %multiply_convert_fusion.1 = (bf16[512,2816]{1,0:T(8,128)(2,1)}, bf16[512,2816]{1,0:T(8,128)(2,1)}, bf16[512,2816]{1,0:T(8,128)(2,1)}) fusion(f32[512,5632]{1,0:T(8,128)} %fusion.121, bf16[512,1024]{1,0:T(8,128)(2,1)} %constant_dynamic-update-slice_fusion.71, bf16[1024,2816]{0,1:T(8,128)(2,1)S(1)} %bitcast.721), kind=kOutput, calls=%fused_computation.20 | convolution fusion | flops 2961440768 | bytes 27000832 | tf_op jit(solution)/shard_map/dot_general | solution.py:53
  309.7 10.7 %fusion.5 = f32[512,1024]{1,0:T(8,128)S(1)} fusion(bf16[1024,5632]{1,0:T(8,128)(2,1)} %constant_dynamic-update-slice_fusion.54, bf16[512,2816]{1,0:T(8,128)(2,1)} %get-tuple-element.43, bf16[512,2816]{1,0:T(8,128)(2,1)} %get-tuple-element.42), kind=kOutput, calls=%fused_computation.28 | convolution fusion | flops 5917114368 | bytes 19398656 | tf_op jit(solution)/shard_map/dot_general | solution.py:61
  322.6 5.5 fusion.122
  349.2 9.1 %convolution_convert_fusion = bf16[1024,5632]{1,0:T(8,128)(2,1)} fusion(bf16[512,1024]{1,0:T(8,128)(2,1)S(1)} %copy-done.77, bf16[512,2816]{1,0:T(8,128)(2,1)S(1)} %copy-done.130, bf16[512,2816]{1,0:T(8,128)(2,1)S(1)} %copy-done.129), kind=kOutput, calls=%fused_computation.8 | convolution fusion | flops 5922881536 | bytes 18350080 | tf_op jit(solution)/shard_map/dot_general | solution.py:57
  358.3 6.8 %convolution_convert_fusion.2 = bf16[1024,2816]{1,0:T(8,128)(2,1)} fusion(bf16[512,1024]{1,0:T(8,128)(2,1)} %constant_dynamic-update-slice_fusion.71, bf16[512,2816]{1,0:T(8,128)(2,1)S(1)} %copy-done.128), kind=kOutput, calls=%fused_computation.22 | convolution fusion | flops 2955673600 | bytes 9699328 | tf_op jit(solution)/shard_map/dot_general | solution.py:57
  367.5 2.6 collective-permute-start.44
  384.1 2.8 collective-permute-start.46
  386.9 9.3 %fusion.114 = (bf16[2,2,1,128,5632]{4,3,2,1,0:T(8,128)(2,1)}, bf16[2,2,1,128,5632]{4,3,2,1,0:T(8,128)(2,1)}) fusion(bf16[2,2,2,128,5632]{4,3,2,1,0:T(8,128)(2,1)} %bitcast.651), kind=kLoop, calls=%fused_computation.592 | loop fusion | bytes 23068672 | tf_op jit(solution)/shard_map/slice | solution.py:113
  396.2 5.5 copy.323
  404.9 11.2 %collective-permute-done.47 = bf16[2,2,2,128,128]{4,3,2,1,0:T(8,128)(2,1)S(1)} collective-permute-done((bf16[2,2,2,128,128]{4,3,2,1,0:T(8,128)(2,1)S(1)}, bf16[2,2,2,128,128]{4,3,2,1,0:T(8,128)(2,1)S(1)}, u32[]{:S(2)}, u32[]{:S(2)}) %collective-permute-start.47) | collective-permute-done | bytes 262176 | tf_op jit(solution)/shard_map/ppermute | solution.py:77
  423.2 2.6 collective-permute-start.49
  429.7 4.2 collective-permute-done.50
  434.8 2.6 gather_fusion.5
  449.5 7.9 %fusion.54 = f32[512,1024]{1,0:T(8,128)S(1)} fusion(bf16[1024,4096]{1,0:T(8,128)(2,1)} %copy-done.83, bf16[512,1024]{1,0:T(8,128)(2,1)S(1)} %copy-done.35, bf16[512,1024]{1,0:T(8,128)(2,1)S(1)} %bitcast.696, bf16[512,1024]{1,0:T(8,128)(2,1)S(1)} %get-tuple-element.50, bf16[512,1024]{1,0:T(8,128)(2,1)S(1)} %get-tuple-element.49), kind=kOutput, calls=%fused_computation.163 | convolution fusion | flops 4311744512 | bytes 14680064 | tf_op jit(solution)/shard_map/dot_general | solution.py:61
  457.4 6.2 convolution_convert_fusion.1
  472.0 6.1 collective-permute-done.62
  480.6 2.8 collective-permute-done.67
  488.3 2.6 fusion.2
  495.8 2.5 collective-permute-done.65
  499.0 7.9 %collective-permute-done.80 = bf16[2,128,1408]{2,1,0:T(8,128)(2,1)S(1)} collective-permute-done((bf16[2,128,1408]{2,1,0:T(8,128)(2,1)S(1)}, bf16[2,128,1408]{2,1,0:T(8,128)(2,1)S(1)}, u32[]{:S(2)}, u32[]{:S(2)}) %collective-permute-start.80) | collective-permute-done | bytes 720928 | tf_op jit(solution)/shard_map/ppermute | solution.py:77
  509.6 5.6 collective-permute-done.85
  518.6 3.5 collective-permute-done.86
  527.8 3.2 collective-permute-done.83
  535.6 5.7 fusion
  541.5 12.5 %collective-permute-done.57 = bf16[2,128,2048]{2,1,0:T(8,128)(2,1)S(1)} collective-permute-done((bf16[2,128,2048]{2,1,0:T(8,128)(2,1)S(1)}, bf16[2,128,2048]{2,1,0:T(8,128)(2,1)S(1)}, u32[]{:S(2)}, u32[]{:S(2)}) %collective-permute-start.57) | collective-permute-done | bytes 1048608 | tf_op jit(solution)/shard_map/ppermute | solution.py:77
  553.9 2.7 fusion.11
  561.1 10.5 %collective-permute-done.54 = bf16[128,2048]{1,0:T(8,128)(2,1)S(1)} collective-permute-done((bf16[128,2048]{1,0:T(8,128)(2,1)S(1)}, bf16[128,2048]{1,0:T(8,128)(2,1)S(1)}, u32[]{:S(2)}, u32[]{:S(2)}) %collective-permute-start.54) | collective-permute-done | bytes 524320 | tf_op jit(solution)/shard_map/ppermute | solution.py:77
  572.1 19.6 %collective-permute-done.58 = bf16[128,2048]{1,0:T(8,128)(2,1)S(1)} collective-permute-done((bf16[128,2048]{1,0:T(8,128)(2,1)S(1)}, bf16[128,2048]{1,0:T(8,128)(2,1)S(1)}, u32[]{:S(2)}, u32[]{:S(2)}) %collective-permute-start.58) | collective-permute-done | bytes 524320 | tf_op jit(solution)/shard_map/ppermute | solution.py:77
  594.8 3.9 collective-permute-done.59
  601.9 2.8 collective-permute-done.60
  608.8 8.0 %collective-permute-done.72 = bf16[128,2816]{1,0:T(8,128)(2,1)S(1)} collective-permute-done((bf16[128,2816]{1,0:T(8,128)(2,1)S(1)}, bf16[128,2816]{1,0:T(8,128)(2,1)S(1)}, u32[]{:S(2)}, u32[]{:S(2)}) %collective-permute-start.72) | collective-permute-done | bytes 720928 | tf_op jit(solution)/shard_map/ppermute | solution.py:77
  621.4 5.3 collective-permute-done.73
  627.0 3.5 collective-permute-done.77
  630.9 3.6 collective-permute-done.74
  635.3 3.1 collective-permute-done.78
  (765 shorter events, 271.4 us)
Async XLA Ops:
  0.7 59.8 %collective-permute-start.18 = (bf16[128,1024]{1,0:T(8,128)(2,1)}, bf16[128,1024]{1,0:T(8,128)(2,1)}, u32[]{:S(2)}, u32[]{:S(2)}) collective-permute-start(bf16[128,1024]{1,0:T(8,128)(2,1)} %param.24), channel_id=1, source_target_pairs={{0,4},{1,5},{2,6},{3,7},{4,0},{5,1},{6,2},{7,3},{8,12},{9,13},{10,... | collective-permute-start | bytes 786440 | tf_op jit(solution)/shard_map/ppermute | solution.py:77
  1.2 55.2 %collective-permute-start.19 = (bf16[128,1024]{1,0:T(8,128)(2,1)}, bf16[128,1024]{1,0:T(8,128)(2,1)}, u32[]{:S(2)}, u32[]{:S(2)}) collective-permute-start(bf16[128,1024]{1,0:T(8,128)(2,1)} %param.24), channel_id=1, source_target_pairs={{0,8},{1,9},{2,10},{3,11},{4,12},{5,13},{6,14},{7,15},{8,0},{9,1},... | collective-permute-start | bytes 786440 | tf_op jit(solution)/shard_map/ppermute | solution.py:77
  3.7 53.9 %collective-permute-start.21 = (bf16[128,1024]{1,0:T(8,128)(2,1)}, bf16[128,1024]{1,0:T(8,128)(2,1)}, u32[]{:S(2)}, u32[]{:S(2)}) collective-permute-start(bf16[128,1024]{1,0:T(8,128)(2,1)} %param.24), channel_id=1, source_target_pairs={{0,16},{1,17},{2,18},{3,19},{4,20},{5,21},{6,22},{7,23},{8,24},{9,... | collective-permute-start | bytes 786440 | tf_op jit(solution)/shard_map/ppermute | solution.py:77
  5.3 77.8 %collective-permute-start.34 = (bf16[128,2816]{0,1:T(8,128)(2,1)}, bf16[128,2816]{0,1:T(8,128)(2,1)}, u32[]{:S(2)}, u32[]{:S(2)}) collective-permute-start(bf16[128,2816]{0,1:T(8,128)(2,1)} %bitcast.63), channel_id=1, source_target_pairs={{0,4},{1,5},{2,6},{3,7},{4,0},{5,1},{6,2},{7,3},{8,12},{9,13},{10,... | collective-permute-start | bytes 2162696 | tf_op jit(solution)/shard_map/ppermute | solution.py:77
  5.3 64.8 %collective-permute-start.35 = (bf16[128,2816]{0,1:T(8,128)(2,1)}, bf16[128,2816]{0,1:T(8,128)(2,1)}, u32[]{:S(2)}, u32[]{:S(2)}) collective-permute-start(bf16[128,2816]{0,1:T(8,128)(2,1)} %bitcast.63), channel_id=1, source_target_pairs={{0,8},{1,9},{2,10},{3,11},{4,12},{5,13},{6,14},{7,15},{8,0},{9,1},... | collective-permute-start | bytes 2162696 | tf_op jit(solution)/shard_map/ppermute | solution.py:77
  63.9 19.1 %collective-permute-start.37 = (bf16[128,2816]{0,1:T(8,128)(2,1)}, bf16[128,2816]{0,1:T(8,128)(2,1)S(1)}, u32[]{:S(2)}, u32[]{:S(2)}) collective-permute-start(bf16[128,2816]{0,1:T(8,128)(2,1)} %bitcast.63), channel_id=1, source_target_pairs={{0,16},{1,17},{2,18},{3,19},{4,20},{5,21},{6,22},{7,23},{8,24},{9,... | collective-permute-start | bytes 2162696 | tf_op jit(solution)/shard_map/ppermute | solution.py:77
  68.6 37.7 %collective-permute-start = (bf16[128,4096]{1,0:T(8,128)(2,1)S(1)}, bf16[128,4096]{1,0:T(8,128)(2,1)S(1)}, u32[]{:S(2)}, u32[]{:S(2)}) collective-permute-start(bf16[128,4096]{1,0:T(8,128)(2,1)S(1)} %copy-done.47), channel_id=1, source_target_pairs={{0,4},{1,5},{2,6},{3,7},{4,0},{5,1},{6,2},{7,3},{8,12},{9,13},{10,... | collective-permute-start | bytes 3145736 | tf_op jit(solution)/shard_map/ppermute | solution.py:77
  69.5 26.0 %collective-permute-start.1 = (bf16[128,4096]{1,0:T(8,128)(2,1)S(1)}, bf16[128,4096]{1,0:T(8,128)(2,1)S(1)}, u32[]{:S(2)}, u32[]{:S(2)}) collective-permute-start(bf16[128,4096]{1,0:T(8,128)(2,1)S(1)} %copy-done.47), channel_id=1, source_target_pairs={{0,8},{1,9},{2,10},{3,11},{4,12},{5,13},{6,14},{7,15},{8,0},{9,1},... | collective-permute-start | bytes 3145736 | tf_op jit(solution)/shard_map/ppermute | solution.py:77
  70.1 35.5 %collective-permute-start.3 = (bf16[128,4096]{1,0:T(8,128)(2,1)S(1)}, bf16[128,4096]{1,0:T(8,128)(2,1)S(1)}, u32[]{:S(2)}, u32[]{:S(2)}) collective-permute-start(bf16[128,4096]{1,0:T(8,128)(2,1)S(1)} %copy-done.47), channel_id=1, source_target_pairs={{0,16},{1,17},{2,18},{3,19},{4,20},{5,21},{6,22},{7,23},{8,24},{9,... | collective-permute-start | bytes 3145736 | tf_op jit(solution)/shard_map/ppermute | solution.py:77
  83.0 52.1 %collective-permute-start.26 = (bf16[128,5632]{1,0:T(8,128)(2,1)S(1)}, bf16[128,5632]{1,0:T(8,128)(2,1)S(1)}, u32[]{:S(2)}, u32[]{:S(2)}) collective-permute-start(bf16[128,5632]{1,0:T(8,128)(2,1)S(1)} %copy-done.39), channel_id=1, source_target_pairs={{0,4},{1,5},{2,6},{3,7},{4,0},{5,1},{6,2},{7,3},{8,12},{9,13},{10,... | collective-permute-start | bytes 4325384 | tf_op jit(solution)/shard_map/ppermute | solution.py:77
  83.1 55.6 %collective-permute-start.27 = (bf16[128,5632]{1,0:T(8,128)(2,1)S(1)}, bf16[128,5632]{1,0:T(8,128)(2,1)}, u32[]{:S(2)}, u32[]{:S(2)}) collective-permute-start(bf16[128,5632]{1,0:T(8,128)(2,1)S(1)} %copy-done.39), channel_id=1, source_target_pairs={{0,8},{1,9},{2,10},{3,11},{4,12},{5,13},{6,14},{7,15},{8,0},{9,1},... | collective-permute-start | bytes 4325384 | tf_op jit(solution)/shard_map/ppermute | solution.py:77
  95.5 17.3 %collective-permute-start.39 = (bf16[128,1408]{0,1:T(8,128)(2,1)S(1)}, bf16[128,1408]{0,1:T(8,128)(2,1)S(1)}, u32[]{:S(2)}, u32[]{:S(2)}) collective-permute-start(bf16[128,1408]{0,1:T(8,128)(2,1)S(1)} %slice.697), channel_id=1, source_target_pairs={{0,16},{1,17},{2,18},{3,19},{4,20},{5,21},{6,22},{7,23},{8,24},{9,... | collective-permute-start | bytes 1081352 | tf_op jit(solution)/shard_map/ppermute | solution.py:77
  105.5 28.0 %collective-permute-start.40 = (bf16[128,1408]{0,1:T(8,128)(2,1)S(1)}, bf16[128,1408]{0,1:T(8,128)(2,1)S(1)}, u32[]{:S(2)}, u32[]{:S(2)}) collective-permute-start(bf16[128,1408]{0,1:T(8,128)(2,1)S(1)} %slice.698), channel_id=1, source_target_pairs={{0,8},{1,9},{2,10},{3,11},{4,12},{5,13},{6,14},{7,15},{8,0},{9,1},... | collective-permute-start | bytes 1081352 | tf_op jit(solution)/shard_map/ppermute | solution.py:77
  106.3 27.3 %collective-permute-start.36 = (bf16[128,2816]{0,1:T(8,128)(2,1)}, bf16[128,2816]{0,1:T(8,128)(2,1)S(1)}, u32[]{:S(2)}, u32[]{:S(2)}) collective-permute-start(bf16[128,2816]{0,1:T(8,128)(2,1)} %collective-permute-done.35), channel_id=1, source_target_pairs={{0,4},{1,5},{2,6},{3,7},{4,0},{5,1},{6,2},{7,3},{8,12},{9,13},{10,... | collective-permute-start | bytes 2162696 | tf_op jit(solution)/shard_map/ppermute | solution.py:77
  112.9 34.6 %collective-permute-start.29 = (bf16[128,5632]{1,0:T(8,128)(2,1)S(1)}, bf16[128,5632]{1,0:T(8,128)(2,1)}, u32[]{:S(2)}, u32[]{:S(2)}) collective-permute-start(bf16[128,5632]{1,0:T(8,128)(2,1)S(1)} %copy-done.39), channel_id=1, source_target_pairs={{0,16},{1,17},{2,18},{3,19},{4,20},{5,21},{6,22},{7,23},{8,24},{9,... | collective-permute-start | bytes 4325384 | tf_op jit(solution)/shard_map/ppermute | solution.py:77
  133.6 23.9 %collective-permute-start.5 = (bf16[128,2048]{1,0:T(8,128)(2,1)S(1)}, bf16[128,2048]{1,0:T(8,128)(2,1)S(1)}, u32[]{:S(2)}, u32[]{:S(2)}) collective-permute-start(bf16[128,2048]{1,0:T(8,128)(2,1)S(1)} %slice.640), channel_id=1, source_target_pairs={{0,16},{1,17},{2,18},{3,19},{4,20},{5,21},{6,22},{7,23},{8,24},{9,... | collective-permute-start | bytes 1572872 | tf_op jit(solution)/shard_map/ppermute | solution.py:77
  135.1 23.8 %collective-permute-start.6 = (bf16[128,2048]{1,0:T(8,128)(2,1)S(1)}, bf16[128,2048]{1,0:T(8,128)(2,1)S(1)}, u32[]{:S(2)}, u32[]{:S(2)}) collective-permute-start(bf16[128,2048]{1,0:T(8,128)(2,1)S(1)} %slice.641), channel_id=1, source_target_pairs={{0,8},{1,9},{2,10},{3,11},{4,12},{5,13},{6,14},{7,15},{8,0},{9,1},... | collective-permute-start | bytes 1572872 | tf_op jit(solution)/shard_map/ppermute | solution.py:77
  138.7 22.0 %collective-permute-start.2 = (bf16[128,4096]{1,0:T(8,128)(2,1)S(1)}, bf16[128,4096]{1,0:T(8,128)(2,1)S(1)}, u32[]{:S(2)}, u32[]{:S(2)}) collective-permute-start(bf16[128,4096]{1,0:T(8,128)(2,1)S(1)} %collective-permute-done.1), channel_id=1, source_target_pairs={{0,4},{1,5},{2,6},{3,7},{4,0},{5,1},{6,2},{7,3},{8,12},{9,13},{10,... | collective-permute-start | bytes 3145736 | tf_op jit(solution)/shard_map/ppermute | solution.py:77
  141.3 18.3 %collective-permute-start.41 = (bf16[128,2816]{0,1:T(8,128)(2,1)S(1)}, bf16[128,2816]{0,1:T(8,128)(2,1)S(1)}, u32[]{:S(2)}, u32[]{:S(2)}) collective-permute-start(bf16[128,2816]{0,1:T(8,128)(2,1)S(1)} %pad_maximum_fusion.8), channel_id=1, source_target_pairs={{0,4},{1,5},{2,6},{3,7},{4,0},{5,1},{6,2},{7,3},{8,12},{9,13},{10,... | collective-permute-start | bytes 2162696 | tf_op jit(solution)/shard_map/ppermute | solution.py:77
  147.4 13.9 %collective-permute-start.4 = (bf16[128,4096]{1,0:T(8,128)(2,1)S(1)}, bf16[128,4096]{1,0:T(8,128)(2,1)S(1)}, u32[]{:S(2)}, u32[]{:S(2)}) collective-permute-start(bf16[128,4096]{1,0:T(8,128)(2,1)S(1)} %collective-permute-done.3), channel_id=1, source_target_pairs={{0,4},{1,5},{2,6},{3,7},{4,0},{5,1},{6,2},{7,3},{8,12},{9,13},{10,... | collective-permute-start | bytes 3145736 | tf_op jit(solution)/shard_map/ppermute | solution.py:77
  157.4 17.0 %collective-permute-start.31 = (bf16[128,2816]{1,0:T(8,128)(2,1)S(1)}, bf16[128,2816]{1,0:T(8,128)(2,1)S(1)}, u32[]{:S(2)}, u32[]{:S(2)}) collective-permute-start(bf16[128,2816]{1,0:T(8,128)(2,1)S(1)} %slice.693), channel_id=1, source_target_pairs={{0,16},{1,17},{2,18},{3,19},{4,20},{5,21},{6,22},{7,23},{8,24},{9,... | collective-permute-start | bytes 2162696 | tf_op jit(solution)/shard_map/ppermute | solution.py:77
  158.9 16.7 %collective-permute-start.32 = (bf16[128,2816]{1,0:T(8,128)(2,1)S(1)}, bf16[128,2816]{1,0:T(8,128)(2,1)S(1)}, u32[]{:S(2)}, u32[]{:S(2)}) collective-permute-start(bf16[128,2816]{1,0:T(8,128)(2,1)S(1)} %slice.694), channel_id=1, source_target_pairs={{0,8},{1,9},{2,10},{3,11},{4,12},{5,13},{6,14},{7,15},{8,0},{9,1},... | collective-permute-start | bytes 2162696 | tf_op jit(solution)/shard_map/ppermute | solution.py:77
  159.6 65.0 %collective-permute-start.28 = (bf16[128,5632]{1,0:T(8,128)(2,1)}, bf16[128,5632]{1,0:T(8,128)(2,1)}, u32[]{:S(2)}, u32[]{:S(2)}) collective-permute-start(bf16[128,5632]{1,0:T(8,128)(2,1)} %collective-permute-done.27), channel_id=1, source_target_pairs={{0,4},{1,5},{2,6},{3,7},{4,0},{5,1},{6,2},{7,3},{8,12},{9,13},{10,... | collective-permute-start | bytes 4325384 | tf_op jit(solution)/shard_map/ppermute | solution.py:77
  160.7 69.1 %collective-permute-start.30 = (bf16[128,5632]{1,0:T(8,128)(2,1)}, bf16[128,5632]{1,0:T(8,128)(2,1)}, u32[]{:S(2)}, u32[]{:S(2)}) collective-permute-start(bf16[128,5632]{1,0:T(8,128)(2,1)} %collective-permute-done.29), channel_id=1, source_target_pairs={{0,4},{1,5},{2,6},{3,7},{4,0},{5,1},{6,2},{7,3},{8,12},{9,13},{10,... | collective-permute-start | bytes 4325384 | tf_op jit(solution)/shard_map/ppermute | solution.py:77
  161.4 15.6 %collective-permute-start.7 = (bf16[128,4096]{1,0:T(8,128)(2,1)S(1)}, bf16[128,4096]{1,0:T(8,128)(2,1)S(1)}, u32[]{:S(2)}, u32[]{:S(2)}) collective-permute-start(bf16[128,4096]{1,0:T(8,128)(2,1)S(1)} %pad_maximum_fusion.7), channel_id=1, source_target_pairs={{0,4},{1,5},{2,6},{3,7},{4,0},{5,1},{6,2},{7,3},{8,12},{9,13},{10,... | collective-permute-start | bytes 3145736 | tf_op jit(solution)/shard_map/ppermute | solution.py:77
  205.7 12.7 %collective-permute-start.10 = (bf16[2,2,128,128]{3,2,1,0:T(8,128)(2,1)}, bf16[2,2,128,128]{3,2,1,0:T(8,128)(2,1)}, u32[]{:S(2)}, u32[]{:S(2)}) collective-permute-start(bf16[2,2,128,128]{3,2,1,0:T(8,128)(2,1)} %get-tuple-element.100), channel_id=1, source_target_pairs={{0,3},{1,2},{2,1},{3,0},{4,7},{5,6},{6,5},{7,4},{8,11},{9,10},{10,... | collective-permute-start | bytes 393224 | tf_op jit(solution)/shard_map/ppermute | solution.py:77
  209.4 9.3 %collective-permute-start.9 = (bf16[2,2,128,128]{3,2,1,0:T(8,128)(2,1)}, bf16[2,2,128,128]{3,2,1,0:T(8,128)(2,1)}, u32[]{:S(2)}, u32[]{:S(2)}) collective-permute-start(bf16[2,2,128,128]{3,2,1,0:T(8,128)(2,1)} %get-tuple-element.101), channel_id=1, source_target_pairs={{0,2},{1,3},{2,0},{3,1},{4,6},{5,7},{6,4},{7,5},{8,10},{9,11},{10,... | collective-permute-start | bytes 393224 | tf_op jit(solution)/shard_map/ppermute | solution.py:77
  209.4 9.3 %collective-permute-start.8 = (bf16[2,2,128,128]{3,2,1,0:T(8,128)(2,1)}, bf16[2,2,128,128]{3,2,1,0:T(8,128)(2,1)}, u32[]{:S(2)}, u32[]{:S(2)}) collective-permute-start(bf16[2,2,128,128]{3,2,1,0:T(8,128)(2,1)} %get-tuple-element.102), channel_id=1, source_target_pairs={{0,1},{1,0},{2,3},{3,2},{4,5},{5,4},{6,7},{7,6},{8,9},{9,8},{10,11... | collective-permute-start | bytes 393224 | tf_op jit(solution)/shard_map/ppermute | solution.py:77
  218.4 65.9 %collective-permute-start.33 = (bf16[128,5632]{1,0:T(8,128)(2,1)}, bf16[128,5632]{1,0:T(8,128)(2,1)}, u32[]{:S(2)}, u32[]{:S(2)}) collective-permute-start(bf16[128,5632]{1,0:T(8,128)(2,1)} %pad_maximum_fusion.6), channel_id=1, source_target_pairs={{0,4},{1,5},{2,6},{3,7},{4,0},{5,1},{6,2},{7,3},{8,12},{9,13},{10,... | collective-permute-start | bytes 4325384 | tf_op jit(solution)/shard_map/ppermute | solution.py:77
  224.2 8.2 %collective-permute-start.11 = (bf16[2,2,128,128]{3,2,1,0:T(8,128)(2,1)S(1)}, bf16[2,2,128,128]{3,2,1,0:T(8,128)(2,1)S(1)}, u32[]{:S(2)}, u32[]{:S(2)}) collective-permute-start(bf16[2,2,128,128]{3,2,1,0:T(8,128)(2,1)S(1)} %fusion.89), channel_id=1, source_target_pairs={{0,4},{1,5},{2,6},{3,7},{4,0},{5,1},{6,2},{7,3},{8,12},{9,13},{10,... | collective-permute-start | bytes 393224 | tf_op jit(solution)/shard_map/ppermute | solution.py:77
  232.4 9.2 %collective-permute-start.12 = (bf16[2,2,2,128,128]{4,3,2,1,0:T(8,128)(2,1)S(1)}, bf16[2,2,2,128,128]{4,3,2,1,0:T(8,128)(2,1)S(1)}, u32[]{:S(2)}, u32[]{:S(2)}) collective-permute-start(bf16[2,2,2,128,128]{4,3,2,1,0:T(8,128)(2,1)S(1)} %pad_maximum_fusion.17), channel_id=1, source_target_pairs={{0,8},{1,9},{2,10},{3,11},{4,12},{5,13},{6,14},{7,15},{8,0},{9,1},... | collective-permute-start | bytes 786440 | tf_op jit(solution)/shard_map/ppermute | solution.py:77
  233.9 13.8 %collective-permute-start.13 = (bf16[2,2,2,128,128]{4,3,2,1,0:T(8,128)(2,1)S(1)}, bf16[2,2,2,128,128]{4,3,2,1,0:T(8,128)(2,1)S(1)}, u32[]{:S(2)}, u32[]{:S(2)}) collective-permute-start(bf16[2,2,2,128,128]{4,3,2,1,0:T(8,128)(2,1)S(1)} %pad_maximum_fusion.17), channel_id=1, source_target_pairs={{0,16},{1,17},{2,18},{3,19},{4,20},{5,21},{6,22},{7,23},{8,24},{9,... | collective-permute-start | bytes 786440 | tf_op jit(solution)/shard_map/ppermute | solution.py:77
  234.5 14.0 %collective-permute-start.14 = (bf16[2,2,2,128,128]{4,3,2,1,0:T(8,128)(2,1)S(1)}, bf16[2,2,2,128,128]{4,3,2,1,0:T(8,128)(2,1)S(1)}, u32[]{:S(2)}, u32[]{:S(2)}) collective-permute-start(bf16[2,2,2,128,128]{4,3,2,1,0:T(8,128)(2,1)S(1)} %pad_maximum_fusion.17), channel_id=1, source_target_pairs={{0,24},{1,25},{2,26},{3,27},{4,28},{5,29},{6,30},{7,31},{8,16},{9,... | collective-permute-start | bytes 786440 | tf_op jit(solution)/shard_map/ppermute | solution.py:77
  258.5 8.9 %collective-permute-start.16 = (bf16[2,2,128,128]{3,2,1,0:T(8,128)(2,1)S(1)}, bf16[2,2,128,128]{3,2,1,0:T(8,128)(2,1)S(1)}, u32[]{:S(2)}, u32[]{:S(2)}) collective-permute-start(bf16[2,2,128,128]{3,2,1,0:T(8,128)(2,1)S(1)} %get-tuple-element.97), channel_id=1, source_target_pairs={{0,2},{1,3},{2,0},{3,1},{4,6},{5,7},{6,4},{7,5},{8,10},{9,11},{10,... | collective-permute-start | bytes 393224 | tf_op jit(solution)/shard_map/ppermute | solution.py:77
  258.5 8.9 %collective-permute-start.15 = (bf16[2,2,128,128]{3,2,1,0:T(8,128)(2,1)S(1)}, bf16[2,2,128,128]{3,2,1,0:T(8,128)(2,1)S(1)}, u32[]{:S(2)}, u32[]{:S(2)}) collective-permute-start(bf16[2,2,128,128]{3,2,1,0:T(8,128)(2,1)S(1)} %get-tuple-element.98), channel_id=1, source_target_pairs={{0,1},{1,0},{2,3},{3,2},{4,5},{5,4},{6,7},{7,6},{8,9},{9,8},{10,11... | collective-permute-start | bytes 393224 | tf_op jit(solution)/shard_map/ppermute | solution.py:77
  367.5 10.6 %collective-permute-start.44 = (bf16[2,2,128,128]{3,2,1,0:T(8,128)(2,1)}, bf16[2,2,128,128]{3,2,1,0:T(8,128)(2,1)}, u32[]{:S(2)}, u32[]{:S(2)}) collective-permute-start(bf16[2,2,128,128]{3,2,1,0:T(8,128)(2,1)} %get-tuple-element.92), channel_id=1, source_target_pairs={{0,3},{1,2},{2,1},{3,0},{4,7},{5,6},{6,5},{7,4},{8,11},{9,10},{10,... | collective-permute-start | bytes 393224 | tf_op jit(solution)/shard_map/ppermute | solution.py:77
  370.1 10.3 %collective-permute-start.43 = (bf16[2,2,128,128]{3,2,1,0:T(8,128)(2,1)}, bf16[2,2,128,128]{3,2,1,0:T(8,128)(2,1)}, u32[]{:S(2)}, u32[]{:S(2)}) collective-permute-start(bf16[2,2,128,128]{3,2,1,0:T(8,128)(2,1)} %get-tuple-element.93), channel_id=1, source_target_pairs={{0,2},{1,3},{2,0},{3,1},{4,6},{5,7},{6,4},{7,5},{8,10},{9,11},{10,... | collective-permute-start | bytes 393224 | tf_op jit(solution)/shard_map/ppermute | solution.py:77
  370.1 10.3 %collective-permute-start.42 = (bf16[2,2,128,128]{3,2,1,0:T(8,128)(2,1)}, bf16[2,2,128,128]{3,2,1,0:T(8,128)(2,1)}, u32[]{:S(2)}, u32[]{:S(2)}) collective-permute-start(bf16[2,2,128,128]{3,2,1,0:T(8,128)(2,1)} %get-tuple-element.94), channel_id=1, source_target_pairs={{0,1},{1,0},{2,3},{3,2},{4,5},{5,4},{6,7},{7,6},{8,9},{9,8},{10,11... | collective-permute-start | bytes 393224 | tf_op jit(solution)/shard_map/ppermute | solution.py:77
  378.0 89.3 %collective-permute-start.61 = (bf16[2,2,128,1024]{3,2,0,1:T(8,128)(2,1)}, bf16[2,2,128,1024]{3,2,0,1:T(8,128)(2,1)}, u32[]{:S(2)}, u32[]{:S(2)}) collective-permute-start(bf16[2,2,128,1024]{3,2,0,1:T(8,128)(2,1)} %bitcast.632), channel_id=1, source_target_pairs={{0,4},{1,5},{2,6},{3,7},{4,0},{5,1},{6,2},{7,3},{8,12},{9,13},{10,... | collective-permute-start | bytes 3145736 | tf_op jit(solution)/shard_map/ppermute | solution.py:77
  384.1 20.1 %collective-permute-start.46 = (bf16[2,2,2,128,128]{4,3,2,1,0:T(8,128)(2,1)S(1)}, bf16[2,2,2,128,128]{4,3,2,1,0:T(8,128)(2,1)S(1)}, u32[]{:S(2)}, u32[]{:S(2)}) collective-permute-start(bf16[2,2,2,128,128]{4,3,2,1,0:T(8,128)(2,1)S(1)} %pad_maximum_fusion.19), channel_id=1, source_target_pairs={{0,8},{1,9},{2,10},{3,11},{4,12},{5,13},{6,14},{7,15},{8,0},{9,1},... | collective-permute-start | bytes 786440 | tf_op jit(solution)/shard_map/ppermute | solution.py:77
  401.7 133.4 %collective-permute-start.70 = (bf16[2,2,128,5632]{3,2,0,1:T(8,128)(2,1)}, bf16[2,2,128,5632]{3,2,0,1:T(8,128)(2,1)}, u32[]{:S(2)}, u32[]{:S(2)}) collective-permute-start(bf16[2,2,128,5632]{3,2,0,1:T(8,128)(2,1)} %bitcast.628), channel_id=1, source_target_pairs={{0,4},{1,5},{2,6},{3,7},{4,0},{5,1},{6,2},{7,3},{8,12},{9,13},{10,... | collective-permute-start | bytes 17301512 | tf_op jit(solution)/shard_map/ppermute | solution.py:77
  401.7 14.3 %collective-permute-start.47 = (bf16[2,2,2,128,128]{4,3,2,1,0:T(8,128)(2,1)S(1)}, bf16[2,2,2,128,128]{4,3,2,1,0:T(8,128)(2,1)S(1)}, u32[]{:S(2)}, u32[]{:S(2)}) collective-permute-start(bf16[2,2,2,128,128]{4,3,2,1,0:T(8,128)(2,1)S(1)} %pad_maximum_fusion.19), channel_id=1, source_target_pairs={{0,16},{1,17},{2,18},{3,19},{4,20},{5,21},{6,22},{7,23},{8,24},{9,... | collective-permute-start | bytes 786440 | tf_op jit(solution)/shard_map/ppermute | solution.py:77
  401.9 14.9 %collective-permute-start.48 = (bf16[2,2,2,128,128]{4,3,2,1,0:T(8,128)(2,1)S(1)}, bf16[2,2,2,128,128]{4,3,2,1,0:T(8,128)(2,1)S(1)}, u32[]{:S(2)}, u32[]{:S(2)}) collective-permute-start(bf16[2,2,2,128,128]{4,3,2,1,0:T(8,128)(2,1)S(1)} %pad_maximum_fusion.19), channel_id=1, source_target_pairs={{0,24},{1,25},{2,26},{3,27},{4,28},{5,29},{6,30},{7,31},{8,16},{9,... | collective-permute-start | bytes 786440 | tf_op jit(solution)/shard_map/ppermute | solution.py:77
  421.3 8.4 %collective-permute-start.51 = (bf16[2,2,128,128]{3,2,1,0:T(8,128)(2,1)S(1)}, bf16[2,2,128,128]{3,2,1,0:T(8,128)(2,1)S(1)}, u32[]{:S(2)}, u32[]{:S(2)}) collective-permute-start(bf16[2,2,128,128]{3,2,1,0:T(8,128)(2,1)S(1)} %get-tuple-element.88), channel_id=1, source_target_pairs={{0,3},{1,2},{2,1},{3,0},{4,7},{5,6},{6,5},{7,4},{8,11},{9,10},{10,... | collective-permute-start | bytes 393224 | tf_op jit(solution)/shard_map/ppermute | solution.py:77
  423.2 10.7 %collective-permute-start.50 = (bf16[2,2,128,128]{3,2,1,0:T(8,128)(2,1)S(1)}, bf16[2,2,128,128]{3,2,1,0:T(8,128)(2,1)S(1)}, u32[]{:S(2)}, u32[]{:S(2)}) collective-permute-start(bf16[2,2,128,128]{3,2,1,0:T(8,128)(2,1)S(1)} %get-tuple-element.89), channel_id=1, source_target_pairs={{0,2},{1,3},{2,0},{3,1},{4,6},{5,7},{6,4},{7,5},{8,10},{9,11},{10,... | collective-permute-start | bytes 393224 | tf_op jit(solution)/shard_map/ppermute | solution.py:77
  423.2 10.7 %collective-permute-start.49 = (bf16[2,2,128,128]{3,2,1,0:T(8,128)(2,1)S(1)}, bf16[2,2,128,128]{3,2,1,0:T(8,128)(2,1)S(1)}, u32[]{:S(2)}, u32[]{:S(2)}) collective-permute-start(bf16[2,2,128,128]{3,2,1,0:T(8,128)(2,1)S(1)} %get-tuple-element.90), channel_id=1, source_target_pairs={{0,1},{1,0},{2,3},{3,2},{4,5},{5,4},{6,7},{7,6},{8,9},{9,8},{10,11... | collective-permute-start | bytes 393224 | tf_op jit(solution)/shard_map/ppermute | solution.py:77
  429.7 58.6 %collective-permute-start.79 = (bf16[2,2,128,2816]{3,2,0,1:T(8,128)(2,1)}, bf16[2,2,128,2816]{3,2,0,1:T(8,128)(2,1)}, u32[]{:S(2)}, u32[]{:S(2)}) collective-permute-start(bf16[2,2,128,2816]{3,2,0,1:T(8,128)(2,1)} %bitcast.630), channel_id=1, source_target_pairs={{0,4},{1,5},{2,6},{3,7},{4,0},{5,1},{6,2},{7,3},{8,12},{9,13},{10,... | collective-permute-start | bytes 8650760 | tf_op jit(solution)/shard_map/ppermute | solution.py:77
  467.2 64.6 %collective-permute-start.52 = (bf16[2,2,128,4096]{3,2,0,1:T(8,128)(2,1)S(1)}, bf16[2,2,128,4096]{3,2,0,1:T(8,128)(2,1)S(1)}, u32[]{:S(2)}, u32[]{:S(2)}) collective-permute-start(bf16[2,2,128,4096]{3,2,0,1:T(8,128)(2,1)S(1)} %bitcast.676), channel_id=1, source_target_pairs={{0,4},{1,5},{2,6},{3,7},{4,0},{5,1},{6,2},{7,3},{8,12},{9,13},{10,... | collective-permute-start | bytes 12582920 | tf_op jit(solution)/shard_map/ppermute | solution.py:77
  469.7 8.3 %collective-permute-start.62 = (bf16[2,128,512]{2,1,0:T(8,128)(2,1)S(1)}, bf16[2,128,512]{2,1,0:T(8,128)(2,1)S(1)}, u32[]{:S(2)}, u32[]{:S(2)}) collective-permute-start(bf16[2,128,512]{2,1,0:T(8,128)(2,1)S(1)} %slice_bitcast_fusion.26), channel_id=1, source_target_pairs={{0,8},{1,9},{2,10},{3,11},{4,12},{5,13},{6,14},{7,15},{8,0},{9,1},... | collective-permute-start | bytes 786440 | tf_op jit(solution)/shard_map/ppermute | solution.py:77
  469.8 8.3 %collective-permute-start.66 = (bf16[2,128,512]{2,1,0:T(8,128)(2,1)S(1)}, bf16[2,128,512]{2,1,0:T(8,128)(2,1)S(1)}, u32[]{:S(2)}, u32[]{:S(2)}) collective-permute-start(bf16[2,128,512]{2,1,0:T(8,128)(2,1)S(1)} %slice_bitcast_fusion.24), channel_id=1, source_target_pairs={{0,16},{1,17},{2,18},{3,19},{4,20},{5,21},{6,22},{7,23},{8,24},{9,... | collective-permute-start | bytes 786440 | tf_op jit(solution)/shard_map/ppermute | solution.py:77
  491.0 15.9 %collective-permute-start.80 = (bf16[2,128,1408]{2,1,0:T(8,128)(2,1)S(1)}, bf16[2,128,1408]{2,1,0:T(8,128)(2,1)S(1)}, u32[]{:S(2)}, u32[]{:S(2)}) collective-permute-start(bf16[2,128,1408]{2,1,0:T(8,128)(2,1)S(1)} %slice_bitcast_fusion.10), channel_id=1, source_target_pairs={{0,8},{1,9},{2,10},{3,11},{4,12},{5,13},{6,14},{7,15},{8,0},{9,1},... | collective-permute-start | bytes 2162696 | tf_op jit(solution)/shard_map/ppermute | solution.py:77
  492.8 14.5 %collective-permute-start.84 = (bf16[2,128,1408]{2,1,0:T(8,128)(2,1)S(1)}, bf16[2,128,1408]{2,1,0:T(8,128)(2,1)S(1)}, u32[]{:S(2)}, u32[]{:S(2)}) collective-permute-start(bf16[2,128,1408]{2,1,0:T(8,128)(2,1)S(1)} %slice_bitcast_fusion.8), channel_id=1, source_target_pairs={{0,16},{1,17},{2,18},{3,19},{4,20},{5,21},{6,22},{7,23},{8,24},{9,... | collective-permute-start | bytes 2162696 | tf_op jit(solution)/shard_map/ppermute | solution.py:77
  509.0 8.2 %collective-permute-start.81 = (bf16[128,1408]{1,0:T(8,128)(2,1)S(1)}, bf16[128,1408]{1,0:T(8,128)(2,1)S(1)}, u32[]{:S(2)}, u32[]{:S(2)}) collective-permute-start(bf16[128,1408]{1,0:T(8,128)(2,1)S(1)} %slice_bitcast_fusion.22), channel_id=1, source_target_pairs={{0,16},{1,17},{2,18},{3,19},{4,20},{5,21},{6,22},{7,23},{8,24},{9,... | collective-permute-start | bytes 1081352 | tf_op jit(solution)/shard_map/ppermute | solution.py:77
  533.6 20.3 %collective-permute-start.57 = (bf16[2,128,2048]{2,1,0:T(8,128)(2,1)S(1)}, bf16[2,128,2048]{2,1,0:T(8,128)(2,1)S(1)}, u32[]{:S(2)}, u32[]{:S(2)}) collective-permute-start(bf16[2,128,2048]{2,1,0:T(8,128)(2,1)S(1)} %slice_bitcast_fusion.4), channel_id=1, source_target_pairs={{0,16},{1,17},{2,18},{3,19},{4,20},{5,21},{6,22},{7,23},{8,24},{9,... | collective-permute-start | bytes 3145736 | tf_op jit(solution)/shard_map/ppermute | solution.py:77
  534.4 19.6 %collective-permute-start.53 = (bf16[2,128,2048]{2,1,0:T(8,128)(2,1)S(1)}, bf16[2,128,2048]{2,1,0:T(8,128)(2,1)}, u32[]{:S(2)}, u32[]{:S(2)}) collective-permute-start(bf16[2,128,2048]{2,1,0:T(8,128)(2,1)S(1)} %slice_bitcast_fusion.6), channel_id=1, source_target_pairs={{0,8},{1,9},{2,10},{3,11},{4,12},{5,13},{6,14},{7,15},{8,0},{9,1},... | collective-permute-start | bytes 3145736 | tf_op jit(solution)/shard_map/ppermute | solution.py:77
  556.7 14.9 %collective-permute-start.54 = (bf16[128,2048]{1,0:T(8,128)(2,1)S(1)}, bf16[128,2048]{1,0:T(8,128)(2,1)S(1)}, u32[]{:S(2)}, u32[]{:S(2)}) collective-permute-start(bf16[128,2048]{1,0:T(8,128)(2,1)S(1)} %slice_bitcast_fusion.18), channel_id=1, source_target_pairs={{0,16},{1,17},{2,18},{3,19},{4,20},{5,21},{6,22},{7,23},{8,24},{9,... | collective-permute-start | bytes 1572872 | tf_op jit(solution)/shard_map/ppermute | solution.py:77
  557.7 47.1 %collective-permute-start.75 = (bf16[2,128,2816]{2,1,0:T(8,128)(2,1)S(1)}, bf16[2,128,2816]{2,1,0:T(8,128)(2,1)S(1)}, u32[]{:S(2)}, u32[]{:S(2)}) collective-permute-start(bf16[2,128,2816]{2,1,0:T(8,128)(2,1)S(1)} %slice_bitcast_fusion), channel_id=1, source_target_pairs={{0,16},{1,17},{2,18},{3,19},{4,20},{5,21},{6,22},{7,23},{8,24},{9,... | collective-permute-start | bytes 4325384 | tf_op jit(solution)/shard_map/ppermute | solution.py:77
  558.9 45.8 %collective-permute-start.71 = (bf16[2,128,2816]{2,1,0:T(8,128)(2,1)S(1)}, bf16[2,128,2816]{2,1,0:T(8,128)(2,1)S(1)}, u32[]{:S(2)}, u32[]{:S(2)}) collective-permute-start(bf16[2,128,2816]{2,1,0:T(8,128)(2,1)S(1)} %slice_bitcast_fusion.2), channel_id=1, source_target_pairs={{0,8},{1,9},{2,10},{3,11},{4,12},{5,13},{6,14},{7,15},{8,0},{9,1},... | collective-permute-start | bytes 4325384 | tf_op jit(solution)/shard_map/ppermute | solution.py:77
  559.5 32.2 %collective-permute-start.58 = (bf16[128,2048]{1,0:T(8,128)(2,1)S(1)}, bf16[128,2048]{1,0:T(8,128)(2,1)S(1)}, u32[]{:S(2)}, u32[]{:S(2)}) collective-permute-start(bf16[128,2048]{1,0:T(8,128)(2,1)S(1)} %slice_bitcast_fusion.16), channel_id=1, source_target_pairs={{0,8},{1,9},{2,10},{3,11},{4,12},{5,13},{6,14},{7,15},{8,0},{9,1},... | collective-permute-start | bytes 1572872 | tf_op jit(solution)/shard_map/ppermute | solution.py:77
  571.8 22.5 %collective-permute-start.55 = (bf16[2,32,2048]{2,1,0:T(8,128)(2,1)S(1)}, bf16[2,32,2048]{2,1,0:T(8,128)(2,1)S(1)}, u32[]{:S(2)}, u32[]{:S(2)}) collective-permute-start(bf16[2,32,2048]{2,1,0:T(8,128)(2,1)S(1)} %dynamic-slice_bitcast_fusion.3), channel_id=1, source_target_pairs={{0,1},{1,0},{2,3},{3,2},{4,5},{5,4},{6,7},{7,6},{8,9},{9,8},{10,11... | collective-permute-start | bytes 786440 | tf_op jit(solution)/shard_map/ppermute | solution.py:77
  605.5 11.4 %collective-permute-start.72 = (bf16[128,2816]{1,0:T(8,128)(2,1)S(1)}, bf16[128,2816]{1,0:T(8,128)(2,1)S(1)}, u32[]{:S(2)}, u32[]{:S(2)}) collective-permute-start(bf16[128,2816]{1,0:T(8,128)(2,1)S(1)} %slice_bitcast_fusion.14), channel_id=1, source_target_pairs={{0,16},{1,17},{2,18},{3,19},{4,20},{5,21},{6,22},{7,23},{8,24},{9,... | collective-permute-start | bytes 2162696 | tf_op jit(solution)/shard_map/ppermute | solution.py:77
  607.7 11.4 %collective-permute-start.76 = (bf16[128,2816]{1,0:T(8,128)(2,1)S(1)}, bf16[128,2816]{1,0:T(8,128)(2,1)S(1)}, u32[]{:S(2)}, u32[]{:S(2)}) collective-permute-start(bf16[128,2816]{1,0:T(8,128)(2,1)S(1)} %slice_bitcast_fusion.12), channel_id=1, source_target_pairs={{0,8},{1,9},{2,10},{3,11},{4,12},{5,13},{6,14},{7,15},{8,0},{9,1},... | collective-permute-start | bytes 2162696 | tf_op jit(solution)/shard_map/ppermute | solution.py:77
  617.0 9.6 %collective-permute-start.73 = (bf16[2,32,2816]{2,1,0:T(8,128)(2,1)S(1)}, bf16[2,32,2816]{2,1,0:T(8,128)(2,1)S(1)}, u32[]{:S(2)}, u32[]{:S(2)}) collective-permute-start(bf16[2,32,2816]{2,1,0:T(8,128)(2,1)S(1)} %dynamic-slice_bitcast_fusion.1), channel_id=1, source_target_pairs={{0,1},{1,0},{2,3},{3,2},{4,5},{5,4},{6,7},{7,6},{8,9},{9,8},{10,11... | collective-permute-start | bytes 1081352 | tf_op jit(solution)/shard_map/ppermute | solution.py:77
  619.3 11.2 %collective-permute-start.77 = (bf16[2,32,2816]{2,1,0:T(8,128)(2,1)S(1)}, bf16[2,32,2816]{2,1,0:T(8,128)(2,1)S(1)}, u32[]{:S(2)}, u32[]{:S(2)}) collective-permute-start(bf16[2,32,2816]{2,1,0:T(8,128)(2,1)S(1)} %dynamic-slice_bitcast_fusion), channel_id=1, source_target_pairs={{0,1},{1,0},{2,3},{3,2},{4,5},{5,4},{6,7},{7,6},{8,9},{9,8},{10,11... | collective-permute-start | bytes 1081352 | tf_op jit(solution)/shard_map/ppermute | solution.py:77
  (163 other events, 927.1 us)

commit v2 on v1

--- a/solution.py
+++ b/solution.py
@@ -1,8 +1,11 @@
+import functools
 import math
 
 import jax
 import jax.numpy as jnp
 from jax import lax
+from jax.experimental import pallas as pl
+from jax.experimental.pallas import tpu as pltpu
 from jax.sharding import PartitionSpec as P
 
 H = 8
@@ -11,6 +14,12 @@
 AXES = ("fsdp", "head")
 F32 = jnp.float32
 BF16 = jnp.bfloat16
+MESH = pl.DeviceIdType.MESH
+ANY = pl.BlockSpec(memory_space=pl.ANY)
+VMEM = pl.BlockSpec(memory_space=pltpu.VMEM)
+SMEM = pl.BlockSpec(memory_space=pltpu.SMEM)
+VMEM_BYTES = 63 * 1024 * 1024
+TILE = 256
 
 
 def norm_parts(values):
@@ -238,7 +247,7 @@
     return within, entering[..., None], leaving[..., None]
 
 
-def local(
+def local_any(
     tokens,
     cotangent,
     lengths,
@@ -377,8 +386,606 @@
     )
 
 
+def flip(index, bit):
+    return index + bit - 2 * bit * ((index // bit) % 2)
+
+
+def kdot(a, b, dims=((1,), (0,))):
+    return lax.dot_general(a, b, (dims, ((), ())), preferred_element_type=F32)
+
+
+def cols(start, size):
+    return pl.ds(pl.multiple_of(start, 128), size)
+
+
+class Place:
+    def __init__(self):
+        self.f = lax.axis_index("fsdp")
+        self.z = lax.axis_index("head")
+        self.fc, self.fx, self.fy = (flip(self.f, b) for b in (1, 2, 4))
+        self.fxy = flip(self.fx, 4)
+        self.zs = [flip(self.z, 1), flip(self.z, 2), flip(flip(self.z, 1), 2)]
+
+    def at(self, f=None, z=None):
+        return {"fsdp": self.f if f is None else f, "head": self.z if z is None else z}
+
+    def greet(self):
+        barrier = pltpu.get_barrier_semaphore()
+        others = [self.at(f=f) for f in (self.fc, self.fx, self.fy, self.fxy)]
+        others += [self.at(z=z) for z in self.zs]
+        for other in others:
+            pl.semaphore_signal(barrier, inc=1, device_id=other, device_id_type=MESH)
+        pl.semaphore_wait(barrier, len(others))
+
+
+class Scan:
+    def __init__(self, place, table, base, states, inbox, totals, outbox, result, send, recv):
+        self.p, self.table, self.base = place, table, base
+        self.states, self.inbox, self.totals = states, inbox, totals
+        self.outbox, self.result = outbox, result
+        self.send, self.recv = send, recv
+
+    def copy(self, src, dst, n, where):
+        return pltpu.make_async_remote_copy(
+            src_ref=src,
+            dst_ref=dst,
+            send_sem=self.send.at[n],
+            recv_sem=self.recv.at[n],
+            device_id=where,
+            device_id_type=MESH,
+        )
+
+    def to_heads(self, i):
+        z = self.p.zs[i]
+        return self.copy(self.states.at[pl.ds(2 * z, 2)], self.inbox.at[self.p.z], i, self.p.at(z=z))
+
+    def from_heads(self, i):
+        z = self.p.zs[i]
+        return self.copy(
+            self.outbox.at[z], self.result.at[pl.ds(2 * self.p.z, 2)], 9 + i, self.p.at(z=z)
+        )
+
+    def total(self, n, origin, where):
+        return self.copy(self.totals.at[origin], self.totals.at[origin], n, self.p.at(f=where))
+
+    def start(self):
+        p = self.p
+        for i in range(3):
+            self.to_heads(i).start()
+        self.inbox[p.z] = self.states[pl.ds(2 * p.z, 2)]
+
+    def factor(self, offset):
+        return self.table[self.base + offset]
+
+    def totals_out(self):
+        p = self.p
+        for i in range(3):
+            self.to_heads(i).wait()
+        for hh in range(2):
+            for m in range(2):
+                acc = self.factor((m * 4) * 2 + hh) * self.inbox[0, hh, m].astype(F32)
+                for i in range(1, 4):
+                    acc += self.factor((m * 4 + i) * 2 + hh) * self.inbox[i, hh, m].astype(F32)
+                self.totals[p.f, hh, m] = acc.astype(BF16)
+        for n, where in ((3, p.fx), (4, p.fy), (5, p.fxy)):
+            self.total(n, p.f, where).start()
+        self.total(12, p.f, p.fc).start()
+
+    def forward(self):
+        p = self.p
+        for n, where in ((3, p.fx), (4, p.fy), (5, p.fxy)):
+            self.total(n, p.f, where).wait()
+            self.total(n + 3, where, p.fc).start()
+
+    def results_out(self):
+        p = self.p
+        self.total(12, p.f, p.fc).wait()
+        for n, where in ((3, p.fx), (4, p.fy), (5, p.fxy)):
+            self.total(n + 3, where, p.fc).wait()
+        for hh in range(2):
+            for m in range(2):
+                outer = self.factor(16 + (m * 8) * 2 + hh) * self.totals[0, hh, m].astype(F32)
+                for g in range(1, 8):
+                    outer += self.factor(16 + (m * 8 + g) * 2 + hh) * self.totals[
+                        g, hh, m
+                    ].astype(F32)
+                for i in range(4):
+                    acc = self.factor(48 + (m * 4 + i) * 2 + hh) * outer
+                    for j in range(4):
+                        if i != j:
+                            acc += self.factor(64 + ((m * 4 + i) * 4 + j) * 2 + hh) * self.inbox[
+                                j, hh, m
+                            ].astype(F32)
+                    self.outbox[i, hh, m] = acc.astype(BF16)
+        for i in range(3):
+            self.from_heads(i).start()
+        self.result[pl.ds(2 * p.z, 2)] = self.outbox[p.z]
+
+    def finish(self):
+        for i in range(3):
+            self.from_heads(i).wait()
+
+
+def edge(seg, mark, rate, gap):
+    return jnp.where(seg == mark, jnp.exp(-rate * gap), 0.0)
+
+
+def decays(rate, rows):
+    up = lax.broadcasted_iota(jnp.int32, (rows, rows), 0)
+    across = lax.broadcasted_iota(jnp.int32, (rows, rows), 1)
+    gap = (up - across).astype(F32)
+    return jnp.where(gap >= 0.0, jnp.exp(-rate * jnp.maximum(gap, 0.0)), 0.0)
+
+
+def forward_kernel(
+    table, marks, x, cosine, sine, seg_col, seg_row,
+    wq, wk, wv, wu, wo, w1, w2, wd,
+    mix_o, wo_o, w1_o, w2_o, wd_o, q_o, k_o, v_o, u_o, qp_o, kp_o, ob_o, hid_o, p1_o, p2_o, s_o,
+    state_o, mixed_o,
+    fm, fo, f1, f2, fd, a1, q, k, v, u, qp, kp, att, ob, g, hid, p1, p2, s, mixed,
+    states, inbox, totals, outbox, result,
+    send, recv, own_sem, save_sem, scan_send, scan_recv,
+):
+    place = Place()
+    f = place.f
+    rows, width = x.shape
+    chunk = rows // 2
+    hidden_size = w1.shape[1]
+    half_hidden = hidden_size // 2
+    place.greet()
+
+    pieces = []
+    for i, w in enumerate((wq, wk, wv, wu)):
+        pieces.append((w, fm, (0, 128), (0, width), (0, i * width)))
+    pieces.append((wo, fo, (0, 128), (0, width), (0, 0)))
+    for part in range(2):
+        for w, full in ((w1, f1), (w2, f2)):
+            pieces.append((w, full, (0, 128), (part * half_hidden, half_hidden), (0, part * half_hidden)))
+    for part in range(2):
+        pieces.append((wd, fd, (part * half_hidden, half_hidden), (0, 128), None))
+    count = len(pieces)
+
+    def own(n):
+        w, _, (r, rs), (c, cs), _ = pieces[n]
+        return w.at[pl.ds(r, rs), pl.ds(c, cs)]
+
+    def block(n, origin, half=None):
+        _, full, (r, rs), (c, cs), to = pieces[n]
+        if to is None:
+            start, size, at, wide = r, rs, origin * 128, 128
+            if half is not None:
+                start, size = r + half * (rs // 2), rs // 2
+            return full.at[pl.ds(start, size), cols(at, wide)]
+        start, size = origin * 128, 128
+        if half is not None:
+            start, size = start + half * 64, 64
+        return full.at[pl.ds(pl.multiple_of(start, 64), size), pl.ds(to[1], cs)]
+
+    def move(n, step, src, dst, where):
+        return pltpu.make_async_remote_copy(
+            src_ref=src,
+            dst_ref=dst,
+            send_sem=send.at[n * 8 + step],
+            recv_sem=recv.at[n * 8 + step],
+            device_id=place.at(f=where),
+            device_id_type=MESH,
+        )
+
+    fc, fx, fy, fxy = place.fc, place.fx, place.fy, place.fxy
+
+    def steps(n):
+        return [
+            (own(n), block(n, f), fc, block(n, fc)),
+            (own(n), block(n, f), fx, block(n, fx)),
+            (own(n), block(n, f), fy, block(n, fy)),
+            (block(n, fx, 0), block(n, fx, 0), fy, block(n, fxy, 0)),
+            (block(n, fy, 1), block(n, fy, 1), fx, block(n, fxy, 1)),
+            (block(n, fx), block(n, fx), fc, block(n, flip(fx, 1))),
+            (block(n, fy), block(n, fy), fc, block(n, flip(fy, 1))),
+            (block(n, fxy), block(n, fxy), fc, block(n, flip(fxy, 1))),
+        ]
+
+    def go(n, step):
+        src, dst, where, _ = steps(n)[step]
+        move(n, step, src, dst, where).start()
+
+    def got(n, step):
+        _, _, where, dst = steps(n)[step]
+        move(n, step, dst, dst, where).wait_recv()
+
+    def own_copy(n):
+        return pltpu.make_async_copy(own(n), block(n, f), own_sem.at[n])
+
+    saves = []
+
+    def save(src, dst):
+        copy = pltpu.make_async_copy(src, dst, save_sem.at[len(saves)])
+        copy.start()
+        saves.append(copy)
+
+    def save_piece(n):
+        full_o = {id(fm): mix_o, id(fo): wo_o, id(f1): w1_o, id(f2): w2_o, id(fd): wd_o}
+        _, full, (r, rs), (c, cs), to = pieces[n]
+        out = full_o[id(full)]
+        if to is None:
+            save(full.at[pl.ds(r, rs)], out.at[pl.ds(r, rs)])
+        else:
+            save(full.at[:, pl.ds(to[1], cs)], out.at[:, pl.ds(to[1], cs)])
+
+    def norm_in():
+        @pl.loop(0, rows // 128)
+        def _(t):
+            at = pl.ds(pl.multiple_of(t * 128, 128), 128)
+            value = x[at, :].astype(F32)
+            scale = lax.rsqrt(jnp.mean(value * value, axis=-1, keepdims=True) + EPSILON)
+            a1[at, :] = (value * scale).astype(BF16)
+
+    def project(base, pre, low, turn):
+        @pl.loop(0, width // TILE)
+        def _(t):
+            at = cols(t * TILE, TILE)
+            acc = kdot(a1[...], fm[:, cols(base + t * TILE, TILE)])
+            if not turn:
+                low[:, at] = acc.astype(BF16)
+                return
+            pre[:, at] = acc.astype(BF16)
+            acc = acc * lax.logistic(acc)
+            turned = []
+            for hh in range(TILE // DH):
+                piece = acc[:, hh * DH : (hh + 1) * DH]
+                turned.append(piece * cosine[...] + pltpu.roll(piece, DH // 2, 1) * sine[...])
+            low[:, at] = jnp.concatenate(turned, axis=1).astype(BF16)
+
+    offset = lax.broadcasted_iota(jnp.int32, (chunk, 1), 0).astype(F32)
+    scan = Scan(
+        place, table, 8, states, inbox, totals, outbox, result, scan_send, scan_recv
+    )
+
+    def local_states():
+        @pl.loop(0, H)
+        def _(h):
+            at = cols(h * DH, DH)
+            for m in range(2):
+                r = slice(m * chunk, (m + 1) * chunk)
+                leaving = edge(seg_col[r], marks[2 + m], table[h], chunk - 1.0 - offset)
+                left = (k[r, at].astype(F32) * leaving).astype(BF16)
+                states[h, m] = kdot(left, v[r, at], ((0,), (0,))).astype(BF16)
+
+    def attend_local():
+        @pl.loop(0, H)
+        def _(h):
+            at = cols(h * DH, DH)
+            decay = decays(table[h], chunk)
+            for m in range(2):
+                r = slice(m * chunk, (m + 1) * chunk)
+                within = jnp.where(seg_col[r] == seg_row[m : m + 1], decay, 0.0)
+                scores = kdot(q[r, at], k[r, at], ((1,), (1,))) * within
+                att[r, at] = kdot(scores.astype(BF16), v[r, at])
+
+    def attend_rest():
+        @pl.loop(0, H)
+        def _(h):
+            at = cols(h * DH, DH)
+            for m in range(2):
+                r = slice(m * chunk, (m + 1) * chunk)
+                entering = edge(seg_col[r], marks[m], table[h], offset + 1.0)
+                ob[r, at] = (att[r, at] + entering * kdot(q[r, at], result[h, m])).astype(BF16)
+
+    def hidden():
+        @pl.loop(0, rows // 128)
+        def _(t):
+            at = pl.ds(pl.multiple_of(t * 128, 128), 128)
+            value = ob[at, :].astype(F32)
+            scale = lax.rsqrt(jnp.mean(value * value, axis=-1, keepdims=True) + EPSILON)
+            g[at, :] = (value * scale * u[at, :].astype(F32)).astype(BF16)
+
+        @pl.loop(0, width // TILE)
+        def _(t):
+            at = cols(t * TILE, TILE)
+            hid[:, at] = x[:, at].astype(F32) + kdot(g[...], fo[:, at])
+
+        @pl.loop(0, rows // 128)
+        def _(t):
+            at = pl.ds(pl.multiple_of(t * 128, 128), 128)
+            value = hid[at, :]
+            scale = lax.rsqrt(jnp.mean(value * value, axis=-1, keepdims=True) + EPSILON)
+            g[at, :] = (value * scale).astype(BF16)
+
+    def up():
+        @pl.loop(0, hidden_size // TILE)
+        def _(t):
+            at = cols(t * TILE, TILE)
+            first = kdot(g[...], f1[:, at])
+            second = kdot(g[...], f2[:, at])
+            p1[:, at] = first.astype(BF16)
+            p2[:, at] = second.astype(BF16)
+            s[:, at] = (first * second).astype(BF16)
+
+    def down():
+        @pl.loop(0, width // TILE)
+        def _(t):
+            at = cols(t * TILE, TILE)
+            mixed[:, at] = (hid[:, at] + kdot(s[...], fd[:, at])).astype(BF16)
+
+    def work(n):
+        if n == 0:
+            project(0, qp, q, True)
+            save(q, q_o)
+            save(qp, qp_o)
+        elif n == 1:
+            project(width, kp, k, True)
+            save(k, k_o)
+            save(kp, kp_o)
+        elif n == 2:
+            project(2 * width, None, v, False)
+            local_states()
+            scan.start()
+            save(v, v_o)
+        elif n == 3:
+            project(3 * width, None, u, False)
+            save(u, u_o)
+            scan.totals_out()
+        elif n == 4:
+            attend_local()
+            scan.forward()
+        elif n == 5:
+            scan.results_out()
+        elif n == 6:
+            scan.finish()
+            save(result, state_o)
+            attend_rest()
+            save(ob, ob_o)
+            hidden()
+            save(hid, hid_o)
+        elif n == 8:
+            up()
+            save(p1, p1_o)
+            save(p2, p2_o)
+            save(s, s_o)
+        elif n == 10:
+            down()
+            save(mixed, mixed_o)
+
+    for n in range(2):
+        for step in (1, 2, 0):
+            go(n, step)
+        own_copy(n).start()
+    norm_in()
+    for n in range(count + 2):
+        if n < count:
+            got(n, 1)
+            go(n, 3)
+            go(n, 5)
+            got(n, 2)
+            go(n, 4)
+            go(n, 6)
+            if n + 2 < count:
+                for step in (1, 2, 0):
+                    go(n + 2, step)
+                own_copy(n + 2).start()
+        if 0 <= n - 1 < count:
+            got(n - 1, 3)
+            got(n - 1, 4)
+            go(n - 1, 7)
+        if n - 2 >= 0:
+            for step in (0, 5, 6, 7):
+                got(n - 2, step)
+            own_copy(n - 2).wait()
+            save_piece(n - 2)
+            work(n - 2)
+    for n in range(count):
+        for step in range(8):
+            src, dst, where, _ = steps(n)[step]
+            move(n, step, src, dst, where).wait_send()
+    for copy in saves:
+        copy.wait()
+
+
+def run_forward(table, marks, x, cosine, sine, seg_col, seg_row, weights):
+    rows, width = x.shape
+    hidden_size = weights[5].shape[1]
+    row = jax.ShapeDtypeStruct((rows, width), BF16)
+    tall = jax.ShapeDtypeStruct((rows, hidden_size), BF16)
+    outs = (
+        [
+            jax.ShapeDtypeStruct(shape, BF16)
+            for shape in (
+                (width, 4 * width), (width, width), (width, hidden_size), (width, hidden_size),
+                (hidden_size, width),
+            )
+        ]
+        + [row] * 7
+        + [jax.ShapeDtypeStruct((rows, width), F32)]
+        + [tall] * 3
+        + [jax.ShapeDtypeStruct((H, 2, DH, DH), BF16), row]
+    )
+    rv = pltpu.VMEM((rows, width), BF16)
+    tv = pltpu.VMEM((rows, hidden_size), BF16)
+    scratch = (
+        [pltpu.VMEM(o.shape, BF16) for o in outs[:5]]
+        + [rv] * 7
+        + [pltpu.VMEM((rows, width), F32), rv, rv, pltpu.VMEM((rows, width), F32)]
+        + [tv] * 3
+        + [rv]
+        + scan_scratch()
+        + [pltpu.SemaphoreType.DMA((88,))] * 2
+        + [pltpu.SemaphoreType.DMA((11,)), pltpu.SemaphoreType.DMA((24,))]
+        + [pltpu.SemaphoreType.DMA((13,))] * 2
+    )
+    return pl.pallas_call(
+        forward_kernel,
+        out_shape=outs,
+        in_specs=[SMEM, SMEM] + [VMEM] * 5 + [ANY] * 8,
+        out_specs=[ANY] * len(outs),
+        scratch_shapes=scratch,
+        compiler_params=pltpu.CompilerParams(
+            collective_id=0, has_side_effects=True, vmem_limit_bytes=VMEM_BYTES
+        ),
+        name="forward",
+    )(table, marks, x, cosine, sine, seg_col, seg_row, *weights)
+
+
+def scan_scratch():
+    return [
+        pltpu.VMEM((H, 2, DH, DH), BF16),
+        pltpu.VMEM((4, 2, 2, DH, DH), BF16),
+        pltpu.VMEM((8, 2, 2, DH, DH), BF16),
+        pltpu.VMEM((4, 2, 2, DH, DH), BF16),
+        pltpu.VMEM((H, 2, DH, DH), BF16),
+    ]
+
+
+def factors(ends, rates, chunk, f, nf, nh, backward):
+    mb = ends.shape[0]
+    places = jnp.arange(nh)
+    groups = jnp.arange(nf)
+    at_group = lax.dynamic_slice_in_dim(ends, f * nh, nh, axis=1)
+    before_group = jnp.where(
+        f > 0, lax.dynamic_index_in_dim(ends, jnp.maximum(f * nh - 1, 0), 1, False), 0
+    )
+    before = jnp.concatenate([before_group[:, None], at_group[:, :-1]], axis=1)
+    last = at_group[:, -1]
+    group_last = ends.reshape(mb, nf, nh)[:, :, -1]
+    group_before = jnp.concatenate([jnp.zeros_like(group_last[:, :1]), group_last[:, :-1]], axis=1)
+
+    def factor(same, gap):
+        gap = jnp.maximum(gap, 0)
+        value = jnp.exp(-rates * (chunk * gap).astype(F32)[..., None])
+        return jnp.where(same[..., None], value, 0.0).reshape(-1)
+
+    rise = jnp.broadcast_to(places, (mb, nh))
+    fall = jnp.broadcast_to(nh - 1 - places, (mb, nh))
+    if backward:
+        to_total = factor(before == before_group[:, None], rise)
+        group_same = (last[:, None] == group_before) & (groups > f)
+        group_gap = jnp.broadcast_to((groups - 1 - f) * nh, (mb, nf))
+        to_place = factor(at_group == last[:, None], fall)
+        same = (at_group[:, :, None] == before[:, None, :]) & (places[None, :] > places[:, None])
+        gap = jnp.broadcast_to(places[None, :] - 1 - places[:, None], (mb, nh, nh))
+    else:
+        to_total = factor(at_group == last[:, None], fall)
+        group_same = (before_group[:, None] == group_last) & (groups < f)
+        group_gap = jnp.broadcast_to((f - 1 - groups) * nh, (mb, nf))
+        to_place = factor(before == before_group[:, None], rise)
+        same = (before[:, :, None] == at_group[:, None, :]) & (places[None, :] < places[:, None])
+        gap = jnp.broadcast_to(places[:, None] - 1 - places[None, :], (mb, nh, nh))
+    return jnp.concatenate([to_total, factor(group_same, group_gap), to_place, factor(same, gap)])
+
+
+def local_fast(tokens, cotangent, lengths, decay_rate, *weights):
+    wires = Wires()
+    mb, chunk, width = tokens.shape
+    rows = mb * chunk
+    nf, nh = wires.nf, wires.nh
+    place = wires.f * nh + wires.h
+    positions = place * chunk + jnp.arange(chunk, dtype=jnp.int32)
+    cosine, sine_vals = rotation_tables(positions, DH)
+    cosine, sine_vals = cosine[:, 0], sine_vals[:, 0]
+    cos_table = jnp.tile(cosine, (mb, 2))
+    sin_table = jnp.tile(jnp.concatenate([-sine_vals, sine_vals], axis=1), (mb, 1))
+    seq_ends = jnp.cumsum(lengths, axis=1)
+    segs = jnp.sum((seq_ends[:, None, :] <= positions[None, :, None]).astype(jnp.int32), axis=2)
+    chunk_ends = (jnp.arange(nf * nh, dtype=jnp.int32) + 1) * chunk - 1
+    ends = jnp.sum((seq_ends[:, None, :] <= chunk_ends[None, :, None]).astype(jnp.int32), axis=2)
+    last = lax.dynamic_index_in_dim(ends, place, 1, False)
+    before = jnp.where(
+        place > 0, lax.dynamic_index_in_dim(ends, jnp.maximum(place - 1, 0), 1, False), 0
+    )
+    marks = jnp.concatenate([before, last])
+    mine = H // nh
+    rates = lax.dynamic_slice_in_dim(decay_rate, wires.h * mine, mine)
+    table = jnp.concatenate([decay_rate, factors(ends, rates, chunk, wires.f, nf, nh, False)])
+    x = tokens.reshape(rows, width)
+    seg_col = segs.reshape(rows, 1)
+    outs = run_forward(table, marks, x, cos_table, sin_table, seg_col, segs, weights)
+    (mix_weights, out_full, first_full, second_full, down_full) = outs[:5]
+    (q, k, v, u, query_pre, key_pre, attended, hidden, p1, p2, product, state_in, mixed) = outs[5:]
+
+    within, entering, leaving = masks(segs, before, last, decay_rate)
+    cosine = jnp.tile(cosine[:, None], (mb, 1, 1))
+    sine_vals = jnp.tile(sine_vals[:, None], (mb, 1, 1))
+
+    def heads(values):
+        return values.reshape(mb, chunk, H, DH).transpose(0, 2, 1, 3)
+
+    def flat(values):
+        return values.transpose(0, 2, 1, 3).reshape(rows, H * DH)
+
+    def mm(spec, a, b):
+        return jnp.einsum(spec, a.astype(BF16), b.astype(BF16), preferred_element_type=F32)
+
+    query_h, key_h, value_h = heads(q), heads(k), heads(v)
+    state_in = state_in.transpose(1, 0, 2, 3)
+    gate_vals = u.astype(F32)
+    query_pre, key_pre = query_pre.astype(F32), key_pre.astype(F32)
+    first_pre, second_pre = p1.astype(F32), p2.astype(F32)
+    normed_in, scale_in = norm_parts(x.astype(F32))
+    act_rel = wires.rel(normed_in.astype(BF16))
+    normed_att, scale_att = norm_parts(attended.astype(F32))
+    gated_rel = wires.rel((normed_att * gate_vals).astype(BF16))
+    normed_mid, scale_mid = norm_parts(hidden)
+    mid_rel = wires.rel(normed_mid.astype(BF16))
+    scores = (mm("mhsd,mhtd->mhst", query_h, key_h) * within).astype(BF16)
+
+    grad_low = cotangent.reshape(rows, width)
+    share_down = wires.reduce(dot_rows(wires.rel(grad_low), product)).T
+    grad_prod = dot_cols(grad_low, down_full)
+    grad_p1 = (grad_prod * second_pre).astype(BF16)
+    grad_p2 = (grad_prod * first_pre).astype(BF16)
+    share_first = wires.reduce(dot_rows(mid_rel, grad_p1))
+    share_second = wires.reduce(dot_rows(mid_rel, grad_p2))
+    grad_mid = dot_cols(grad_p1, first_full) + dot_cols(grad_p2, second_full)
+    grad_hidden = grad_low.astype(F32) + norm_back(grad_mid, normed_mid, scale_mid)
+    grad_hidden_low = grad_hidden.astype(BF16)
+    share_out = wires.reduce(dot_rows(gated_rel, grad_hidden_low))
+    grad_gated = dot_cols(grad_hidden_low, out_full)
+    grad_gate_low = (grad_gated * normed_att).astype(BF16)
+    grad_att = heads(norm_back(grad_gated * gate_vals, normed_att, scale_att).astype(BF16))
+    grad_state = mm("mhsd,mhse->mhde", query_h * entering, grad_att)
+    grad_end = chain(wires, grad_state, ends, decay_rate, chunk, True)
+    grad_scores = (mm("mhse,mhte->mhst", grad_att, value_h) * within).astype(BF16)
+    grad_q = mm("mhst,mhtd->mhsd", grad_scores, key_h)
+    grad_q = grad_q + entering * mm("mhse,mhde->mhsd", grad_att, state_in)
+    grad_k = mm("mhst,mhsd->mhtd", grad_scores, query_h)
+    grad_k = grad_k + leaving * mm("mhte,mhde->mhtd", value_h, grad_end)
+    grad_v = mm("mhst,mhse->mhte", scores, grad_att)
+    grad_v = grad_v + leaving * mm("mhtd,mhde->mhte", key_h, grad_end)
+
+    def turned_back(values, pre_values):
+        back = flat(values.astype(BF16)).astype(F32).reshape(rows, H, DH)
+        back = rotate_pairs(back, cosine, -sine_vals).reshape(rows, width)
+        return (silu_slope(pre_values) * back).astype(BF16)
+
+    grad_mix = jnp.concatenate(
+        [
+            turned_back(grad_q, query_pre),
+            turned_back(grad_k, key_pre),
+            flat(grad_v.astype(BF16)),
+            grad_gate_low,
+        ],
+        axis=1,
+    )
+    share_mix = wires.reduce(dot_rows(act_rel, grad_mix))
+    grad_act = dot_cols(grad_mix, mix_weights)
+    grad_tokens = (grad_hidden + norm_back(grad_act, normed_in, scale_in)).astype(BF16)
+    return (
+        mixed.reshape(mb, chunk, width),
+        grad_tokens.reshape(mb, chunk, width),
+        share_mix[:, :width],
+        share_mix[:, width : 2 * width],
+        share_mix[:, 2 * width : 3 * width],
+        share_mix[:, 3 * width :],
+        share_out,
+        share_first,
+        share_second,
+        share_down,
+    )
+
+
 def solution(mesh):
     rows = P(None, AXES, None)
     in_specs = (rows, rows, P(), P()) + (P("fsdp", None),) * 7 + (P(None, "fsdp"),)
     out_specs = (rows, rows) + (P(AXES, None),) * 7 + (P(None, AXES),)
+    fast = mesh.shape["fsdp"] == 8 and mesh.shape["head"] == 4
+    local = local_fast if fast else local_any
     return jax.shard_map(local, mesh=mesh, in_specs=in_specs, out_specs=out_specs, check_vma=False)

time: 650 us -> 527 us (0.81)
  Pallas kernels: 0 us -> 139 us
  local copies, waits for them, and re-layouts: 167 us -> 62.5 us
  waiting for transfers between devices: 221 us -> 147 us
  starting transfers between devices: 82.5 us -> 50.2 us
  matrix products: 95 us -> 67.4 us
  other arithmetic: 70.4 us -> 49.7 us
    pallas_call x0 -> x1, Pallas kernels: none -> 139 us  [run_forward(): pl.pallas_call(forward_kernel, out_shape=outs, in_specs=[SMEM, SMEM] + [V...]
    ppermute x88 -> x55, waiting for transfers between devices: 221 us -> 147 us  [swap(): return lax.ppermute(values, AXES, pairs)]
    unnamed x393 -> x228, local copies, waits for them, and re-layouts: 97.2 us -> 28.5 us
    ppermute x88 -> x55, starting transfers between devices: 82.5 us -> 50.2 us  [swap(): return lax.ppermute(values, AXES, pairs)]
    dot_general x4 -> x0, matrix products: 29.5 us -> none  [dot(): return jnp.dot(a, b, preferred_element_type=F32)]
    concatenate x11 -> x3, local copies, waits for them, and re-layouts: 11.9 us -> 0.83 us  [the longest x1 0.65 us: local_fast(): jnp.concatenate([decay_rate, factors(ends, rates, chunk, wires.f, nf, nh,...]
    dot_general x4 -> x5, matrix products: 25.5 us -> 30.3 us  [dot_cols(): lax.dot_general(a, b, (((1,), (1,)), ((), ())), preferred_element_type=F32)]
    slice x4 -> x5, local copies, waits for them, and re-layouts: 13.8 us -> 10.1 us  [reduce(): low[:, :, 0].astype(F32) + self.swap(low[:, :, 1], core).astype(F32)]
  transfers between devices with their start and end apart: 88 -> 55, of which waited for: 41 -> 39; matrix products, arithmetic and copies ran while one was open for 36% -> 24% of each run, Pallas kernels for 0% -> 0%
where the time goes in v2:
time: 527 us; the launch traced here: 519 us
  waiting for transfers between devices  147 us (28%)
  Pallas kernels  139 us (26%)
  matrix products  67.4 us (13%)
  local copies, waits for them, and re-layouts  62.5 us (12%)
  starting transfers between devices  50.2 us (10%)
  other arithmetic  49.7 us (9%)
    ppermute x55, waiting for transfers between devices, swap(): return lax.ppermute(values, AXES, pairs)  147 us
    pallas_call x1, Pallas kernels, run_forward(): pl.pallas_call(forward_kernel, out_shape=outs, in_specs=[SMEM, SMEM] + [V...  139 us
    ppermute x55, starting transfers between devices, swap(): return lax.ppermute(values, AXES, pairs)  50.2 us
    dot_general x5, matrix products, dot_cols(): lax.dot_general(a, b, (((1,), (1,)), ((), ())), preferred_element_type=F32)  30.3 us
    unnamed x228, local copies, waits for them, and re-layouts  28.5 us
    dot_general x5, matrix products, dot_rows(): lax.dot_general(a, b, (((0,), (0,)), ((), ())), preferred_element_type=F32)  20.1 us
    dot_general x8, matrix products, mm(): jnp.einsum(spec, a.astype(BF16), b.astype(BF16), preferred_element_type=F32)  17 us
    convert_element_type x5, other arithmetic, reduce(): (low[:, :, 0].astype(F32) + self.swap(low[:, :, 1], core).astype(F32)).as...  11.1 us
  transfers between devices with their start and end apart: 55, of which 39 were waited for; matrix products, arithmetic and copies ran while one was open for 24% of the time, Pallas kernels for 0%

profile of v2, /device:TPU:0, one launch (start us, length us, event | category | flops | bytes accessed | tf_op | source)
XLA Modules:
  0.0 519.3 jit_solution(8519535877243616430)
XLA Ops:
  11.7 138.8 %forward.1 = (bf16[1024,4096]{1,0:T(8,128)(2,1)}, bf16[1024,1024]{1,0:T(8,128)(2,1)}, bf16[1024,2816]{1,0:T(8,128)(2,1)}, bf16[1024,2816]{1,0:T(8,128)(2,1)}, bf...) custom-call(f32[136]{0:T(256)} %concatenate.58.table, ...), custom_call_target="tpu_custom_call" | custom-call | tf_op jit(solution)/shard_map/forward/pallas_call | solution.py:815
  150.5 2.0 multiply_reduce_fusion.3
  152.5 8.6 %fusion.152 = f32[2816,512]{0,1:T(8,128)} fusion(bf16[2816,1024]{1,0:T(8,128)(2,1)} %get-tuple-element.31, bf16[512,1024]{1,0:T(8,128)(2,1)S(1)} %bitcast.595), kind=kOutput, calls=%fused_computation.473 | convolution fusion | flops 2952790016 | bytes 12582912 | tf_op jit(solution)/shard_map/dot_general | solution.py:70
  161.2 6.0 %fusion.140 = f32[512,1024]{1,0:T(8,128)S(1)} fusion(bf16[1024,2816]{1,0:T(8,128)(2,1)S(1)} %bitcast.653, f32[2816,512]{0,1:T(8,128)} %fusion.152, bf16[512,2816]{1,0:T(8,128)(2,1)S(1)} %copy-done.83), kind=kOutput, calls=%fused_computation.464 | convolution fusion | flops 2957115392 | bytes 16515072 | tf_op jit(solution)/shard_map/dot_general | solution.py:70
  167.2 6.1 %multiply_reduce_fusion.2 = (f32[512]{0:T(512)S(1)}, f32[512,1024]{1,0:T(8,128)S(1)}) fusion(f32[512,1024]{1,0:T(8,128)S(1)} %copy-done.11, f32[512]{0:T(512)S(1)} %add_rsqrt_fusion.1, f32[512,1024]{1,0:T(8,128)S(1)} %fusion.140, bf16[1024,2816]{1,0:T(8,128)(2,1)S(1)} %bitcast.651, f32[2816,512]{0,1:T(8,128)} %fusion.152, bf16[512,2816]{1,0:T(8,128)(2,1)S(1)} %copy-done.81), kind=kOutput, calls=%fused_computation.93 | convolution fusion | flops 2959212032 | bytes 20713472 | tf_op jit(solution)/shard_map/dot_general | solution.py:70
  178.8 1.8 fusion.51
  181.9 2.9 convolution_convert_fusion.5
  187.6 2.4 collective-permute-start
  195.5 3.5 convolution_convert_fusion.3
  199.1 2.0 fusion.148
  201.0 1.8 copy.347
  206.2 1.7 multiply_exponential_fusion
  209.7 5.0 fusion.42
  214.7 3.1 fusion.6
  219.0 2.1 fusion.57
  221.9 6.2 %convolution_convert_fusion.2 = bf16[1024,2816]{1,0:T(8,128)(2,1)S(1)} fusion(bf16[512,1024]{1,0:T(8,128)(2,1)S(1)} %copy-done.39, f32[2816,512]{0,1:T(8,128)} %fusion.152, bf16[512,2816]{1,0:T(8,128)(2,1)S(1)} %copy-done.82), kind=kOutput, calls=%fused_computation.19 | convolution fusion | flops 2959998976 | bytes 15466496 | tf_op jit(solution)/shard_map/dot_general | solution.py:66
  230.9 3.2 fusion.147
  234.5 3.6 convolution_convert_fusion.1
  238.1 2.8 fusion.146
  240.9 1.7 fusion.43
  252.3 4.2 copy.202
  256.5 3.8 copy.346
  260.3 1.8 copy.345
  264.8 1.7 constant_dynamic-update-slice_fusion.2
  266.5 9.8 %collective-permute-done.5 = bf16[2,2,2,128,128]{4,3,2,1,0:T(8,128)(2,1)S(1)} collective-permute-done((bf16[2,2,2,128,128]{4,3,2,1,0:T(8,128)(2,1)}, bf16[2,2,2,128,128]{4,3,2,1,0:T(8,128)(2,1)S(1)}, u32[]{:S(2)}, u32[]{:S(2)}) %collective-permute-start.5) | collective-permute-done | bytes 262176 | tf_op jit(solution)/shard_map/ppermute | solution.py:86
  277.7 3.0 gather_fusion
  285.2 2.9 collective-permute-start.7
  288.1 3.8 collective-permute-done.9
  291.9 4.7 collective-permute-done.8
  297.4 2.6 gather_fusion.2
  313.1 8.0 %multiply_reduce_fusion = (f32[512]{0:T(512)S(1)}, f32[512,1024]{1,0:T(8,128)S(1)}) fusion(f32[512]{0:T(512)S(1)} %bitcast.645, bf16[2,256,1024]{2,1,0:T(8,128)(2,1)S(1)} %copy-done.6, bf16[1024,4096]{1,0:T(8,128)(2,1)} %get-tuple-element.45, bf16[512,1024]{1,0:T(8,128)(2,1)S(1)} %copy-done.22, bf16[512,1024]{1,0:T(8,128)(2,1)S(1)} %bitcast.630, ...), kind=kOutput, calls=%fused_computation.82 | convolution fusion | flops 4313841152 | bytes 15732736 | tf_op jit(solution)/shard_map/dot_general | solution.py:70
  323.9 5.4 %convolution_convert_fusion = bf16[1024,4096]{1,0:T(8,128)(2,1)S(1)} fusion(bf16[512,1024]{1,0:T(8,128)(2,1)S(1)} %dynamic-slice_dynamic-update-slice_fusion.24, bf16[512,1024]{1,0:T(8,128)(2,1)S(1)} %copy-done.22, bf16[512,1024]{1,0:T(8,128)(2,1)S(1)} %bitcast.631, bf16[512,1024]{1,0:T(8,128)(2,1)S(1)} %fusion.31, bf16[512,1024]{1,0:T(8,128)(2,1)S(1)} %copy-done.30), kind=kOutput, calls=%fused_computation.5 | convolution fusion | flops 4315938816 | bytes 13631488 | tf_op jit(solution)/shard_map/dot_general | solution.py:66
  334.6 5.2 collective-permute-done.20
  341.8 4.2 collective-permute-done.25
  346.8 4.1 collective-permute-done.21
  351.0 4.6 collective-permute-done.26
  355.6 4.6 collective-permute-done.22
  360.2 4.8 collective-permute-done.27
  365.0 4.8 collective-permute-done.23
  370.5 2.6 fusion.3
  375.3 2.6 fusion.2
  380.2 2.6 fusion.1
  382.9 9.4 %collective-permute-done.29 = bf16[2,128,1408]{2,1,0:T(8,128)(2,1)S(1)} collective-permute-done((bf16[2,128,1408]{2,1,0:T(8,128)(2,1)S(1)}, bf16[2,128,1408]{2,1,0:T(8,128)(2,1)S(1)}, u32[]{:S(2)}, u32[]{:S(2)}) %collective-permute-start.29) | collective-permute-done | bytes 720928 | tf_op jit(solution)/shard_map/ppermute | solution.py:86
  394.8 12.9 %collective-permute-done.38 = bf16[2,128,1408]{2,1,0:T(8,128)(2,1)S(1)} collective-permute-done((bf16[2,128,1408]{2,1,0:T(8,128)(2,1)S(1)}, bf16[2,128,1408]{2,1,0:T(8,128)(2,1)S(1)}, u32[]{:S(2)}, u32[]{:S(2)}) %collective-permute-start.38) | collective-permute-done | bytes 720928 | tf_op jit(solution)/shard_map/ppermute | solution.py:86
  410.2 12.9 %collective-permute-done.47 = bf16[2,128,1408]{2,1,0:T(8,128)(2,1)S(1)} collective-permute-done((bf16[2,128,1408]{2,1,0:T(8,128)(2,1)S(1)}, bf16[2,128,1408]{2,1,0:T(8,128)(2,1)S(1)}, u32[]{:S(2)}, u32[]{:S(2)}) %collective-permute-start.47) | collective-permute-done | bytes 720928 | tf_op jit(solution)/shard_map/ppermute | solution.py:86
  425.7 5.2 %collective-permute-done.34 = bf16[128,1408]{1,0:T(8,128)(2,1)S(1)} collective-permute-done((bf16[128,1408]{1,0:T(8,128)(2,1)S(1)}, bf16[128,1408]{1,0:T(8,128)(2,1)S(1)}, u32[]{:S(2)}, u32[]{:S(2)}) %collective-permute-start.34) | collective-permute-done | bytes 360480 | tf_op jit(solution)/shard_map/ppermute | solution.py:86
  433.2 1.7 collective-permute-done.43
  441.1 3.2 collective-permute-done.35
  444.3 4.0 collective-permute-done.31
  448.4 1.9 collective-permute-done.44
  450.7 3.3 collective-permute-done.40
  454.3 3.6 collective-permute-done.53
  458.0 2.5 collective-permute-done.49
  461.1 2.5 collective-permute-start.54
  464.3 1.7 collective-permute-done.41
  466.9 1.8 fusion
  472.7 16.7 %collective-permute-done.15 = bf16[2,128,2048]{2,1,0:T(8,128)(2,1)S(1)} collective-permute-done((bf16[2,128,2048]{2,1,0:T(8,128)(2,1)S(1)}, bf16[2,128,2048]{2,1,0:T(8,128)(2,1)S(1)}, u32[]{:S(2)}, u32[]{:S(2)}) %collective-permute-start.15) | collective-permute-done | bytes 1048608 | tf_op jit(solution)/shard_map/ppermute | solution.py:86
  494.1 6.2 %collective-permute-done.12 = bf16[128,2048]{1,0:T(8,128)(2,1)S(1)} collective-permute-done((bf16[128,2048]{1,0:T(8,128)(2,1)S(1)}, bf16[128,2048]{1,0:T(8,128)(2,1)S(1)}, u32[]{:S(2)}, u32[]{:S(2)}) %collective-permute-start.12) | collective-permute-done | bytes 524320 | tf_op jit(solution)/shard_map/ppermute | solution.py:86
  502.6 1.8 collective-permute-start.17
  504.3 2.6 collective-permute-done.13
  507.0 2.5 collective-permute-start.14
  509.8 2.5 collective-permute-start.18
  512.3 2.0 collective-permute-done.14
  515.1 2.1 collective-permute-done.18
  (503 shorter events, 116.6 us)
Async XLA Ops:
  1.3 180.5 %copy-start.44 = (f32[256]{0:T(256)}, f32[256]{0:T(256)S(1)}, u32[]{:S(2)}) copy-start(f32[256]{0:T(256)S(1)} %get-tuple-element.167) | copy-start | bytes 3076
  3.6 202.6 %copy-start.49 = (f32[8]{0:T(128)}, f32[8]{0:T(128)S(1)}, u32[]{:S(2)}) copy-start(f32[8]{0:T(128)S(1)} %neg.40) | copy-start | bytes 100
  9.5 172.5 %copy-start.42 = (pred[2,256]{1,0:T(4,128)(4,1)}, pred[2,256]{1,0:T(4,128)(4,1)S(1)}, u32[]{:S(2)}) copy-start(pred[2,256]{1,0:T(4,128)(4,1)S(1)} %get-tuple-element.135) | copy-start | bytes 1540
  150.5 10.6 %slice-start.2 = ((s8[5767168]{0:T(1024)(128)(4,1)}), s8[4194304]{0:T(1024)(128)(4,1)S(1)}, s32[]{:S(2)}) async-start(s8[5767168]{0:T(1024)(128)(4,1)} %bitcast.652), calls=%async_computation.2 | async-start | bytes 8388608
  150.5 16.7 %slice-start = ((s8[5767168]{0:T(1024)(128)(4,1)}), s8[4194304]{0:T(1024)(128)(4,1)S(1)}, s32[]{:S(2)}) async-start(s8[5767168]{0:T(1024)(128)(4,1)} %bitcast.650), calls=%async_computation | async-start | bytes 8388608
  152.5 14.7 %slice-start.1 = ((s8[5767168]{0:T(1024)(128)(4,1)}), s8[1572864]{0:T(1024)(128)(4,1)S(1)}, s32[]{:S(2)}) async-start(s8[5767168]{0:T(1024)(128)(4,1)} %bitcast.650), calls=%async_computation.1 | async-start | bytes 3145728
  185.6 57.7 %collective-permute-start.2 = (bf16[2,2,128,128]{3,2,1,0:T(8,128)(2,1)}, bf16[2,2,128,128]{3,2,1,0:T(8,128)(2,1)}, u32[]{:S(2)}, u32[]{:S(2)}) collective-permute-start(bf16[2,2,128,128]{3,2,1,0:T(8,128)(2,1)} %get-tuple-element.97), channel_id=1, source_target_pairs={{0,3},{1,2},{2,1},{3,0},{4,7},{5,6},{6,5},{7,4},{8,11},{9,10},{10,... | collective-permute-start | bytes 393224 | tf_op jit(solution)/shard_map/ppermute | solution.py:86
  187.1 56.2 %collective-permute-start.1 = (bf16[2,2,128,128]{3,2,1,0:T(8,128)(2,1)}, bf16[2,2,128,128]{3,2,1,0:T(8,128)(2,1)}, u32[]{:S(2)}, u32[]{:S(2)}) collective-permute-start(bf16[2,2,128,128]{3,2,1,0:T(8,128)(2,1)} %get-tuple-element.98), channel_id=1, source_target_pairs={{0,2},{1,3},{2,0},{3,1},{4,6},{5,7},{6,4},{7,5},{8,10},{9,11},{10,... | collective-permute-start | bytes 393224 | tf_op jit(solution)/shard_map/ppermute | solution.py:86
  187.6 55.7 %collective-permute-start = (bf16[2,2,128,128]{3,2,1,0:T(8,128)(2,1)}, bf16[2,2,128,128]{3,2,1,0:T(8,128)(2,1)}, u32[]{:S(2)}, u32[]{:S(2)}) collective-permute-start(bf16[2,2,128,128]{3,2,1,0:T(8,128)(2,1)} %get-tuple-element.99), channel_id=1, source_target_pairs={{0,1},{1,0},{2,3},{3,2},{4,5},{5,4},{6,7},{7,6},{8,9},{9,8},{10,11... | collective-permute-start | bytes 393224 | tf_op jit(solution)/shard_map/ppermute | solution.py:86
  194.0 135.3 %collective-permute-start.19 = (bf16[2,2,128,1024]{3,2,0,1:T(8,128)(2,1)}, bf16[2,2,128,1024]{3,2,0,1:T(8,128)(2,1)}, u32[]{:S(2)}, u32[]{:S(2)}) collective-permute-start(bf16[2,2,128,1024]{3,2,0,1:T(8,128)(2,1)} %bitcast.567), channel_id=1, source_target_pairs={{0,4},{1,5},{2,6},{3,7},{4,0},{5,1},{6,2},{7,3},{8,12},{9,13},{10,... | collective-permute-start | bytes 3145736 | tf_op jit(solution)/shard_map/ppermute | solution.py:86
  202.8 167.7 %collective-permute-start.28 = (bf16[2,2,128,2816]{3,2,0,1:T(8,128)(2,1)}, bf16[2,2,128,2816]{3,2,0,1:T(8,128)(2,1)}, u32[]{:S(2)}, u32[]{:S(2)}) collective-permute-start(bf16[2,2,128,2816]{3,2,0,1:T(8,128)(2,1)} %bitcast.565), channel_id=1, source_target_pairs={{0,4},{1,5},{2,6},{3,7},{4,0},{5,1},{6,2},{7,3},{8,12},{9,13},{10,... | collective-permute-start | bytes 8650760 | tf_op jit(solution)/shard_map/ppermute | solution.py:86
  228.8 15.6 %copy-start.48 = (s32[1024]{0:T(1024)}, s32[1024]{0:T(1024)S(1)}, u32[]{:S(2)}) copy-start(s32[1024]{0:T(1024)S(1)} %pad_clamp_fusion.1) | copy-start | bytes 12292
  247.2 1.4 collective-permute-start.3
  249.3 15.5 %collective-permute-start.4 = (bf16[2,2,2,128,128]{4,3,2,1,0:T(8,128)(2,1)}, bf16[2,2,2,128,128]{4,3,2,1,0:T(8,128)(2,1)}, u32[]{:S(2)}, u32[]{:S(2)}) collective-permute-start(bf16[2,2,2,128,128]{4,3,2,1,0:T(8,128)(2,1)} %pad_maximum_fusion.10), channel_id=1, source_target_pairs={{0,8},{1,9},{2,10},{3,11},{4,12},{5,13},{6,14},{7,15},{8,0},{9,1},... | collective-permute-start | bytes 786440 | tf_op jit(solution)/shard_map/ppermute | solution.py:86
  262.2 14.1 %collective-permute-start.5 = (bf16[2,2,2,128,128]{4,3,2,1,0:T(8,128)(2,1)}, bf16[2,2,2,128,128]{4,3,2,1,0:T(8,128)(2,1)S(1)}, u32[]{:S(2)}, u32[]{:S(2)}) collective-permute-start(bf16[2,2,2,128,128]{4,3,2,1,0:T(8,128)(2,1)} %pad_maximum_fusion.10), channel_id=1, source_target_pairs={{0,16},{1,17},{2,18},{3,19},{4,20},{5,21},{6,22},{7,23},{8,24},{9,... | collective-permute-start | bytes 786440 | tf_op jit(solution)/shard_map/ppermute | solution.py:86
  262.7 14.3 %collective-permute-start.6 = (bf16[2,2,2,128,128]{4,3,2,1,0:T(8,128)(2,1)}, bf16[2,2,2,128,128]{4,3,2,1,0:T(8,128)(2,1)S(1)}, u32[]{:S(2)}, u32[]{:S(2)}) collective-permute-start(bf16[2,2,2,128,128]{4,3,2,1,0:T(8,128)(2,1)} %pad_maximum_fusion.10), channel_id=1, source_target_pairs={{0,24},{1,25},{2,26},{3,27},{4,28},{5,29},{6,30},{7,31},{8,16},{9,... | collective-permute-start | bytes 786440 | tf_op jit(solution)/shard_map/ppermute | solution.py:86
  283.6 8.3 %collective-permute-start.9 = (bf16[2,2,128,128]{3,2,1,0:T(8,128)(2,1)S(1)}, bf16[2,2,128,128]{3,2,1,0:T(8,128)(2,1)S(1)}, u32[]{:S(2)}, u32[]{:S(2)}) collective-permute-start(bf16[2,2,128,128]{3,2,1,0:T(8,128)(2,1)S(1)} %get-tuple-element.93), channel_id=1, source_target_pairs={{0,3},{1,2},{2,1},{3,0},{4,7},{5,6},{6,5},{7,4},{8,11},{9,10},{10,... | collective-permute-start | bytes 393224 | tf_op jit(solution)/shard_map/ppermute | solution.py:86
  285.1 11.5 %collective-permute-start.8 = (bf16[2,2,128,128]{3,2,1,0:T(8,128)(2,1)S(1)}, bf16[2,2,128,128]{3,2,1,0:T(8,128)(2,1)S(1)}, u32[]{:S(2)}, u32[]{:S(2)}) collective-permute-start(bf16[2,2,128,128]{3,2,1,0:T(8,128)(2,1)S(1)} %get-tuple-element.94), channel_id=1, source_target_pairs={{0,2},{1,3},{2,0},{3,1},{4,6},{5,7},{6,4},{7,5},{8,10},{9,11},{10,... | collective-permute-start | bytes 393224 | tf_op jit(solution)/shard_map/ppermute | solution.py:86
  285.2 11.4 %collective-permute-start.7 = (bf16[2,2,128,128]{3,2,1,0:T(8,128)(2,1)S(1)}, bf16[2,2,128,128]{3,2,1,0:T(8,128)(2,1)S(1)}, u32[]{:S(2)}, u32[]{:S(2)}) collective-permute-start(bf16[2,2,128,128]{3,2,1,0:T(8,128)(2,1)S(1)} %get-tuple-element.95), channel_id=1, source_target_pairs={{0,1},{1,0},{2,3},{3,2},{4,5},{5,4},{6,7},{7,6},{8,9},{9,8},{10,11... | collective-permute-start | bytes 393224 | tf_op jit(solution)/shard_map/ppermute | solution.py:86
  291.9 83.4 %collective-permute-start.37 = (bf16[2,2,128,2816]{3,2,0,1:T(8,128)(2,1)}, bf16[2,2,128,2816]{3,2,0,1:T(8,128)(2,1)}, u32[]{:S(2)}, u32[]{:S(2)}) collective-permute-start(bf16[2,2,128,2816]{3,2,0,1:T(8,128)(2,1)} %bitcast.564), channel_id=1, source_target_pairs={{0,4},{1,5},{2,6},{3,7},{4,0},{5,1},{6,2},{7,3},{8,12},{9,13},{10,... | collective-permute-start | bytes 8650760 | tf_op jit(solution)/shard_map/ppermute | solution.py:86
  296.6 82.6 %collective-permute-start.46 = (bf16[2,2,128,2816]{3,2,0,1:T(8,128)(2,1)}, bf16[2,2,128,2816]{3,2,0,1:T(8,128)(2,1)}, u32[]{:S(2)}, u32[]{:S(2)}) collective-permute-start(bf16[2,2,128,2816]{3,2,0,1:T(8,128)(2,1)} %bitcast.563), channel_id=1, source_target_pairs={{0,4},{1,5},{2,6},{3,7},{4,0},{5,1},{6,2},{7,3},{8,12},{9,13},{10,... | collective-permute-start | bytes 8650760 | tf_op jit(solution)/shard_map/ppermute | solution.py:86
  331.0 8.8 %collective-permute-start.20 = (bf16[2,128,512]{2,1,0:T(8,128)(2,1)S(1)}, bf16[2,128,512]{2,1,0:T(8,128)(2,1)S(1)}, u32[]{:S(2)}, u32[]{:S(2)}) collective-permute-start(bf16[2,128,512]{2,1,0:T(8,128)(2,1)S(1)} %slice_bitcast_fusion.34), channel_id=1, source_target_pairs={{0,8},{1,9},{2,10},{3,11},{4,12},{5,13},{6,14},{7,15},{8,0},{9,1},... | collective-permute-start | bytes 786440 | tf_op jit(solution)/shard_map/ppermute | solution.py:86
  331.7 8.4 %collective-permute-start.24 = (bf16[2,128,512]{2,1,0:T(8,128)(2,1)S(1)}, bf16[2,128,512]{2,1,0:T(8,128)(2,1)S(1)}, u32[]{:S(2)}, u32[]{:S(2)}) collective-permute-start(bf16[2,128,512]{2,1,0:T(8,128)(2,1)S(1)} %slice_bitcast_fusion.32), channel_id=1, source_target_pairs={{0,16},{1,17},{2,18},{3,19},{4,20},{5,21},{6,22},{7,23},{8,24},{9,... | collective-permute-start | bytes 786440 | tf_op jit(solution)/shard_map/ppermute | solution.py:86
  339.8 30.7 %copy-start.1 = (bf16[2,2,1,128,2816]{4,3,2,1,0:T(8,128)(2,1)S(1)}, bf16[2,2,1,128,2816]{4,3,2,1,0:T(8,128)(2,1)}, u32[]{:S(2)}) copy-start(bf16[2,2,1,128,2816]{4,3,2,1,0:T(8,128)(2,1)} %get-tuple-element.63) | copy-start | bytes 8650756
  339.8 127.1 %collective-permute-start.10 = (bf16[2,2,128,4096]{3,2,0,1:T(8,128)(2,1)S(1)}, bf16[2,2,128,4096]{3,2,0,1:T(8,128)(2,1)S(1)}, u32[]{:S(2)}, u32[]{:S(2)}) collective-permute-start(bf16[2,2,128,4096]{3,2,0,1:T(8,128)(2,1)S(1)} %bitcast.587), channel_id=1, source_target_pairs={{0,4},{1,5},{2,6},{3,7},{4,0},{5,1},{6,2},{7,3},{8,12},{9,13},{10,... | collective-permute-start | bytes 12582920 | tf_op jit(solution)/shard_map/ppermute | solution.py:86
  340.2 5.7 %collective-permute-start.25 = (bf16[128,512]{1,0:T(8,128)(2,1)S(1)}, bf16[128,512]{1,0:T(8,128)(2,1)S(1)}, u32[]{:S(2)}, u32[]{:S(2)}) collective-permute-start(bf16[128,512]{1,0:T(8,128)(2,1)S(1)} %slice_bitcast_fusion.36), channel_id=1, source_target_pairs={{0,8},{1,9},{2,10},{3,11},{4,12},{5,13},{6,14},{7,15},{8,0},{9,1},... | collective-permute-start | bytes 393224 | tf_op jit(solution)/shard_map/ppermute | solution.py:86
  345.9 5.0 collective-permute-start.21
  350.9 4.6 collective-permute-start.26
  355.5 4.6 collective-permute-start.22
  360.2 4.8 collective-permute-start.27
  365.0 4.8 collective-permute-start.23
  373.1 19.1 %collective-permute-start.29 = (bf16[2,128,1408]{2,1,0:T(8,128)(2,1)S(1)}, bf16[2,128,1408]{2,1,0:T(8,128)(2,1)S(1)}, u32[]{:S(2)}, u32[]{:S(2)}) collective-permute-start(bf16[2,128,1408]{2,1,0:T(8,128)(2,1)S(1)} %slice_bitcast_fusion.14), channel_id=1, source_target_pairs={{0,8},{1,9},{2,10},{3,11},{4,12},{5,13},{6,14},{7,15},{8,0},{9,1},... | collective-permute-start | bytes 2162696 | tf_op jit(solution)/shard_map/ppermute | solution.py:86
  374.3 19.1 %collective-permute-start.33 = (bf16[2,128,1408]{2,1,0:T(8,128)(2,1)S(1)}, bf16[2,128,1408]{2,1,0:T(8,128)(2,1)S(1)}, u32[]{:S(2)}, u32[]{:S(2)}) collective-permute-start(bf16[2,128,1408]{2,1,0:T(8,128)(2,1)S(1)} %slice_bitcast_fusion.12), channel_id=1, source_target_pairs={{0,16},{1,17},{2,18},{3,19},{4,20},{5,21},{6,22},{7,23},{8,24},{9,... | collective-permute-start | bytes 2162696 | tf_op jit(solution)/shard_map/ppermute | solution.py:86
  377.9 29.8 %collective-permute-start.38 = (bf16[2,128,1408]{2,1,0:T(8,128)(2,1)S(1)}, bf16[2,128,1408]{2,1,0:T(8,128)(2,1)S(1)}, u32[]{:S(2)}, u32[]{:S(2)}) collective-permute-start(bf16[2,128,1408]{2,1,0:T(8,128)(2,1)S(1)} %slice_bitcast_fusion.10), channel_id=1, source_target_pairs={{0,8},{1,9},{2,10},{3,11},{4,12},{5,13},{6,14},{7,15},{8,0},{9,1},... | collective-permute-start | bytes 2162696 | tf_op jit(solution)/shard_map/ppermute | solution.py:86
  379.1 29.7 %collective-permute-start.42 = (bf16[2,128,1408]{2,1,0:T(8,128)(2,1)S(1)}, bf16[2,128,1408]{2,1,0:T(8,128)(2,1)S(1)}, u32[]{:S(2)}, u32[]{:S(2)}) collective-permute-start(bf16[2,128,1408]{2,1,0:T(8,128)(2,1)S(1)} %slice_bitcast_fusion.8), channel_id=1, source_target_pairs={{0,16},{1,17},{2,18},{3,19},{4,20},{5,21},{6,22},{7,23},{8,24},{9,... | collective-permute-start | bytes 2162696 | tf_op jit(solution)/shard_map/ppermute | solution.py:86
  392.3 30.9 %collective-permute-start.47 = (bf16[2,128,1408]{2,1,0:T(8,128)(2,1)S(1)}, bf16[2,128,1408]{2,1,0:T(8,128)(2,1)S(1)}, u32[]{:S(2)}, u32[]{:S(2)}) collective-permute-start(bf16[2,128,1408]{2,1,0:T(8,128)(2,1)S(1)} %slice_bitcast_fusion.6), channel_id=1, source_target_pairs={{0,8},{1,9},{2,10},{3,11},{4,12},{5,13},{6,14},{7,15},{8,0},{9,1},... | collective-permute-start | bytes 2162696 | tf_op jit(solution)/shard_map/ppermute | solution.py:86
  393.4 30.9 %collective-permute-start.51 = (bf16[2,128,1408]{2,1,0:T(8,128)(2,1)S(1)}, bf16[2,128,1408]{2,1,0:T(8,128)(2,1)S(1)}, u32[]{:S(2)}, u32[]{:S(2)}) collective-permute-start(bf16[2,128,1408]{2,1,0:T(8,128)(2,1)S(1)} %slice_bitcast_fusion.4), channel_id=1, source_target_pairs={{0,16},{1,17},{2,18},{3,19},{4,20},{5,21},{6,22},{7,23},{8,24},{9,... | collective-permute-start | bytes 2162696 | tf_op jit(solution)/shard_map/ppermute | solution.py:86
  407.7 23.2 %collective-permute-start.34 = (bf16[128,1408]{1,0:T(8,128)(2,1)S(1)}, bf16[128,1408]{1,0:T(8,128)(2,1)S(1)}, u32[]{:S(2)}, u32[]{:S(2)}) collective-permute-start(bf16[128,1408]{1,0:T(8,128)(2,1)S(1)} %slice_bitcast_fusion.28), channel_id=1, source_target_pairs={{0,8},{1,9},{2,10},{3,11},{4,12},{5,13},{6,14},{7,15},{8,0},{9,1},... | collective-permute-start | bytes 1081352 | tf_op jit(solution)/shard_map/ppermute | solution.py:86
  408.9 23.1 %collective-permute-start.30 = (bf16[128,1408]{1,0:T(8,128)(2,1)S(1)}, bf16[128,1408]{1,0:T(8,128)(2,1)S(1)}, u32[]{:S(2)}, u32[]{:S(2)}) collective-permute-start(bf16[128,1408]{1,0:T(8,128)(2,1)S(1)} %slice_bitcast_fusion.30), channel_id=1, source_target_pairs={{0,16},{1,17},{2,18},{3,19},{4,20},{5,21},{6,22},{7,23},{8,24},{9,... | collective-permute-start | bytes 1081352 | tf_op jit(solution)/shard_map/ppermute | solution.py:86
  423.2 11.7 %collective-permute-start.43 = (bf16[128,1408]{1,0:T(8,128)(2,1)S(1)}, bf16[128,1408]{1,0:T(8,128)(2,1)S(1)}, u32[]{:S(2)}, u32[]{:S(2)}) collective-permute-start(bf16[128,1408]{1,0:T(8,128)(2,1)S(1)} %slice_bitcast_fusion.24), channel_id=1, source_target_pairs={{0,8},{1,9},{2,10},{3,11},{4,12},{5,13},{6,14},{7,15},{8,0},{9,1},... | collective-permute-start | bytes 1081352 | tf_op jit(solution)/shard_map/ppermute | solution.py:86
  424.3 11.2 %collective-permute-start.39 = (bf16[128,1408]{1,0:T(8,128)(2,1)S(1)}, bf16[128,1408]{1,0:T(8,128)(2,1)S(1)}, u32[]{:S(2)}, u32[]{:S(2)}) collective-permute-start(bf16[128,1408]{1,0:T(8,128)(2,1)S(1)} %slice_bitcast_fusion.26), channel_id=1, source_target_pairs={{0,16},{1,17},{2,18},{3,19},{4,20},{5,21},{6,22},{7,23},{8,24},{9,... | collective-permute-start | bytes 1081352 | tf_op jit(solution)/shard_map/ppermute | solution.py:86
  430.9 7.8 %collective-permute-start.52 = (bf16[128,1408]{1,0:T(8,128)(2,1)S(1)}, bf16[128,1408]{1,0:T(8,128)(2,1)S(1)}, u32[]{:S(2)}, u32[]{:S(2)}) collective-permute-start(bf16[128,1408]{1,0:T(8,128)(2,1)S(1)} %slice_bitcast_fusion.20), channel_id=1, source_target_pairs={{0,8},{1,9},{2,10},{3,11},{4,12},{5,13},{6,14},{7,15},{8,0},{9,1},... | collective-permute-start | bytes 1081352 | tf_op jit(solution)/shard_map/ppermute | solution.py:86
  431.9 7.5 %collective-permute-start.48 = (bf16[128,1408]{1,0:T(8,128)(2,1)S(1)}, bf16[128,1408]{1,0:T(8,128)(2,1)S(1)}, u32[]{:S(2)}, u32[]{:S(2)}) collective-permute-start(bf16[128,1408]{1,0:T(8,128)(2,1)S(1)} %slice_bitcast_fusion.22), channel_id=1, source_target_pairs={{0,16},{1,17},{2,18},{3,19},{4,20},{5,21},{6,22},{7,23},{8,24},{9,... | collective-permute-start | bytes 1081352 | tf_op jit(solution)/shard_map/ppermute | solution.py:86
  434.9 9.4 %collective-permute-start.35 = (bf16[2,32,1408]{2,1,0:T(8,128)(2,1)S(1)}, bf16[2,32,1408]{2,1,0:T(8,128)(2,1)S(1)}, u32[]{:S(2)}, u32[]{:S(2)}) collective-permute-start(bf16[2,32,1408]{2,1,0:T(8,128)(2,1)S(1)} %dynamic-slice_bitcast_fusion.6), channel_id=1, source_target_pairs={{0,1},{1,0},{2,3},{3,2},{4,5},{5,4},{6,7},{7,6},{8,9},{9,8},{10,11... | collective-permute-start | bytes 540680 | tf_op jit(solution)/shard_map/ppermute | solution.py:86
  435.5 12.8 %collective-permute-start.31 = (bf16[2,32,1408]{2,1,0:T(8,128)(2,1)S(1)}, bf16[2,32,1408]{2,1,0:T(8,128)(2,1)S(1)}, u32[]{:S(2)}, u32[]{:S(2)}) collective-permute-start(bf16[2,32,1408]{2,1,0:T(8,128)(2,1)S(1)} %dynamic-slice_bitcast_fusion.7), channel_id=1, source_target_pairs={{0,1},{1,0},{2,3},{3,2},{4,5},{5,4},{6,7},{7,6},{8,9},{9,8},{10,11... | collective-permute-start | bytes 540680 | tf_op jit(solution)/shard_map/ppermute | solution.py:86
  438.7 11.5 %collective-permute-start.44 = (bf16[2,32,1408]{2,1,0:T(8,128)(2,1)S(1)}, bf16[2,32,1408]{2,1,0:T(8,128)(2,1)S(1)}, u32[]{:S(2)}, u32[]{:S(2)}) collective-permute-start(bf16[2,32,1408]{2,1,0:T(8,128)(2,1)S(1)} %dynamic-slice_bitcast_fusion.4), channel_id=1, source_target_pairs={{0,1},{1,0},{2,3},{3,2},{4,5},{5,4},{6,7},{7,6},{8,9},{9,8},{10,11... | collective-permute-start | bytes 540680 | tf_op jit(solution)/shard_map/ppermute | solution.py:86
  439.4 14.5 %collective-permute-start.40 = (bf16[2,32,1408]{2,1,0:T(8,128)(2,1)S(1)}, bf16[2,32,1408]{2,1,0:T(8,128)(2,1)S(1)}, u32[]{:S(2)}, u32[]{:S(2)}) collective-permute-start(bf16[2,32,1408]{2,1,0:T(8,128)(2,1)S(1)} %dynamic-slice_bitcast_fusion.5), channel_id=1, source_target_pairs={{0,1},{1,0},{2,3},{3,2},{4,5},{5,4},{6,7},{7,6},{8,9},{9,8},{10,11... | collective-permute-start | bytes 540680 | tf_op jit(solution)/shard_map/ppermute | solution.py:86
  444.3 13.7 %collective-permute-start.53 = (bf16[2,32,1408]{2,1,0:T(8,128)(2,1)S(1)}, bf16[2,32,1408]{2,1,0:T(8,128)(2,1)S(1)}, u32[]{:S(2)}, u32[]{:S(2)}) collective-permute-start(bf16[2,32,1408]{2,1,0:T(8,128)(2,1)S(1)} %dynamic-slice_bitcast_fusion.2), channel_id=1, source_target_pairs={{0,1},{1,0},{2,3},{3,2},{4,5},{5,4},{6,7},{7,6},{8,9},{9,8},{10,11... | collective-permute-start | bytes 540680 | tf_op jit(solution)/shard_map/ppermute | solution.py:86
  448.3 12.2 %collective-permute-start.49 = (bf16[2,32,1408]{2,1,0:T(8,128)(2,1)S(1)}, bf16[2,32,1408]{2,1,0:T(8,128)(2,1)S(1)}, u32[]{:S(2)}, u32[]{:S(2)}) collective-permute-start(bf16[2,32,1408]{2,1,0:T(8,128)(2,1)S(1)} %dynamic-slice_bitcast_fusion.3), channel_id=1, source_target_pairs={{0,1},{1,0},{2,3},{3,2},{4,5},{5,4},{6,7},{7,6},{8,9},{9,8},{10,11... | collective-permute-start | bytes 540680 | tf_op jit(solution)/shard_map/ppermute | solution.py:86
  450.2 10.9 %collective-permute-start.36 = (bf16[32,1408]{1,0:T(8,128)(2,1)S(1)}, bf16[32,1408]{1,0:T(8,128)(2,1)S(1)}, u32[]{:S(2)}, u32[]{:S(2)}) collective-permute-start(bf16[32,1408]{1,0:T(8,128)(2,1)S(1)} %dynamic-slice_bitcast_fusion.21), channel_id=1, source_target_pairs={{0,2},{1,3},{2,0},{3,1},{4,6},{5,7},{6,4},{7,5},{8,10},{9,11},{10,... | collective-permute-start | bytes 270344 | tf_op jit(solution)/shard_map/ppermute | solution.py:86
  453.9 9.7 %collective-permute-start.32 = (bf16[32,1408]{1,0:T(8,128)(2,1)S(1)}, bf16[32,1408]{1,0:T(8,128)(2,1)S(1)}, u32[]{:S(2)}, u32[]{:S(2)}) collective-permute-start(bf16[32,1408]{1,0:T(8,128)(2,1)S(1)} %dynamic-slice_bitcast_fusion.22), channel_id=1, source_target_pairs={{0,2},{1,3},{2,0},{3,1},{4,6},{5,7},{6,4},{7,5},{8,10},{9,11},{10,... | collective-permute-start | bytes 270344 | tf_op jit(solution)/shard_map/ppermute | solution.py:86
  457.9 6.3 %collective-permute-start.45 = (bf16[32,1408]{1,0:T(8,128)(2,1)S(1)}, bf16[32,1408]{1,0:T(8,128)(2,1)S(1)}, u32[]{:S(2)}, u32[]{:S(2)}) collective-permute-start(bf16[32,1408]{1,0:T(8,128)(2,1)S(1)} %dynamic-slice_bitcast_fusion.19), channel_id=1, source_target_pairs={{0,2},{1,3},{2,0},{3,1},{4,6},{5,7},{6,4},{7,5},{8,10},{9,11},{10,... | collective-permute-start | bytes 270344 | tf_op jit(solution)/shard_map/ppermute | solution.py:86
  460.5 5.4 %collective-permute-start.41 = (bf16[32,1408]{1,0:T(8,128)(2,1)S(1)}, bf16[32,1408]{1,0:T(8,128)(2,1)S(1)}, u32[]{:S(2)}, u32[]{:S(2)}) collective-permute-start(bf16[32,1408]{1,0:T(8,128)(2,1)S(1)} %dynamic-slice_bitcast_fusion.20), channel_id=1, source_target_pairs={{0,2},{1,3},{2,0},{3,1},{4,6},{5,7},{6,4},{7,5},{8,10},{9,11},{10,... | collective-permute-start | bytes 270344 | tf_op jit(solution)/shard_map/ppermute | solution.py:86
  461.1 5.8 %collective-permute-start.54 = (bf16[32,1408]{1,0:T(8,128)(2,1)S(1)}, bf16[32,1408]{1,0:T(8,128)(2,1)S(1)}, u32[]{:S(2)}, u32[]{:S(2)}) collective-permute-start(bf16[32,1408]{1,0:T(8,128)(2,1)S(1)} %dynamic-slice_bitcast_fusion.17), channel_id=1, source_target_pairs={{0,2},{1,3},{2,0},{3,1},{4,6},{5,7},{6,4},{7,5},{8,10},{9,11},{10,... | collective-permute-start | bytes 270344 | tf_op jit(solution)/shard_map/ppermute | solution.py:86
  463.6 9.0 %collective-permute-start.50 = (bf16[32,1408]{1,0:T(8,128)(2,1)S(1)}, bf16[32,1408]{1,0:T(8,128)(2,1)S(1)}, u32[]{:S(2)}, u32[]{:S(2)}) collective-permute-start(bf16[32,1408]{1,0:T(8,128)(2,1)S(1)} %dynamic-slice_bitcast_fusion.18), channel_id=1, source_target_pairs={{0,2},{1,3},{2,0},{3,1},{4,6},{5,7},{6,4},{7,5},{8,10},{9,11},{10,... | collective-permute-start | bytes 270344 | tf_op jit(solution)/shard_map/ppermute | solution.py:86
  468.9 20.5 %collective-permute-start.15 = (bf16[2,128,2048]{2,1,0:T(8,128)(2,1)S(1)}, bf16[2,128,2048]{2,1,0:T(8,128)(2,1)S(1)}, u32[]{:S(2)}, u32[]{:S(2)}) collective-permute-start(bf16[2,128,2048]{2,1,0:T(8,128)(2,1)S(1)} %slice_bitcast_fusion), channel_id=1, source_target_pairs={{0,16},{1,17},{2,18},{3,19},{4,20},{5,21},{6,22},{7,23},{8,24},{9,... | collective-permute-start | bytes 3145736 | tf_op jit(solution)/shard_map/ppermute | solution.py:86
  469.8 20.4 %collective-permute-start.11 = (bf16[2,128,2048]{2,1,0:T(8,128)(2,1)S(1)}, bf16[2,128,2048]{2,1,0:T(8,128)(2,1)S(1)}, u32[]{:S(2)}, u32[]{:S(2)}) collective-permute-start(bf16[2,128,2048]{2,1,0:T(8,128)(2,1)S(1)} %slice_bitcast_fusion.2), channel_id=1, source_target_pairs={{0,8},{1,9},{2,10},{3,11},{4,12},{5,13},{6,14},{7,15},{8,0},{9,1},... | collective-permute-start | bytes 3145736 | tf_op jit(solution)/shard_map/ppermute | solution.py:86
  491.1 9.2 %collective-permute-start.12 = (bf16[128,2048]{1,0:T(8,128)(2,1)S(1)}, bf16[128,2048]{1,0:T(8,128)(2,1)S(1)}, u32[]{:S(2)}, u32[]{:S(2)}) collective-permute-start(bf16[128,2048]{1,0:T(8,128)(2,1)S(1)} %slice_bitcast_fusion.18), channel_id=1, source_target_pairs={{0,16},{1,17},{2,18},{3,19},{4,20},{5,21},{6,22},{7,23},{8,24},{9,... | collective-permute-start | bytes 1572872 | tf_op jit(solution)/shard_map/ppermute | solution.py:86
  493.1 9.2 %collective-permute-start.16 = (bf16[128,2048]{1,0:T(8,128)(2,1)S(1)}, bf16[128,2048]{1,0:T(8,128)(2,1)S(1)}, u32[]{:S(2)}, u32[]{:S(2)}) collective-permute-start(bf16[128,2048]{1,0:T(8,128)(2,1)S(1)} %slice_bitcast_fusion.16), channel_id=1, source_target_pairs={{0,8},{1,9},{2,10},{3,11},{4,12},{5,13},{6,14},{7,15},{8,0},{9,1},... | collective-permute-start | bytes 1572872 | tf_op jit(solution)/shard_map/ppermute | solution.py:86
  500.5 6.4 %collective-permute-start.13 = (bf16[2,32,2048]{2,1,0:T(8,128)(2,1)S(1)}, bf16[2,32,2048]{2,1,0:T(8,128)(2,1)S(1)}, u32[]{:S(2)}, u32[]{:S(2)}) collective-permute-start(bf16[2,32,2048]{2,1,0:T(8,128)(2,1)S(1)} %dynamic-slice_bitcast_fusion.1), channel_id=1, source_target_pairs={{0,1},{1,0},{2,3},{3,2},{4,5},{5,4},{6,7},{7,6},{8,9},{9,8},{10,11... | collective-permute-start | bytes 786440 | tf_op jit(solution)/shard_map/ppermute | solution.py:86
  502.5 15.4 %copy-start.23 = (bf16[512,1024]{1,0:T(8,128)(2,1)S(1)}, bf16[512,1024]{1,0:T(8,128)(2,1)}, u32[]{:S(2)}) copy-start(bf16[512,1024]{1,0:T(8,128)(2,1)} %get-tuple-element.29) | copy-start | bytes 3145732
  502.6 7.2 %collective-permute-start.17 = (bf16[2,32,2048]{2,1,0:T(8,128)(2,1)S(1)}, bf16[2,32,2048]{2,1,0:T(8,128)(2,1)S(1)}, u32[]{:S(2)}, u32[]{:S(2)}) collective-permute-start(bf16[2,32,2048]{2,1,0:T(8,128)(2,1)S(1)} %dynamic-slice_bitcast_fusion), channel_id=1, source_target_pairs={{0,1},{1,0},{2,3},{3,2},{4,5},{5,4},{6,7},{7,6},{8,9},{9,8},{10,11... | collective-permute-start | bytes 786440 | tf_op jit(solution)/shard_map/ppermute | solution.py:86
  507.0 7.3 %collective-permute-start.14 = (bf16[32,2048]{1,0:T(8,128)(2,1)S(1)}, bf16[32,2048]{1,0:T(8,128)(2,1)S(1)}, u32[]{:S(2)}, u32[]{:S(2)}) collective-permute-start(bf16[32,2048]{1,0:T(8,128)(2,1)S(1)} %dynamic-slice_bitcast_fusion.9), channel_id=1, source_target_pairs={{0,2},{1,3},{2,0},{3,1},{4,6},{5,7},{6,4},{7,5},{8,10},{9,11},{10,... | collective-permute-start | bytes 393224 | tf_op jit(solution)/shard_map/ppermute | solution.py:86
  509.8 7.3 %collective-permute-start.18 = (bf16[32,2048]{1,0:T(8,128)(2,1)S(1)}, bf16[32,2048]{1,0:T(8,128)(2,1)S(1)}, u32[]{:S(2)}, u32[]{:S(2)}) collective-permute-start(bf16[32,2048]{1,0:T(8,128)(2,1)S(1)} %dynamic-slice_bitcast_fusion.8), channel_id=1, source_target_pairs={{0,2},{1,3},{2,0},{3,1},{4,6},{5,7},{6,4},{7,5},{8,10},{9,11},{10,... | collective-permute-start | bytes 393224 | tf_op jit(solution)/shard_map/ppermute | solution.py:86
  (82 other events, 272.4 us)

commit v3 on v2

--- a/solution.py
+++ b/solution.py
@@ -518,12 +518,12 @@
 
 
 def forward_kernel(
-    table, marks, x, cosine, sine, seg_col, seg_row,
+    table, marks, x, dy, cosine, sine, seg_col, seg_row,
     wq, wk, wv, wu, wo, w1, w2, wd,
     mix_o, wo_o, w1_o, w2_o, wd_o, q_o, k_o, v_o, u_o, qp_o, kp_o, ob_o, hid_o, p1_o, p2_o, s_o,
-    state_o, mixed_o,
+    state_o, mixed_o, a1t_o, a2t_o, gt_o, dyt_o,
     fm, fo, f1, f2, fd, a1, q, k, v, u, qp, kp, att, ob, g, hid, p1, p2, s, mixed,
-    states, inbox, totals, outbox, result,
+    a1t, a2t, gt, dyt, states, inbox, totals, outbox, result,
     send, recv, own_sem, save_sem, scan_send, scan_recv,
 ):
     place = Place()
@@ -619,6 +619,16 @@
             value = x[at, :].astype(F32)
             scale = lax.rsqrt(jnp.mean(value * value, axis=-1, keepdims=True) + EPSILON)
             a1[at, :] = (value * scale).astype(BF16)
+
+    def turn_over(src, dst):
+        @pl.loop(0, width // 128)
+        def _(b):
+            other_c = (b + f) % 2
+            other_x = (b // 2 + f // 2) % 2
+            other_y = (b // 4 + f // 4) % 2
+            slot = other_c * 4 + other_y * 2 + other_x
+            value = src[:, cols(b * 128, 128)].astype(F32)
+            dst[pl.ds(pl.multiple_of(slot * 128, 128), 128), :] = value.T.astype(BF16)
 
     def project(base, pre, low, turn):
         @pl.loop(0, width // TILE)
@@ -678,6 +688,9 @@
             value = ob[at, :].astype(F32)
             scale = lax.rsqrt(jnp.mean(value * value, axis=-1, keepdims=True) + EPSILON)
             g[at, :] = (value * scale * u[at, :].astype(F32)).astype(BF16)
+
+        turn_over(g, gt)
+        save(gt, gt_o)
 
         @pl.loop(0, width // TILE)
         def _(t):
@@ -725,11 +738,15 @@
             project(3 * width, None, u, False)
             save(u, u_o)
             scan.totals_out()
+            turn_over(a1, a1t)
+            save(a1t, a1t_o)
         elif n == 4:
             attend_local()
             scan.forward()
         elif n == 5:
             scan.results_out()
+            turn_over(dy, dyt)
+            save(dyt, dyt_o)
         elif n == 6:
             scan.finish()
             save(result, state_o)
@@ -737,6 +754,8 @@
             save(ob, ob_o)
             hidden()
             save(hid, hid_o)
+            turn_over(g, a2t)
+            save(a2t, a2t_o)
         elif n == 8:
             up()
             save(p1, p1_o)
@@ -781,7 +800,7 @@
         copy.wait()
 
 
-def run_forward(table, marks, x, cosine, sine, seg_col, seg_row, weights):
+def run_forward(table, marks, x, dy, cosine, sine, seg_col, seg_row, weights):
     rows, width = x.shape
     hidden_size = weights[5].shape[1]
     row = jax.ShapeDtypeStruct((rows, width), BF16)
@@ -798,6 +817,7 @@
         + [jax.ShapeDtypeStruct((rows, width), F32)]
         + [tall] * 3
         + [jax.ShapeDtypeStruct((H, 2, DH, DH), BF16), row]
+        + [jax.ShapeDtypeStruct((width, rows), BF16)] * 4
     )
     rv = pltpu.VMEM((rows, width), BF16)
     tv = pltpu.VMEM((rows, hidden_size), BF16)
@@ -807,22 +827,23 @@
         + [pltpu.VMEM((rows, width), F32), rv, rv, pltpu.VMEM((rows, width), F32)]
         + [tv] * 3
         + [rv]
+        + [pltpu.VMEM((width, rows), BF16)] * 4
         + scan_scratch()
         + [pltpu.SemaphoreType.DMA((88,))] * 2
-        + [pltpu.SemaphoreType.DMA((11,)), pltpu.SemaphoreType.DMA((24,))]
+        + [pltpu.SemaphoreType.DMA((11,)), pltpu.SemaphoreType.DMA((28,))]
         + [pltpu.SemaphoreType.DMA((13,))] * 2
     )
     return pl.pallas_call(
         forward_kernel,
         out_shape=outs,
-        in_specs=[SMEM, SMEM] + [VMEM] * 5 + [ANY] * 8,
+        in_specs=[SMEM, SMEM] + [VMEM] * 6 + [ANY] * 8,
         out_specs=[ANY] * len(outs),
         scratch_shapes=scratch,
         compiler_params=pltpu.CompilerParams(
             collective_id=0, has_side_effects=True, vmem_limit_bytes=VMEM_BYTES
         ),
         name="forward",
-    )(table, marks, x, cosine, sine, seg_col, seg_row, *weights)
+    )(table, marks, x, dy, cosine, sine, seg_col, seg_row, *weights)
 
 
 def scan_scratch():
@@ -833,6 +854,436 @@
         pltpu.VMEM((4, 2, 2, DH, DH), BF16),
         pltpu.VMEM((H, 2, DH, DH), BF16),
     ]
+
+
+def backward_kernel(
+    table, marks, cosine, sine, seg_col, seg_row,
+    x_i, dy_i, wm_i, wo_i, w1_i, w2_i, wd_i, q_i, k_i, v_i, u_i, qp_i, kp_i, ob_i, hid_i,
+    p1_i, p2_i, s_i, state_i, a1t_i, a2t_i, gt_i, dyt_i,
+    grad_x_o, gq_o, gk_o, gv_o, gu_o, go_o, g1_o, g2_o, gd_o,
+    wd, w1, w2, s, p1, p2, dy, hid, dh, dz, ob, u, q, k, v, dqp, dkp, dv, state_in,
+    a1t, a2t, gt, dyt, states, inbox, totals, outbox, result,
+    give, take, merged, take_a, take_b, half_a, half_b, take2, mine, take3, pair, take4, final,
+    send, recv, free, load_sem, out_sem, scan_send, scan_recv,
+):
+    place = Place()
+    rows, width = dy.shape
+    chunk = rows // 2
+    hidden_size = s.shape[1]
+    place.greet()
+
+    loads = {}
+
+    def load(name, src, dst):
+        copy = pltpu.make_async_copy(src, dst, load_sem.at[len(loads)])
+        copy.start()
+        loads[name] = copy
+
+    def ready(*names):
+        for name in names:
+            loads[name].wait()
+
+    for name, src, dst in (
+        ("dyt", dyt_i, dyt), ("s", s_i, s), ("dy", dy_i, dy), ("wd", wd_i, wd), ("p1", p1_i, p1),
+        ("p2", p2_i, p2), ("a2t", a2t_i, a2t), ("w1", w1_i, w1), ("w2", w2_i, w2),
+        ("hid", hid_i, hid), ("ob", ob_i, ob), ("u", u_i, u), ("q", q_i, q), ("gt", gt_i, gt),
+        ("k", k_i, k), ("v", v_i, v), ("state", state_i, state_in), ("a1t", a1t_i, a1t),
+    ):
+        load(name, src, dst)
+
+    pieces = []
+    for left, right, out in ((dyt, s, gd_o), (a2t, p1, g1_o), (a2t, p2, g2_o)):
+        start = 0
+        while start < hidden_size:
+            size = min(1024, hidden_size - start)
+            pieces.append((left, right, out, start, size))
+            start += size
+    for left, right, out in (
+        (gt, dz, go_o), (a1t, u, gu_o), (a1t, dqp, gq_o), (a1t, dkp, gk_o), (a1t, dv, gv_o),
+    ):
+        pieces.append((left, right, out, 0, width))
+    count = len(pieces)
+    low, high = place.z % 2, place.z // 2
+    f = place.f
+    partner = [
+        place.at(f=place.fc),
+        place.at(f=place.fx),
+        place.at(f=place.fy),
+        place.at(f=place.fy),
+        place.at(f=place.fx),
+        place.at(z=place.zs[0]),
+        place.at(z=place.zs[1]),
+    ]
+
+    def move(n, t):
+        _, _, _, _, size = pieces[n]
+        slot, half = n % 2, size // 2
+        a, b, whole = pl.ds(0, half), pl.ds(half, half), pl.ds(0, size)
+        src, dst = [
+            (give.at[slot, :, whole], take.at[slot, :, whole]),
+            (merged.at[slot, :, 1, :, a], take_a.at[slot, :, :, a]),
+            (merged.at[slot, 1, :, :, b], take_b.at[slot, :, :, a]),
+            (half_a.at[slot, 1, :, a], take2.at[slot, 0, :, a]),
+            (half_b.at[slot, 1, :, a], take2.at[slot, 1, :, a]),
+            (mine.at[slot, :, 1 - low, :, whole], take3.at[slot, :, :, whole]),
+            (pair.at[slot, 1 - high, :, whole], take4.at[slot, :, whole]),
+        ][t]
+        return pltpu.make_async_remote_copy(
+            src_ref=src,
+            dst_ref=dst,
+            send_sem=send.at[2 * t + slot],
+            recv_sem=recv.at[2 * t + slot],
+            device_id=partner[t],
+            device_id_type=MESH,
+        )
+
+    def go(n, t):
+        if n >= 2:
+            pl.semaphore_wait(free.at[t], 1)
+        move(n, t).start()
+
+    def reuse(n, t):
+        if n >= 2:
+            move(n - 2, t).wait_send()
+
+    def got(n, t):
+        move(n, t).wait_recv()
+
+    def used(n, t):
+        if n + 2 < count:
+            pl.semaphore_signal(free.at[t], 1, device_id=partner[t], device_id_type=MESH)
+
+    def tiles(size):
+        return size // TILE
+
+    def give_half(n):
+        left, right, _, start, size = pieces[n]
+        slot = n % 2
+        reuse(n, 0)
+
+        @pl.loop(0, tiles(size))
+        def _(t):
+            value = kdot(left[rows : 2 * rows, :], right[:, cols(start + t * TILE, TILE)])
+            give[slot, :, cols(t * TILE, TILE)] = value.astype(BF16)
+
+        go(n, 0)
+
+    def merge(n):
+        left, right, _, start, size = pieces[n]
+        slot = n % 2
+        got(n, 0)
+        reuse(n, 1)
+        reuse(n, 2)
+
+        @pl.loop(0, tiles(size))
+        def _(t):
+            at = cols(t * TILE, TILE)
+            value = kdot(left[0:rows, :], right[:, cols(start + t * TILE, TILE)])
+            value = (value + take[slot, :, at].astype(F32)).astype(BF16)
+            for y in range(2):
+                for x in range(2):
+                    r = (2 * y + x) * 128
+                    merged[slot, y, x, :, at] = value[r : r + 128]
+
+        used(n, 0)
+        go(n, 1)
+        go(n, 2)
+
+    def add(a, b):
+        return a.astype(F32) + b.astype(F32)
+
+    def halve(n):
+        size = pieces[n][4]
+        slot, half = n % 2, size // 2
+        got(n, 1)
+        reuse(n, 3)
+        for i in (1, 0):
+            half_a[slot, i, :, :half] = add(
+                merged[slot, i, 0, :, :half], take_a[slot, i, :, :half]
+            ).astype(BF16)
+        used(n, 1)
+        go(n, 3)
+        got(n, 2)
+        reuse(n, 4)
+        for i in (1, 0):
+            half_b[slot, i, :, :half] = add(
+                merged[slot, 0, i, :, half:size], take_b[slot, i, :, :half]
+            ).astype(BF16)
+        used(n, 2)
+        go(n, 4)
+
+    def quarter(n):
+        size = pieces[n][4]
+        slot, half = n % 2, size // 2
+        reuse(n, 5)
+        for t, kept, at in ((3, half_a, slice(0, half)), (4, half_b, slice(half, size))):
+            got(n, t)
+            value = add(kept[slot, 0, :, :half], take2[slot, t - 3, :, :half]).astype(BF16)
+            used(n, t)
+            for i in range(4):
+                mine[slot, i // 2, i % 2, :, at] = value[32 * i : 32 * i + 32]
+        go(n, 5)
+
+    def along(n):
+        size = pieces[n][4]
+        slot = n % 2
+        got(n, 5)
+        reuse(n, 6)
+        for i in range(2):
+            pair[slot, i, :, :size] = add(
+                mine[slot, i, low, :, :size], take3[slot, i, :, :size]
+            ).astype(BF16)
+        used(n, 5)
+        go(n, 6)
+
+    def final_copy(n):
+        _, _, out, start, size = pieces[n]
+        slot = n % 2
+        return pltpu.make_async_copy(
+            final.at[slot, :, pl.ds(0, size)], out.at[:, pl.ds(start, size)], out_sem.at[slot]
+        )
+
+    def end(n):
+        size = pieces[n][4]
+        slot = n % 2
+        got(n, 6)
+        if n >= 2:
+            final_copy(n - 2).wait()
+        final[slot, :, :size] = add(pair[slot, high, :, :size], take4[slot, :, :size])
+        used(n, 6)
+        final_copy(n).start()
+
+    offset = lax.broadcasted_iota(jnp.int32, (chunk, 1), 0).astype(F32)
+    scan = Scan(place, table, 8, states, inbox, totals, outbox, result, scan_send, scan_recv)
+
+    def row_tiles(body):
+        @pl.loop(0, rows // 128)
+        def _(t):
+            body(pl.ds(pl.multiple_of(t * 128, 128), 128))
+
+    def inner():
+        ready("dy", "wd", "p1", "p2")
+
+        @pl.loop(0, hidden_size // TILE)
+        def _(t):
+            at = cols(t * TILE, TILE)
+            ds = kdot(dy[...], wd[pl.ds(pl.multiple_of(t * TILE, TILE), TILE), :], ((1,), (1,)))
+            first = p1[:, at].astype(F32)
+            p1[:, at] = (ds * p2[:, at].astype(F32)).astype(BF16)
+            p2[:, at] = (ds * first).astype(BF16)
+
+        load("wo", wo_i, wd.at[pl.ds(0, width)])
+
+    def middle():
+        ready("w1", "w2", "hid")
+
+        @pl.loop(0, width // TILE)
+        def _(t):
+            r = pl.ds(pl.multiple_of(t * TILE, TILE), TILE)
+            dh[:, cols(t * TILE, TILE)] = kdot(p1[...], w1[r, :], ((1,), (1,))) + kdot(
+                p2[...], w2[r, :], ((1,), (1,))
+            )
+
+        load("wq", wm_i.at[:, pl.ds(0, 2 * width)], w1.at[:, pl.ds(0, 2 * width)])
+        load("wv", wm_i.at[:, pl.ds(2 * width, 2 * width)], w2.at[:, pl.ds(0, 2 * width)])
+
+        def body(at):
+            value = hid[at, :]
+            scale = lax.rsqrt(jnp.mean(value * value, axis=-1, keepdims=True) + EPSILON)
+            normed = value * scale
+            grad = dh[at, :]
+            mean = jnp.mean(grad * normed, axis=-1, keepdims=True)
+            grad = dy[at, :].astype(F32) + scale * (grad - normed * mean)
+            dh[at, :] = grad
+            dz[at, :] = grad.astype(BF16)
+
+        row_tiles(body)
+        load("x", x_i, dy)
+
+    def outer():
+        ready("wo", "ob", "u", "q")
+
+        @pl.loop(0, width // TILE)
+        def _(t):
+            r = pl.ds(pl.multiple_of(t * TILE, TILE), TILE)
+            hid[:, cols(t * TILE, TILE)] = kdot(dz[...], wd[r, :], ((1,), (1,)))
+
+        def body(at):
+            value = ob[at, :].astype(F32)
+            scale = lax.rsqrt(jnp.mean(value * value, axis=-1, keepdims=True) + EPSILON)
+            normed = value * scale
+            grad = hid[at, :]
+            dm = grad * u[at, :].astype(F32)
+            u[at, :] = (grad * normed).astype(BF16)
+            mean = jnp.mean(dm * normed, axis=-1, keepdims=True)
+            ob[at, :] = (scale * (dm - normed * mean)).astype(BF16)
+
+        row_tiles(body)
+
+        @pl.loop(0, H)
+        def _(h):
+            at = cols(h * DH, DH)
+            for m in range(2):
+                r = slice(m * chunk, (m + 1) * chunk)
+                entering = edge(seg_col[r], marks[m], table[h], offset + 1.0)
+                left = (q[r, at].astype(F32) * entering).astype(BF16)
+                states[h, m] = kdot(left, ob[r, at], ((0,), (0,))).astype(BF16)
+
+        scan.start()
+
+    def turn_back(grad, pre):
+        grad = grad.astype(BF16).astype(F32)
+        pre = pre.astype(F32)
+        return grad, pre
+
+    def attend(first, last):
+        @pl.loop(first, last)
+        def _(h):
+            at = cols(h * DH, DH)
+            decay = decays(table[h], chunk)
+            for m in range(2):
+                r = slice(m * chunk, (m + 1) * chunk)
+                within = jnp.where(seg_col[r] == seg_row[m : m + 1], decay, 0.0)
+                entering = edge(seg_col[r], marks[m], table[h], offset + 1.0)
+                leaving = edge(seg_col[r], marks[2 + m], table[h], chunk - 1.0 - offset)
+                qh, kh, vh, oh = q[r, at], k[r, at], v[r, at], ob[r, at]
+                scores = (kdot(qh, kh, ((1,), (1,))) * within).astype(BF16)
+                grads = (kdot(oh, vh, ((1,), (1,))) * within).astype(BF16)
+                dq = kdot(grads, kh) + entering * kdot(oh, state_in[h, m], ((1,), (1,)))
+                dk = kdot(grads, qh, ((0,), (0,)))
+                dk = dk + leaving * kdot(vh, result[h, m], ((1,), (1,)))
+                grad_v = kdot(scores, oh, ((0,), (0,))) + leaving * kdot(kh, result[h, m])
+                dv[r, at] = grad_v.astype(BF16)
+                for grad, base, low_out in ((dq, 0, dqp), (dk, width, dkp)):
+                    grad = grad.astype(BF16).astype(F32)
+                    back = grad * cosine[r, :] - pltpu.roll(grad, DH // 2, 1) * sine[r, :]
+                    pre = s[r, cols(base + h * DH, DH)].astype(F32)
+                    sig = lax.logistic(pre)
+                    slope = sig * (1.0 + pre * (1.0 - sig))
+                    low_out[r, at] = (slope * back).astype(BF16)
+
+    def inputs():
+        ready("wq", "wv", "x")
+
+        @pl.loop(0, width // TILE)
+        def _(t):
+            r = pl.ds(pl.multiple_of(t * TILE, TILE), TILE)
+            acc = kdot(dqp[...], w1[r, 0:width], ((1,), (1,)))
+            acc += kdot(dkp[...], w1[r, width : 2 * width], ((1,), (1,)))
+            acc += kdot(dv[...], w2[r, 0:width], ((1,), (1,)))
+            acc += kdot(u[...], w2[r, width : 2 * width], ((1,), (1,)))
+            hid[:, cols(t * TILE, TILE)] = acc
+
+        def body(at):
+            value = dy[at, :].astype(F32)
+            scale = lax.rsqrt(jnp.mean(value * value, axis=-1, keepdims=True) + EPSILON)
+            normed = value * scale
+            grad = hid[at, :]
+            mean = jnp.mean(grad * normed, axis=-1, keepdims=True)
+            dz[at, :] = (dh[at, :] + scale * (grad - normed * mean)).astype(BF16)
+
+        row_tiles(body)
+        load("grad_x", dz, grad_x_o)
+
+    def work(n):
+        if n == 1:
+            inner()
+        elif n == 2:
+            ready("a2t")
+            middle()
+        elif n == 3:
+            load("qp", qp_i, s.at[:, pl.ds(0, width)])
+            load("kp", kp_i, s.at[:, pl.ds(width, width)])
+            outer()
+        elif n == 4:
+            scan.totals_out()
+        elif n == 5:
+            scan.forward()
+        elif n == 6:
+            scan.results_out()
+            ready("gt", "k", "v", "state", "a1t", "qp", "kp")
+        elif n == 7:
+            scan.finish()
+            attend(0, H // 2)
+        elif n == 8:
+            attend(H // 2, H)
+        elif n == 11:
+            inputs()
+
+    ready("dyt", "s")
+    for n in range(count + 5):
+        if n < count:
+            give_half(n)
+        if 0 <= n - 1 < count:
+            merge(n - 1)
+        if 0 <= n - 2 < count:
+            halve(n - 2)
+        if 0 <= n - 3 < count:
+            quarter(n - 3)
+        if 0 <= n - 4 < count:
+            along(n - 4)
+        if 0 <= n - 5 < count:
+            end(n - 5)
+        work(n)
+    for n in (count - 2, count - 1):
+        for t in range(7):
+            move(n, t).wait_send()
+        final_copy(n).wait()
+    ready("grad_x")
+
+
+def run_backward(table, marks, cosine, sine, seg_col, seg_row, x, dy, kept):
+    rows, width = x.shape
+    hidden_size = kept[2].shape[1]
+    part = width // 32
+    row = jax.ShapeDtypeStruct((rows, width), BF16)
+    outs = (
+        [row]
+        + [jax.ShapeDtypeStruct((part, width), F32)] * 5
+        + [jax.ShapeDtypeStruct((part, hidden_size), F32)] * 3
+    )
+    rv = pltpu.VMEM((rows, width), BF16)
+    fv = pltpu.VMEM((rows, width), F32)
+    tv = pltpu.VMEM((rows, hidden_size), BF16)
+    wv = pltpu.VMEM((width, hidden_size), BF16)
+    n = 1024
+    scratch = (
+        [pltpu.VMEM((hidden_size, width), BF16), wv, wv, tv, tv, tv, rv, fv, fv]
+        + [rv] * 9
+        + [pltpu.VMEM((H, 2, DH, DH), BF16)]
+        + [pltpu.VMEM((width, rows), BF16)] * 4
+        + scan_scratch()
+        + [
+            pltpu.VMEM((2, 512, n), BF16),
+            pltpu.VMEM((2, 512, n), BF16),
+            pltpu.VMEM((2, 2, 2, 128, n), BF16),
+            pltpu.VMEM((2, 2, 128, n // 2), BF16),
+            pltpu.VMEM((2, 2, 128, n // 2), BF16),
+            pltpu.VMEM((2, 2, 128, n // 2), BF16),
+            pltpu.VMEM((2, 2, 128, n // 2), BF16),
+            pltpu.VMEM((2, 2, 128, n // 2), BF16),
+            pltpu.VMEM((2, 2, 2, 32, n), BF16),
+            pltpu.VMEM((2, 2, 32, n), BF16),
+            pltpu.VMEM((2, 2, 32, n), BF16),
+            pltpu.VMEM((2, 32, n), BF16),
+            pltpu.VMEM((2, 32, n), F32),
+        ]
+        + [pltpu.SemaphoreType.DMA((14,))] * 2
+        + [pltpu.SemaphoreType.REGULAR((7,)), pltpu.SemaphoreType.DMA((26,))]
+        + [pltpu.SemaphoreType.DMA((2,))]
+        + [pltpu.SemaphoreType.DMA((13,))] * 2
+    )
+    return pl.pallas_call(
+        backward_kernel,
+        out_shape=outs,
+        in_specs=[SMEM, SMEM] + [VMEM] * 4 + [ANY] * (2 + len(kept)),
+        out_specs=[ANY] * len(outs),
+        scratch_shapes=scratch,
+        compiler_params=pltpu.CompilerParams(
+            collective_id=1, has_side_effects=True, vmem_limit_bytes=VMEM_BYTES
+        ),
+        name="backward",
+    )(table, marks, cosine, sine, seg_col, seg_row, x, dy, *kept)
 
 
 def factors(ends, rates, chunk, f, nf, nh, backward):
@@ -895,90 +1346,20 @@
     mine = H // nh
     rates = lax.dynamic_slice_in_dim(decay_rate, wires.h * mine, mine)
     table = jnp.concatenate([decay_rate, factors(ends, rates, chunk, wires.f, nf, nh, False)])
+    back_table = jnp.concatenate([decay_rate, factors(ends, rates, chunk, wires.f, nf, nh, True)])
     x = tokens.reshape(rows, width)
+    dy = cotangent.reshape(rows, width)
     seg_col = segs.reshape(rows, 1)
-    outs = run_forward(table, marks, x, cos_table, sin_table, seg_col, segs, weights)
-    (mix_weights, out_full, first_full, second_full, down_full) = outs[:5]
-    (q, k, v, u, query_pre, key_pre, attended, hidden, p1, p2, product, state_in, mixed) = outs[5:]
-
-    within, entering, leaving = masks(segs, before, last, decay_rate)
-    cosine = jnp.tile(cosine[:, None], (mb, 1, 1))
-    sine_vals = jnp.tile(sine_vals[:, None], (mb, 1, 1))
-
-    def heads(values):
-        return values.reshape(mb, chunk, H, DH).transpose(0, 2, 1, 3)
-
-    def flat(values):
-        return values.transpose(0, 2, 1, 3).reshape(rows, H * DH)
-
-    def mm(spec, a, b):
-        return jnp.einsum(spec, a.astype(BF16), b.astype(BF16), preferred_element_type=F32)
-
-    query_h, key_h, value_h = heads(q), heads(k), heads(v)
-    state_in = state_in.transpose(1, 0, 2, 3)
-    gate_vals = u.astype(F32)
-    query_pre, key_pre = query_pre.astype(F32), key_pre.astype(F32)
-    first_pre, second_pre = p1.astype(F32), p2.astype(F32)
-    normed_in, scale_in = norm_parts(x.astype(F32))
-    act_rel = wires.rel(normed_in.astype(BF16))
-    normed_att, scale_att = norm_parts(attended.astype(F32))
-    gated_rel = wires.rel((normed_att * gate_vals).astype(BF16))
-    normed_mid, scale_mid = norm_parts(hidden)
-    mid_rel = wires.rel(normed_mid.astype(BF16))
-    scores = (mm("mhsd,mhtd->mhst", query_h, key_h) * within).astype(BF16)
-
-    grad_low = cotangent.reshape(rows, width)
-    share_down = wires.reduce(dot_rows(wires.rel(grad_low), product)).T
-    grad_prod = dot_cols(grad_low, down_full)
-    grad_p1 = (grad_prod * second_pre).astype(BF16)
-    grad_p2 = (grad_prod * first_pre).astype(BF16)
-    share_first = wires.reduce(dot_rows(mid_rel, grad_p1))
-    share_second = wires.reduce(dot_rows(mid_rel, grad_p2))
-    grad_mid = dot_cols(grad_p1, first_full) + dot_cols(grad_p2, second_full)
-    grad_hidden = grad_low.astype(F32) + norm_back(grad_mid, normed_mid, scale_mid)
-    grad_hidden_low = grad_hidden.astype(BF16)
-    share_out = wires.reduce(dot_rows(gated_rel, grad_hidden_low))
-    grad_gated = dot_cols(grad_hidden_low, out_full)
-    grad_gate_low = (grad_gated * normed_att).astype(BF16)
-    grad_att = heads(norm_back(grad_gated * gate_vals, normed_att, scale_att).astype(BF16))
-    grad_state = mm("mhsd,mhse->mhde", query_h * entering, grad_att)
-    grad_end = chain(wires, grad_state, ends, decay_rate, chunk, True)
-    grad_scores = (mm("mhse,mhte->mhst", grad_att, value_h) * within).astype(BF16)
-    grad_q = mm("mhst,mhtd->mhsd", grad_scores, key_h)
-    grad_q = grad_q + entering * mm("mhse,mhde->mhsd", grad_att, state_in)
-    grad_k = mm("mhst,mhsd->mhtd", grad_scores, query_h)
-    grad_k = grad_k + leaving * mm("mhte,mhde->mhtd", value_h, grad_end)
-    grad_v = mm("mhst,mhse->mhte", scores, grad_att)
-    grad_v = grad_v + leaving * mm("mhtd,mhde->mhte", key_h, grad_end)
-
-    def turned_back(values, pre_values):
-        back = flat(values.astype(BF16)).astype(F32).reshape(rows, H, DH)
-        back = rotate_pairs(back, cosine, -sine_vals).reshape(rows, width)
-        return (silu_slope(pre_values) * back).astype(BF16)
-
-    grad_mix = jnp.concatenate(
-        [
-            turned_back(grad_q, query_pre),
-            turned_back(grad_k, key_pre),
-            flat(grad_v.astype(BF16)),
-            grad_gate_low,
-        ],
-        axis=1,
-    )
-    share_mix = wires.reduce(dot_rows(act_rel, grad_mix))
-    grad_act = dot_cols(grad_mix, mix_weights)
-    grad_tokens = (grad_hidden + norm_back(grad_act, normed_in, scale_in)).astype(BF16)
+    around = (marks, cos_table, sin_table, seg_col, segs)
+    outs = run_forward(table, marks, x, dy, *around[1:], weights)
+    mixed = outs[17]
+    kept = outs[:17] + outs[18:]
+    grads = run_backward(back_table, *around, x, dy, kept)
     return (
         mixed.reshape(mb, chunk, width),
-        grad_tokens.reshape(mb, chunk, width),
-        share_mix[:, :width],
-        share_mix[:, width : 2 * width],
-        share_mix[:, 2 * width : 3 * width],
-        share_mix[:, 3 * width :],
-        share_out,
-        share_first,
-        share_second,
-        share_down,
+        grads[0].reshape(mb, chunk, width),
+        *grads[1:8],
+        grads[8].T,
     )
 
 

time: 527 us -> 315 us (0.60); the launches traced: 519 us -> 314 us
  Pallas kernels: 139 us -> 293 us
  waiting for transfers between devices: 147 us -> 0 us
  matrix products: 67.4 us -> 0 us
  starting transfers between devices: 50.2 us -> 0 us
  local copies, waits for them, and re-layouts: 62.5 us -> 16.5 us
  other arithmetic: 49.7 us -> 3.73 us
    pallas_call x0 -> x1, Pallas kernels: none -> 154 us  [run_backward(): pl.pallas_call(backward_kernel, out_shape=outs, in_specs=[SMEM, SMEM] + [...]
    ppermute x55 -> x0, waiting for transfers between devices: 147 us -> none  [swap(): return lax.ppermute(values, AXES, pairs)]
    dot_general x18 -> x0, matrix products: 67.4 us -> none  [the longest x5 30.3 us: dot_cols(): lax.dot_general(a, b, (((1,), (1,)), ((), ())), preferred_element_type=F32)]
    ppermute x55 -> x0, starting transfers between devices: 50.2 us -> none  [swap(): return lax.ppermute(values, AXES, pairs)]
    convert_element_type x39 -> x0, other arithmetic: 22.2 us -> none  [the longest x5 11.1 us: reduce(): (low[:, :, 0].astype(F32) + self.swap(low[:, :, 1], core).astype(F32)).as...]
    unnamed x228 -> x31, local copies, waits for them, and re-layouts: 28.5 us -> 11.1 us
    slice x7 -> x1, local copies, waits for them, and re-layouts: 11.5 us -> 0.19 us  [factors(): last = at_group[:, -1]]
    gather x3 -> x0, local copies, waits for them, and re-layouts: 6.99 us -> none  [the longest x2 3.98 us: scatter(): return jnp.take(got, order, axis=0)]
  transfers between devices with their start and end apart: 55 -> 0, of which waited for: 39 -> 0; matrix products, arithmetic and copies ran while one was open for 24% -> 0% of each run, Pallas kernels for 0% -> 0%
where the time goes in v3:
time: 315 us; the launch traced here: 314 us
  Pallas kernels  293 us (93%)
  local copies, waits for them, and re-layouts  16.5 us (5%)
  other arithmetic  3.73 us (1%)
    pallas_call x1, Pallas kernels, run_backward(): pl.pallas_call(backward_kernel, out_shape=outs, in_specs=[SMEM, SMEM] + [...  154 us
    pallas_call x1, Pallas kernels, run_forward(): pl.pallas_call(forward_kernel, out_shape=outs, in_specs=[SMEM, SMEM] + [V...  139 us
    unnamed x31, local copies, waits for them, and re-layouts  11.1 us

profile of v3, /device:TPU:0, one launch (start us, length us, event | category | flops | bytes accessed | tf_op | source)
XLA Modules:
  0.0 314.5 jit_solution(8460210773801346519)
XLA Ops:
  0.7 0.7 dynamic-slice_negate_fusion
  1.5 0.9 reduce_window_sum.11
  2.3 0.1 convert_reduce_fusion.1
  2.4 0.2 select_reduce_fusion
  2.6 0.6 pad_add_fusion.1
  3.2 0.1 convert_reduce_fusion.seg_row
  3.3 0.0 copy-start.8
  3.3 0.1 constant_dynamic-slice_fusion
  3.4 0.2 slice_reduce_fusion.1
  3.6 0.1 broadcast_compare_fusion
  3.7 0.1 compare_and_fusion
  3.7 0.1 multiply_convert_fusion
  3.8 0.1 exponential_select_fusion.4
  3.9 0.1 select_n.110
  4.0 0.1 select_n.104
  4.1 0.1 reshape.288
  4.1 0.2 and_reduce_fusion
  4.3 0.2 slice_reduce_fusion
  4.6 0.1 compare_and_fusion.2
  4.6 0.1 exponential_select_fusion.2
  4.7 0.1 select_n.120
  4.8 0.1 select_n.108
  4.9 0.1 exponential_select_fusion
  5.0 0.1 select_n.122
  5.1 1.3 concatenate.28.table
  6.4 0.1 select_n.112
  6.5 1.3 concatenate.24.table
  7.8 0.3 fusion.5
  8.2 0.1 copy.46
  8.3 0.7 tile.19
  9.0 0.9 copy.53
  9.9 0.1 tile.8
  10.0 0.8 copy.47.cosine
  10.8 0.0 copy-done.8
  10.8 139.1 %forward.1 = (bf16[1024,4096]{1,0:T(8,128)(2,1)}, bf16[1024,1024]{1,0:T(8,128)(2,1)}, bf16[1024,2816]{1,0:T(8,128)(2,1)}, bf16[1024,2816]{1,0:T(8,128)(2,1)}, bf...) custom-call(f32[136]{0:T(256)} %concatenate.24.table, ...), custom_call_target="tpu_custom_call" | custom-call | tf_op jit(solution)/shard_map/forward/pallas_call | solution.py:836
  149.9 154.3 %backward.1 = (bf16[512,1024]{1,0:T(8,128)(2,1)}, f32[32,1024]{1,0:T(8,128)}, f32[32,1024]{1,0:T(8,128)}, f32[32,1024]{1,0:T(8,128)}, f32[32,1024]{1,0:T(8,128)}...) custom-call(f32[136]{0:T(256)} %concatenate.28.table, ...), custom_call_target="tpu_custom_call" | custom-call | tf_op jit(solution)/shard_map/backward/pallas_call | solution.py:1276
  304.2 0.0 copy-start.7
  304.2 0.0 copy-start.6
  304.3 0.0 copy-start.5
  304.3 0.0 copy-start.4
  304.3 0.0 copy-start.3
  304.3 0.0 copy-start.2
  304.3 0.0 copy-start.1
  304.3 2.4 copy.64
  306.7 0.0 copy-start
  306.7 2.3 copy.65
  309.0 0.0 copy-done.7
  309.0 0.7 copy.66
  309.6 0.0 copy-done.6
  309.6 0.7 copy.67
  310.3 0.0 copy-done.5
  310.3 0.7 copy.68
  311.0 0.0 copy-done.4
  311.0 0.7 copy.69
  311.6 0.0 copy-done.3
  311.6 0.7 copy.70
  312.3 0.0 copy-done.2
  312.3 0.7 copy.71
  313.0 0.0 copy-done.1
  313.0 0.7 copy.72
  313.8 0.0 copy-done
  313.8 0.7 copy.73
  (11 shorter events, 0.1 us)
Async XLA Ops:
  3.3 7.5 %copy-start.8 = (s32[2,256]{1,0:T(2,128)}, s32[2,256]{1,0:T(2,128)S(1)}, u32[]{:S(2)}) copy-start(s32[2,256]{1,0:T(2,128)S(1)} %convert_reduce_fusion.seg_row) | copy-start | bytes 6148
  304.2 4.7 %copy-start.7 = (f32[32,1024]{1,0:T(8,128)S(1)}, f32[32,1024]{1,0:T(8,128)}, u32[]{:S(2)}) copy-start(f32[32,1024]{1,0:T(8,128)} %get-tuple-element.114) | copy-start | bytes 393220
  304.2 5.4 %copy-start.6 = (f32[32,1024]{1,0:T(8,128)S(1)}, f32[32,1024]{1,0:T(8,128)}, u32[]{:S(2)}) copy-start(f32[32,1024]{1,0:T(8,128)} %get-tuple-element.115) | copy-start | bytes 393220
  304.3 6.0 %copy-start.5 = (f32[32,1024]{1,0:T(8,128)S(1)}, f32[32,1024]{1,0:T(8,128)}, u32[]{:S(2)}) copy-start(f32[32,1024]{1,0:T(8,128)} %get-tuple-element.116) | copy-start | bytes 393220
  304.3 6.7 %copy-start.4 = (f32[32,1024]{1,0:T(8,128)S(1)}, f32[32,1024]{1,0:T(8,128)}, u32[]{:S(2)}) copy-start(f32[32,1024]{1,0:T(8,128)} %get-tuple-element.117) | copy-start | bytes 393220
  304.3 7.3 %copy-start.3 = (f32[32,1024]{1,0:T(8,128)S(1)}, f32[32,1024]{1,0:T(8,128)}, u32[]{:S(2)}) copy-start(f32[32,1024]{1,0:T(8,128)} %get-tuple-element.118) | copy-start | bytes 393220
  304.3 8.0 %copy-start.2 = (f32[32,2816]{1,0:T(8,128)S(1)}, f32[32,2816]{1,0:T(8,128)}, u32[]{:S(2)}) copy-start(f32[32,2816]{1,0:T(8,128)} %get-tuple-element.119) | copy-start | bytes 1081348
  304.3 8.7 %copy-start.1 = (f32[32,2816]{1,0:T(8,128)S(1)}, f32[32,2816]{1,0:T(8,128)}, u32[]{:S(2)}) copy-start(f32[32,2816]{1,0:T(8,128)} %get-tuple-element.120) | copy-start | bytes 1081348
  306.7 7.1 %copy-start = (f32[32,2816]{1,0:T(8,128)S(1)}, f32[32,2816]{1,0:T(8,128)}, u32[]{:S(2)}) copy-start(f32[32,2816]{1,0:T(8,128)} %get-tuple-element.71) | copy-start | bytes 1081348

commit v4 on v3

--- a/solution.py
+++ b/solution.py
@@ -418,9 +418,88 @@
         pl.semaphore_wait(barrier, len(others))
 
 
+class Weigh:
+    def __init__(self, place, lengths, decay, chunk, backward):
+        self.p, self.decay, self.chunk, self.backward = place, decay, chunk, backward
+        self.sums = []
+        for m in range(2):
+            total, row = 0, []
+            for j in range(lengths.shape[1]):
+                total = total + lengths[m, j]
+                row.append(total)
+            self.sums.append(row)
+        first = 4 * place.f
+        self.ends = [[self.end(m, first + i) for i in range(-1, 4)] for m in range(2)]
+        self.groups = [[self.end(m, 4 * g + 3) for g in range(8)] for m in range(2)]
+        own = first + place.z
+        self.before = [self.end(m, own - 1) for m in range(2)]
+        self.last = [self.end(m, own) for m in range(2)]
+
+    def end(self, m, i):
+        position = (i + 1) * self.chunk - 1
+        return sum(jnp.where(total <= position, 1, 0) for total in self.sums[m])
+
+    def tables(self, cosine, sine, seg_col, seg_row):
+        chunk = self.chunk
+        base = (4 * self.p.f + self.p.z) * chunk
+        shape = (chunk, DH)
+        lane = lax.broadcasted_iota(jnp.int32, shape, 1)
+        row = lax.broadcasted_iota(jnp.int32, shape, 0) + base
+        half = DH // 2
+        turn = lane % half
+        speed = jnp.right_shift(jnp.full(shape, 651, jnp.int32), turn * 10 // half) + 1
+        angle = ((row * speed) % 4096).astype(F32) * (2.0 * math.pi / 4096.0)
+        cos, sin = jnp.cos(angle), jnp.sin(angle)
+        sin = jnp.where(lane < half, -sin, sin)
+        down = lax.broadcasted_iota(jnp.int32, (chunk, 1), 0) + base
+        across = lax.broadcasted_iota(jnp.int32, (1, chunk), 1) + base
+        for m in range(2):
+            at = slice(m * chunk, (m + 1) * chunk)
+            cosine[at, :] = cos
+            sine[at, :] = sin
+            seg_col[at, :] = sum(jnp.where(total <= down, 1, 0) for total in self.sums[m])
+            seg_row[m : m + 1, :] = sum(jnp.where(total <= across, 1, 0) for total in self.sums[m])
+
+    def power(self, same, chunks, hh):
+        rate = self.decay[2 * self.p.z + hh]
+        gap = jnp.asarray(chunks * self.chunk, jnp.int32).astype(F32)
+        value = jnp.exp(jnp.full((1, DH), -rate * gap, F32))
+        return jnp.where(same, value, 0.0)
+
+    def to_total(self, m, i, hh):
+        ends = self.ends[m]
+        if self.backward:
+            return self.power(ends[i] == ends[0], i, hh)
+        return self.power(ends[i + 1] == ends[4], 3 - i, hh)
+
+    def to_place(self, m, i, hh):
+        ends = self.ends[m]
+        if self.backward:
+            return self.power(ends[i + 1] == ends[4], 3 - i, hh)
+        return self.power(ends[i] == ends[0], i, hh)
+
+    def from_group(self, m, g, hh):
+        f = self.p.f
+        if self.backward:
+            before = self.groups[m][g - 1] if g > 0 else 0
+            same = (self.ends[m][4] == before) & (g > f)
+            return self.power(same, 4 * jnp.maximum(g - 1 - f, 0), hh)
+        same = (self.ends[m][0] == self.groups[m][g]) & (g < f)
+        return self.power(same, 4 * jnp.maximum(f - 1 - g, 0), hh)
+
+    def others(self, i):
+        return range(i + 1, 4) if self.backward else range(i)
+
+    def between(self, m, i, j, hh):
+        ends = self.ends[m]
+        if self.backward:
+            return self.power(ends[i + 1] == ends[j], j - 1 - i, hh)
+        return self.power(ends[i] == ends[j + 1], i - 1 - j, hh)
+
+
 class Scan:
-    def __init__(self, place, table, base, states, inbox, totals, outbox, result, send, recv):
-        self.p, self.table, self.base = place, table, base
+    def __init__(self, place, weigh, states, inbox, totals, outbox, result, send, recv):
+        self.p, self.weigh = place, weigh
         self.states, self.inbox, self.totals = states, inbox, totals
         self.outbox, self.result = outbox, result
         self.send, self.recv = send, recv
@@ -454,18 +533,16 @@
             self.to_heads(i).start()
         self.inbox[p.z] = self.states[pl.ds(2 * p.z, 2)]
 
-    def factor(self, offset):
-        return self.table[self.base + offset]
-
     def totals_out(self):
         p = self.p
         for i in range(3):
             self.to_heads(i).wait()
         for hh in range(2):
             for m in range(2):
-                acc = self.factor((m * 4) * 2 + hh) * self.inbox[0, hh, m].astype(F32)
-                for i in range(1, 4):
-                    acc += self.factor((m * 4 + i) * 2 + hh) * self.inbox[i, hh, m].astype(F32)
+                acc = sum(
+                    self.weigh.to_total(m, i, hh) * self.inbox[i, hh, m].astype(F32)
+                    for i in range(4)
+                )
                 self.totals[p.f, hh, m] = acc.astype(BF16)
         for n, where in ((3, p.fx), (4, p.fy), (5, p.fxy)):
             self.total(n, p.f, where).start()
@@ -484,18 +561,14 @@
             self.total(n + 3, where, p.fc).wait()
         for hh in range(2):
             for m in range(2):
-                outer = self.factor(16 + (m * 8) * 2 + hh) * self.totals[0, hh, m].astype(F32)
-                for g in range(1, 8):
-                    outer += self.factor(16 + (m * 8 + g) * 2 + hh) * self.totals[
-                        g, hh, m
-                    ].astype(F32)
+                outer = sum(
+                    self.weigh.from_group(m, g, hh) * self.totals[g, hh, m].astype(F32)
+                    for g in range(8)
+                )
                 for i in range(4):
-                    acc = self.factor(48 + (m * 4 + i) * 2 + hh) * outer
-                    for j in range(4):
-                        if i != j:
-                            acc += self.factor(64 + ((m * 4 + i) * 4 + j) * 2 + hh) * self.inbox[
-                                j, hh, m
-                            ].astype(F32)
+                    acc = self.weigh.to_place(m, i, hh) * outer
+                    for j in self.weigh.others(i):
+                        acc += self.weigh.between(m, i, j, hh) * self.inbox[j, hh, m].astype(F32)
                     self.outbox[i, hh, m] = acc.astype(BF16)
         for i in range(3):
             self.from_heads(i).start()
@@ -517,13 +590,23 @@
     return jnp.where(gap >= 0.0, jnp.exp(-rate * jnp.maximum(gap, 0.0)), 0.0)
 
 
+def up_tile(a2, w1, w2, s, dp1, dp2, t):
+    at = cols(t * TILE, TILE)
+    first = kdot(a2[...], w1[:, at])
+    second = kdot(a2[...], w2[:, at])
+    ds = dp1[:, at].astype(F32)
+    s[:, at] = (first * second).astype(BF16)
+    dp1[:, at] = (ds * second).astype(BF16)
+    dp2[:, at] = (ds * first).astype(BF16)
+
+
 def forward_kernel(
-    table, marks, x, dy, cosine, sine, seg_col, seg_row,
+    lengths, decay_rate, x, dy,
     wq, wk, wv, wu, wo, w1, w2, wd,
-    mix_o, wo_o, w1_o, w2_o, wd_o, q_o, k_o, v_o, u_o, qp_o, kp_o, ob_o, hid_o, p1_o, p2_o, s_o,
-    state_o, mixed_o, a1t_o, a2t_o, gt_o, dyt_o,
-    fm, fo, f1, f2, fd, a1, q, k, v, u, qp, kp, att, ob, g, hid, p1, p2, s, mixed,
-    a1t, a2t, gt, dyt, states, inbox, totals, outbox, result,
+    mix_o, wo_o, w1_o, w2_o, wd_o, q_o, k_o, v_o, u_o, qp_o, kp_o, ob_o, hid_o, dp1_o, dp2_o, s_o,
+    state_o, a2_o, a1t_o, a2t_o, gt_o, dyt_o,
+    fm, fo, f1, f2, fd, a1, q, k, v, u, qp, kp, att, ob, g, hid, dp1, dp2, s,
+    cosine, sine, seg_col, seg_row, a1t, a2t, gt, dyt, states, inbox, totals, outbox, result,
     send, recv, own_sem, save_sem, scan_send, scan_recv,
 ):
     place = Place()
@@ -535,63 +618,87 @@
     place.greet()
 
     pieces = []
-    for i, w in enumerate((wq, wk, wv, wu)):
-        pieces.append((w, fm, (0, 128), (0, width), (0, i * width)))
-    pieces.append((wo, fo, (0, 128), (0, width), (0, 0)))
+    for i, w in ((1, wk), (2, wv), (0, wq), (3, wu)):
+        pieces.append((w, fm, (0, 128), (0, width), i * width))
+    for part in range(2):
+        pieces.append((wd, fd, (part * half_hidden, half_hidden), (0, 128), None))
+    pieces.append((wo, fo, (0, 128), (0, width), 0))
     for part in range(2):
         for w, full in ((w1, f1), (w2, f2)):
-            pieces.append((w, full, (0, 128), (part * half_hidden, half_hidden), (0, part * half_hidden)))
-    for part in range(2):
-        pieces.append((wd, fd, (part * half_hidden, half_hidden), (0, 128), None))
+            at = part * half_hidden
+            pieces.append((w, full, (0, 128), (at, half_hidden), at))
     count = len(pieces)
-
-    def own(n):
+    parity = place.z % 2
+
+    def parts(n):
+        thin = (3, 2)[n % 2]
+        wide = 8 - thin
+        near = (wide + (n // 2) % 2) // 2
+        fetch = (parity * thin, wide)
+        return {
+            "all": (0, 8),
+            "fetch": fetch,
+            "near": (fetch[0], near),
+            "far": (fetch[0] + near, wide - near),
+            "give": (parity * wide, thin),
+            "take": ((1 - parity) * wide, thin),
+        }
+
+    def own(n, part="all"):
         w, _, (r, rs), (c, cs), _ = pieces[n]
-        return w.at[pl.ds(r, rs), pl.ds(c, cs)]
-
-    def block(n, origin, half=None):
+        at, size = parts(n)[part]
+        eighth = rs // 8
+        return w.at[pl.ds(pl.multiple_of(r + at * eighth, 16), size * eighth), pl.ds(c, cs)]
+
+    def block(n, origin, part="all"):
         _, full, (r, rs), (c, cs), to = pieces[n]
+        at, size = parts(n)[part]
+        eighth = rs // 8
         if to is None:
-            start, size, at, wide = r, rs, origin * 128, 128
-            if half is not None:
-                start, size = r + half * (rs // 2), rs // 2
-            return full.at[pl.ds(start, size), cols(at, wide)]
-        start, size = origin * 128, 128
-        if half is not None:
-            start, size = start + half * 64, 64
-        return full.at[pl.ds(pl.multiple_of(start, 64), size), pl.ds(to[1], cs)]
-
-    def move(n, step, src, dst, where):
+            start = pl.multiple_of(r + at * eighth, 16)
+            return full.at[pl.ds(start, size * eighth), cols(origin * 128, 128)]
+        start = pl.multiple_of(origin * 128 + at * eighth, 16)
+        return full.at[pl.ds(start, size * eighth), pl.ds(to, cs)]
+
+    fc, fx, fy, fxy = place.fc, place.fx, place.fy, place.fxy
+    at_c, at_x, at_y = (place.at(f=o) for o in (fc, fx, fy))
+    at_z = place.at(z=place.zs[0])
+
+    def step(n, t):
+        fetched = own(n, "fetch"), block(n, f, "fetch")
+        src, dst, where, lands = [
+            (own(n), block(n, f), at_c, (fc, "all")),
+            (*fetched, at_x, (fx, "fetch")),
+            (*fetched, at_y, (fy, "fetch")),
+            (block(n, fx, "near"), None, at_y, (fxy, "near")),
+            (block(n, fy, "far"), None, at_x, (fxy, "far")),
+            (block(n, fx, "give"), None, at_z, (fx, "take")),
+            (block(n, fy, "give"), None, at_z, (fy, "take")),
+            (block(n, fxy, "give"), None, at_z, (fxy, "take")),
+            (block(n, fx), None, at_c, (flip(fx, 1), "all")),
+            (block(n, fy), None, at_c, (flip(fy, 1), "all")),
+            (block(n, fxy), None, at_c, (flip(fxy, 1), "all")),
+        ][t]
+        return src, src if dst is None else dst, where, block(n, *lands)
+
+    def move(n, t, src, dst, where):
         return pltpu.make_async_remote_copy(
             src_ref=src,
             dst_ref=dst,
-            send_sem=send.at[n * 8 + step],
-            recv_sem=recv.at[n * 8 + step],
-            device_id=place.at(f=where),
+            send_sem=send.at[n * 11 + t],
+            recv_sem=recv.at[n * 11 + t],
+            device_id=where,
             device_id_type=MESH,
         )
 
-    fc, fx, fy, fxy = place.fc, place.fx, place.fy, place.fxy
-
-    def steps(n):
-        return [
-            (own(n), block(n, f), fc, block(n, fc)),
-            (own(n), block(n, f), fx, block(n, fx)),
-            (own(n), block(n, f), fy, block(n, fy)),
-            (block(n, fx, 0), block(n, fx, 0), fy, block(n, fxy, 0)),
-            (block(n, fy, 1), block(n, fy, 1), fx, block(n, fxy, 1)),
-            (block(n, fx), block(n, fx), fc, block(n, flip(fx, 1))),
-            (block(n, fy), block(n, fy), fc, block(n, flip(fy, 1))),
-            (block(n, fxy), block(n, fxy), fc, block(n, flip(fxy, 1))),
-        ]
-
-    def go(n, step):
-        src, dst, where, _ = steps(n)[step]
-        move(n, step, src, dst, where).start()
-
-    def got(n, step):
-        _, _, where, dst = steps(n)[step]
-        move(n, step, dst, dst, where).wait_recv()
+    def go(n, t):
+        src, dst, where, _ = step(n, t)
+        move(n, t, src, dst, where).start()
+
+    def got(n, *which):
+        for t in which:
+            _, _, where, lands = step(n, t)
+            move(n, t, lands, lands, where).wait_recv()
 
     def own_copy(n):
         return pltpu.make_async_copy(own(n), block(n, f), own_sem.at[n])
@@ -610,7 +717,7 @@
         if to is None:
             save(full.at[pl.ds(r, rs)], out.at[pl.ds(r, rs)])
         else:
-            save(full.at[:, pl.ds(to[1], cs)], out.at[:, pl.ds(to[1], cs)])
+            save(full.at[:, pl.ds(to, cs)], out.at[:, pl.ds(to, cs)])
 
     def norm_in():
         @pl.loop(0, rows // 128)
@@ -647,9 +754,8 @@
             low[:, at] = jnp.concatenate(turned, axis=1).astype(BF16)
 
     offset = lax.broadcasted_iota(jnp.int32, (chunk, 1), 0).astype(F32)
-    scan = Scan(
-        place, table, 8, states, inbox, totals, outbox, result, scan_send, scan_recv
-    )
+    weigh = Weigh(place, lengths, decay_rate, chunk, False)
+    scan = Scan(place, weigh, states, inbox, totals, outbox, result, scan_send, scan_recv)
 
     def local_states():
         @pl.loop(0, H)
@@ -657,15 +763,15 @@
             at = cols(h * DH, DH)
             for m in range(2):
                 r = slice(m * chunk, (m + 1) * chunk)
-                leaving = edge(seg_col[r], marks[2 + m], table[h], chunk - 1.0 - offset)
+                leaving = edge(seg_col[r], weigh.last[m], decay_rate[h], chunk - 1.0 - offset)
                 left = (k[r, at].astype(F32) * leaving).astype(BF16)
                 states[h, m] = kdot(left, v[r, at], ((0,), (0,))).astype(BF16)
 
-    def attend_local():
-        @pl.loop(0, H)
+    def attend_local(first, last):
+        @pl.loop(first, last)
         def _(h):
             at = cols(h * DH, DH)
-            decay = decays(table[h], chunk)
+            decay = decays(decay_rate[h], chunk)
             for m in range(2):
                 r = slice(m * chunk, (m + 1) * chunk)
                 within = jnp.where(seg_col[r] == seg_row[m : m + 1], decay, 0.0)
@@ -678,7 +784,7 @@
             at = cols(h * DH, DH)
             for m in range(2):
                 r = slice(m * chunk, (m + 1) * chunk)
-                entering = edge(seg_col[r], marks[m], table[h], offset + 1.0)
+                entering = edge(seg_col[r], weigh.before[m], decay_rate[h], offset + 1.0)
                 ob[r, at] = (att[r, at] + entering * kdot(q[r, at], result[h, m])).astype(BF16)
 
     def hidden():
@@ -704,73 +810,79 @@
             scale = lax.rsqrt(jnp.mean(value * value, axis=-1, keepdims=True) + EPSILON)
             g[at, :] = (value * scale).astype(BF16)
 
+    def inner(part):
+        @pl.loop(0, half_hidden // 128)
+        def _(t):
+            start = part * half_hidden + t * 128
+            rhs = fd[pl.ds(pl.multiple_of(start, 128), 128), :]
+            dp1[:, cols(start, 128)] = kdot(dy[...], rhs, ((1,), (1,))).astype(BF16)
+
     def up():
-        @pl.loop(0, hidden_size // TILE)
+        @pl.loop(0, half_hidden // TILE)
         def _(t):
-            at = cols(t * TILE, TILE)
-            first = kdot(g[...], f1[:, at])
-            second = kdot(g[...], f2[:, at])
-            p1[:, at] = first.astype(BF16)
-            p2[:, at] = second.astype(BF16)
-            s[:, at] = (first * second).astype(BF16)
-
-    def down():
-        @pl.loop(0, width // TILE)
-        def _(t):
-            at = cols(t * TILE, TILE)
-            mixed[:, at] = (hid[:, at] + kdot(s[...], fd[:, at])).astype(BF16)
+            up_tile(g, f1, f2, s, dp1, dp2, t)
 
     def work(n):
         if n == 0:
-            project(0, qp, q, True)
-            save(q, q_o)
-            save(qp, qp_o)
-        elif n == 1:
             project(width, kp, k, True)
             save(k, k_o)
             save(kp, kp_o)
-        elif n == 2:
+        elif n == 1:
             project(2 * width, None, v, False)
             local_states()
             scan.start()
             save(v, v_o)
+        elif n == 2:
+            project(0, qp, q, True)
+            save(q, q_o)
+            save(qp, qp_o)
         elif n == 3:
             project(3 * width, None, u, False)
             save(u, u_o)
             scan.totals_out()
-            turn_over(a1, a1t)
-            save(a1t, a1t_o)
         elif n == 4:
-            attend_local()
+            attend_local(0, H // 2)
             scan.forward()
         elif n == 5:
+            attend_local(H // 2, H)
             scan.results_out()
-            turn_over(dy, dyt)
-            save(dyt, dyt_o)
         elif n == 6:
+            inner(0)
+            inner(1)
+        elif n == 7:
             scan.finish()
             save(result, state_o)
             attend_rest()
             save(ob, ob_o)
             hidden()
             save(hid, hid_o)
+            save(g, a2_o)
+        elif n == 8:
+            up()
+            done = pl.ds(0, half_hidden // TILE * TILE)
+            save(s.at[:, done], s_o.at[:, done])
+            save(dp1, dp1_o)
+            save(dp2.at[:, done], dp2_o.at[:, done])
+        elif n == 9:
             turn_over(g, a2t)
             save(a2t, a2t_o)
-        elif n == 8:
-            up()
-            save(p1, p1_o)
-            save(p2, p2_o)
-            save(s, s_o)
-        elif n == 10:
-            down()
-            save(mixed, mixed_o)
-
-    for n in range(2):
-        for step in (1, 2, 0):
-            go(n, step)
+
+    def early(n):
+        if n == 0:
+            turn_over(dy, dyt)
+            save(dyt, dyt_o)
+        elif n == 1:
+            turn_over(a1, a1t)
+            save(a1t, a1t_o)
+
+    ahead = 2
+    for n in range(ahead):
+        for t in (1, 2, 0):
+            go(n, t)
         own_copy(n).start()
+    weigh.tables(cosine, sine, seg_col, seg_row)
     norm_in()
-    for n in range(count + 2):
+    for n in range(count + 3):
         if n < count:
             got(n, 1)
             go(n, 3)
@@ -778,29 +890,36 @@
             got(n, 2)
             go(n, 4)
             go(n, 6)
-            if n + 2 < count:
-                for step in (1, 2, 0):
-                    go(n + 2, step)
-                own_copy(n + 2).start()
+            if n + ahead < count:
+                for t in (1, 2, 0):
+                    go(n + ahead, t)
+                own_copy(n + ahead).start()
         if 0 <= n - 1 < count:
-            got(n - 1, 3)
-            got(n - 1, 4)
+            got(n - 1, 3, 4)
             go(n - 1, 7)
-        if n - 2 >= 0:
-            for step in (0, 5, 6, 7):
-                got(n - 2, step)
-            own_copy(n - 2).wait()
-            save_piece(n - 2)
-            work(n - 2)
+            got(n - 1, 5)
+            go(n - 1, 8)
+            got(n - 1, 6)
+            go(n - 1, 9)
+        if 0 <= n - 2 < count:
+            got(n - 2, 7)
+            go(n - 2, 10)
+        if n - 3 >= 0:
+            got(n - 3, 0, 8, 9, 10)
+            own_copy(n - 3).wait()
+            save_piece(n - 3)
+            work(n - 3)
+        else:
+            early(n)
     for n in range(count):
-        for step in range(8):
-            src, dst, where, _ = steps(n)[step]
-            move(n, step, src, dst, where).wait_send()
+        for t in range(11):
+            src, dst, where, _ = step(n, t)
+            move(n, t, src, dst, where).wait_send()
     for copy in saves:
         copy.wait()
 
 
-def run_forward(table, marks, x, dy, cosine, sine, seg_col, seg_row, weights):
+def run_forward(lengths, decay_rate, x, dy, weights):
     rows, width = x.shape
     hidden_size = weights[5].shape[1]
     row = jax.ShapeDtypeStruct((rows, width), BF16)
@@ -826,24 +945,33 @@
         + [rv] * 7
         + [pltpu.VMEM((rows, width), F32), rv, rv, pltpu.VMEM((rows, width), F32)]
         + [tv] * 3
-        + [rv]
+        + table_scratch(rows)
         + [pltpu.VMEM((width, rows), BF16)] * 4
         + scan_scratch()
-        + [pltpu.SemaphoreType.DMA((88,))] * 2
+        + [pltpu.SemaphoreType.DMA((121,))] * 2
         + [pltpu.SemaphoreType.DMA((11,)), pltpu.SemaphoreType.DMA((28,))]
         + [pltpu.SemaphoreType.DMA((13,))] * 2
     )
     return pl.pallas_call(
         forward_kernel,
         out_shape=outs,
-        in_specs=[SMEM, SMEM] + [VMEM] * 6 + [ANY] * 8,
+        in_specs=[SMEM, SMEM] + [VMEM] * 2 + [ANY] * 8,
         out_specs=[ANY] * len(outs),
         scratch_shapes=scratch,
         compiler_params=pltpu.CompilerParams(
             collective_id=0, has_side_effects=True, vmem_limit_bytes=VMEM_BYTES
         ),
         name="forward",
-    )(table, marks, x, dy, cosine, sine, seg_col, seg_row, *weights)
+    )(lengths, decay_rate, x, dy, *weights)
+
+
+def table_scratch(rows):
+    return [
+        pltpu.VMEM((rows, DH), F32),
+        pltpu.VMEM((rows, DH), F32),
+        pltpu.VMEM((rows, 1), jnp.int32),
+        pltpu.VMEM((2, rows // 2), jnp.int32),
+    ]
 
 
 def scan_scratch():
@@ -856,15 +984,20 @@
     ]
 
 
+Z_FIRST = (10,)
+LAST = 1024
+
+
 def backward_kernel(
-    table, marks, cosine, sine, seg_col, seg_row,
+    lengths, decay_rate,
     x_i, dy_i, wm_i, wo_i, w1_i, w2_i, wd_i, q_i, k_i, v_i, u_i, qp_i, kp_i, ob_i, hid_i,
-    p1_i, p2_i, s_i, state_i, a1t_i, a2t_i, gt_i, dyt_i,
-    grad_x_o, gq_o, gk_o, gv_o, gu_o, go_o, g1_o, g2_o, gd_o,
+    p1_i, p2_i, s_i, state_i, a2_i, a1t_i, a2t_i, gt_i, dyt_i,
+    mixed_o, grad_x_o, gq_o, gk_o, gv_o, gu_o, go_o, g1_o, g2_o, gd_o,
     wd, w1, w2, s, p1, p2, dy, hid, dh, dz, ob, u, q, k, v, dqp, dkp, dv, state_in,
-    a1t, a2t, gt, dyt, states, inbox, totals, outbox, result,
+    cosine, sine, seg_col, seg_row, a1t, a2t, gt, dyt, states, inbox, totals, outbox, result,
     give, take, merged, take_a, take_b, half_a, half_b, take2, mine, take3, pair, take4, final,
-    send, recv, free, load_sem, out_sem, scan_send, scan_recv,
+    z_take, z_sum, z_take2, z_sum2, z_take_a, z_take_b, z_half_a, z_half_b, z_take3, z_final,
+    send, recv, free, z_send, z_recv, z_free, load_sem, out_sem, scan_send, scan_recv,
 ):
     place = Place()
     rows, width = dy.shape
@@ -883,51 +1016,50 @@
         for name in names:
             loads[name].wait()
 
+    done = pl.ds(0, hidden_size // 2 // TILE * TILE)
     for name, src, dst in (
-        ("dyt", dyt_i, dyt), ("s", s_i, s), ("dy", dy_i, dy), ("wd", wd_i, wd), ("p1", p1_i, p1),
-        ("p2", p2_i, p2), ("a2t", a2t_i, a2t), ("w1", w1_i, w1), ("w2", w2_i, w2),
-        ("hid", hid_i, hid), ("ob", ob_i, ob), ("u", u_i, u), ("q", q_i, q), ("gt", gt_i, gt),
+        ("dyt", dyt_i, dyt), ("s", s_i.at[:, done], s.at[:, done]), ("a2t", a2t_i, a2t), ("p1", p1_i, p1),
+        ("p2", p2_i.at[:, done], p2.at[:, done]), ("a2", a2_i, dkp), ("w1", w1_i, w1), ("w2", w2_i, w2),
+        ("hid", hid_i, hid), ("wd", wd_i, wd), ("dy", dy_i, dy), ("ob", ob_i, ob), ("u", u_i, u), ("q", q_i, q), ("gt", gt_i, gt),
         ("k", k_i, k), ("v", v_i, v), ("state", state_i, state_in), ("a1t", a1t_i, a1t),
     ):
         load(name, src, dst)
 
     pieces = []
-    for left, right, out in ((dyt, s, gd_o), (a2t, p1, g1_o), (a2t, p2, g2_o)):
-        start = 0
-        while start < hidden_size:
-            size = min(1024, hidden_size - start)
+    for start in range(0, hidden_size, 1024):
+        size = min(1024, hidden_size - start)
+        for left, right, out in ((dyt, s, gd_o), (a2t, p1, g1_o), (a2t, p2, g2_o)):
             pieces.append((left, right, out, start, size))
-            start += size
-    for left, right, out in (
-        (gt, dz, go_o), (a1t, u, gu_o), (a1t, dqp, gq_o), (a1t, dkp, gk_o), (a1t, dv, gv_o),
-    ):
+    for left, right, out in ((gt, dz, go_o), (a1t, u, gu_o), (a1t, dqp, gq_o), (a1t, dkp, gk_o)):
         pieces.append((left, right, out, 0, width))
+    for start in range(0, width, LAST):
+        pieces.append((a1t, dv, gv_o, start, LAST))
     count = len(pieces)
+    level = [n for n in range(count) if n not in Z_FIRST]
+    upright = [n for n in range(count) if n in Z_FIRST]
     low, high = place.z % 2, place.z // 2
     f = place.f
-    partner = [
-        place.at(f=place.fc),
-        place.at(f=place.fx),
-        place.at(f=place.fy),
-        place.at(f=place.fy),
-        place.at(f=place.fx),
-        place.at(z=place.zs[0]),
-        place.at(z=place.zs[1]),
-    ]
+    at_c, at_x, at_y = (place.at(f=o) for o in (place.fc, place.fx, place.fy))
+    at_z1, at_z2 = (place.at(z=place.zs[i]) for i in range(2))
+    partner = [at_c, at_x, at_y, at_y, at_x, at_z1, at_z2]
+    z_partner = [at_z1, at_z2, at_x, at_y, at_y, at_x]
+
+    def turn(n, t):
+        return n if t == 0 else level.index(n)
 
     def move(n, t):
-        _, _, _, _, size = pieces[n]
-        slot, half = n % 2, size // 2
+        size = pieces[n][4]
+        m, slot, half = n % 2, turn(n, t) % 2, size // 2
         a, b, whole = pl.ds(0, half), pl.ds(half, half), pl.ds(0, size)
         src, dst = [
-            (give.at[slot, :, whole], take.at[slot, :, whole]),
-            (merged.at[slot, :, 1, :, a], take_a.at[slot, :, :, a]),
-            (merged.at[slot, 1, :, :, b], take_b.at[slot, :, :, a]),
-            (half_a.at[slot, 1, :, a], take2.at[slot, 0, :, a]),
-            (half_b.at[slot, 1, :, a], take2.at[slot, 1, :, a]),
-            (mine.at[slot, :, 1 - low, :, whole], take3.at[slot, :, :, whole]),
-            (pair.at[slot, 1 - high, :, whole], take4.at[slot, :, whole]),
-        ][t]
+            lambda: (give.at[slot, :, whole], take.at[slot, :, whole]),
+            lambda: (merged.at[m, :, 1, :, :, :, a], take_a.at[slot, :, :, :, :, a]),
+            lambda: (merged.at[m, 1, :, :, :, :, b], take_b.at[slot, :, :, :, :, a]),
+            lambda: (half_a.at[slot, 1, :, :, :, a], take2.at[slot, 0, :, :, :, a]),
+            lambda: (half_b.at[slot, 1, :, :, :, a], take2.at[slot, 1, :, :, :, a]),
+            lambda: (mine.at[slot, :, 1 - low, :, whole], take3.at[slot, :, :, whole]),
+            lambda: (pair.at[slot, 1 - high, :, whole], take4.at[slot, :, whole]),
+        ][t]()
         return pltpu.make_async_remote_copy(
             src_ref=src,
             dst_ref=dst,
@@ -937,96 +1069,141 @@
             device_id_type=MESH,
         )
 
+    def z_move(n, t):
+        size = pieces[n][4]
+        half = size // 2
+        a, b, whole = pl.ds(0, half), pl.ds(half, half), pl.ds(0, size)
+        src, dst = [
+            lambda: (merged.at[n % 2, :, :, :, 1 - low, :, whole], z_take.at[:, :, :, :, whole]),
+            lambda: (z_sum.at[:, :, 1 - high, :, whole], z_take2.at[:, :, :, whole]),
+            lambda: (z_sum2.at[:, 1, :, a], z_take_a.at[:, :, a]),
+            lambda: (z_sum2.at[1, :, :, b], z_take_b.at[:, :, a]),
+            lambda: (z_half_a.at[1, :, a], z_take3.at[0, :, a]),
+            lambda: (z_half_b.at[1, :, a], z_take3.at[1, :, a]),
+        ][t]()
+        return pltpu.make_async_remote_copy(
+            src_ref=src,
+            dst_ref=dst,
+            send_sem=z_send.at[t],
+            recv_sem=z_recv.at[t],
+            device_id=z_partner[t],
+            device_id_type=MESH,
+        )
+
+    def order(t):
+        return list(range(count)) if t == 0 else level
+
     def go(n, t):
-        if n >= 2:
+        if turn(n, t) >= 2:
             pl.semaphore_wait(free.at[t], 1)
         move(n, t).start()
 
     def reuse(n, t):
-        if n >= 2:
-            move(n - 2, t).wait_send()
+        i = turn(n, t)
+        if i >= 2:
+            move(order(t)[i - 2], t).wait_send()
 
     def got(n, t):
         move(n, t).wait_recv()
 
     def used(n, t):
-        if n + 2 < count:
+        if turn(n, t) + 2 < len(order(t)):
             pl.semaphore_signal(free.at[t], 1, device_id=partner[t], device_id_type=MESH)
 
-    def tiles(size):
-        return size // TILE
+    def z_go(n, t):
+        if n != upright[0]:
+            pl.semaphore_wait(z_free.at[t], 1)
+        z_move(n, t).start()
+
+    def z_reuse(n, t):
+        i = upright.index(n)
+        if i >= 1:
+            z_move(upright[i - 1], t).wait_send()
+
+    def z_used(n, t):
+        if n != upright[-1]:
+            pl.semaphore_signal(z_free.at[t], 1, device_id=z_partner[t], device_id_type=MESH)
 
     def give_half(n):
         left, right, _, start, size = pieces[n]
         slot = n % 2
         reuse(n, 0)
 
-        @pl.loop(0, tiles(size))
+        @pl.loop(0, size // TILE)
         def _(t):
             value = kdot(left[rows : 2 * rows, :], right[:, cols(start + t * TILE, TILE)])
             give[slot, :, cols(t * TILE, TILE)] = value.astype(BF16)
 
         go(n, 0)
+
+    def sent(n):
+        if n in level:
+            move(n, 1).wait_send()
+            move(n, 2).wait_send()
+        else:
+            z_move(n, 0).wait_send()
 
     def merge(n):
         left, right, _, start, size = pieces[n]
         slot = n % 2
         got(n, 0)
-        reuse(n, 1)
-        reuse(n, 2)
-
-        @pl.loop(0, tiles(size))
+        if n >= 2:
+            sent(n - 2)
+
+        @pl.loop(0, size // TILE)
         def _(t):
             at = cols(t * TILE, TILE)
             value = kdot(left[0:rows, :], right[:, cols(start + t * TILE, TILE)])
             value = (value + take[slot, :, at].astype(F32)).astype(BF16)
-            for y in range(2):
-                for x in range(2):
-                    r = (2 * y + x) * 128
-                    merged[slot, y, x, :, at] = value[r : r + 128]
+            for i in range(16):
+                r = i * 32
+                merged[slot, i // 8, i // 4 % 2, i // 2 % 2, i % 2, :, at] = value[r : r + 32]
 
         used(n, 0)
-        go(n, 1)
-        go(n, 2)
+        if n in level:
+            go(n, 1)
+            go(n, 2)
+        else:
+            z_go(n, 0)
 
     def add(a, b):
         return a.astype(F32) + b.astype(F32)
 
     def halve(n):
         size = pieces[n][4]
-        slot, half = n % 2, size // 2
+        m, slot, half = n % 2, turn(n, 1) % 2, size // 2
         got(n, 1)
         reuse(n, 3)
         for i in (1, 0):
-            half_a[slot, i, :, :half] = add(
-                merged[slot, i, 0, :, :half], take_a[slot, i, :, :half]
+            half_a[slot, i, :, :, :, :half] = add(
+                merged[m, i, 0, :, :, :, :half], take_a[slot, i, :, :, :, :half]
             ).astype(BF16)
         used(n, 1)
         go(n, 3)
         got(n, 2)
         reuse(n, 4)
         for i in (1, 0):
-            half_b[slot, i, :, :half] = add(
-                merged[slot, 0, i, :, half:size], take_b[slot, i, :, :half]
+            half_b[slot, i, :, :, :, :half] = add(
+                merged[m, 0, i, :, :, :, half:size], take_b[slot, i, :, :, :, :half]
             ).astype(BF16)
         used(n, 2)
         go(n, 4)
 
     def quarter(n):
         size = pieces[n][4]
-        slot, half = n % 2, size // 2
+        slot, half = turn(n, 1) % 2, size // 2
         reuse(n, 5)
         for t, kept, at in ((3, half_a, slice(0, half)), (4, half_b, slice(half, size))):
             got(n, t)
-            value = add(kept[slot, 0, :, :half], take2[slot, t - 3, :, :half]).astype(BF16)
+            mine[slot, :, :, :, at] = add(
+                kept[slot, 0, :, :, :, :half], take2[slot, t - 3, :, :, :, :half]
+            ).astype(BF16)
             used(n, t)
-            for i in range(4):
-                mine[slot, i // 2, i % 2, :, at] = value[32 * i : 32 * i + 32]
         go(n, 5)
 
     def along(n):
         size = pieces[n][4]
-        slot = n % 2
+        slot = turn(n, 1) % 2
         got(n, 5)
         reuse(n, 6)
         for i in range(2):
@@ -1036,54 +1213,113 @@
         used(n, 5)
         go(n, 6)
 
+    def result_copy(n, src, sem):
+        _, _, out, start, size = pieces[n]
+        return pltpu.make_async_copy(src.at[:, pl.ds(0, size)], out.at[:, pl.ds(start, size)], sem)
+
     def final_copy(n):
-        _, _, out, start, size = pieces[n]
-        slot = n % 2
-        return pltpu.make_async_copy(
-            final.at[slot, :, pl.ds(0, size)], out.at[:, pl.ds(start, size)], out_sem.at[slot]
-        )
+        slot = turn(n, 1) % 2
+        return result_copy(n, final.at[slot], out_sem.at[slot])
 
     def end(n):
         size = pieces[n][4]
-        slot = n % 2
+        i = turn(n, 1)
+        slot = i % 2
         got(n, 6)
-        if n >= 2:
-            final_copy(n - 2).wait()
+        if i >= 2:
+            final_copy(level[i - 2]).wait()
         final[slot, :, :size] = add(pair[slot, high, :, :size], take4[slot, :, :size])
         used(n, 6)
         final_copy(n).start()
 
+    def z_halve(n):
+        size = pieces[n][4]
+        z_move(n, 0).wait_recv()
+        z_reuse(n, 1)
+        for y in range(2):
+            z_sum[y, :, :, :, :size] = add(
+                merged[n % 2, y, :, :, low, :, :size], z_take[y, :, :, :, :size]
+            ).astype(BF16)
+        z_used(n, 0)
+        z_go(n, 1)
+
+    def z_quarter(n):
+        size = pieces[n][4]
+        z_move(n, 1).wait_recv()
+        z_reuse(n, 2)
+        z_reuse(n, 3)
+        z_sum2[:, :, :, :size] = add(
+            z_sum[:, :, high, :, :size], z_take2[:, :, :, :size]
+        ).astype(BF16)
+        z_used(n, 1)
+        z_go(n, 2)
+        z_go(n, 3)
+
+    def z_along(n):
+        size = pieces[n][4]
+        half = size // 2
+        z_move(n, 2).wait_recv()
+        z_reuse(n, 4)
+        z_half_a[:, :, :half] = add(z_sum2[:, 0, :, :half], z_take_a[:, :, :half]).astype(BF16)
+        z_used(n, 2)
+        z_go(n, 4)
+        z_move(n, 3).wait_recv()
+        z_reuse(n, 5)
+        z_half_b[:, :, :half] = add(z_sum2[0, :, :, half:size], z_take_b[:, :, :half]).astype(BF16)
+        z_used(n, 3)
+        z_go(n, 5)
+
+    def z_copy(n):
+        return result_copy(n, z_final, out_sem.at[2])
+
+    def z_end(n):
+        size = pieces[n][4]
+        half = size // 2
+        if n != upright[0]:
+            z_copy(upright[upright.index(n) - 1]).wait()
+        for t, kept, at in ((4, z_half_a, slice(0, half)), (5, z_half_b, slice(half, size))):
+            z_move(n, t).wait_recv()
+            z_final[:, at] = add(kept[0, :, :half], z_take3[t - 4, :, :half])
+            z_used(n, t)
+        z_copy(n).start()
+
     offset = lax.broadcasted_iota(jnp.int32, (chunk, 1), 0).astype(F32)
-    scan = Scan(place, table, 8, states, inbox, totals, outbox, result, scan_send, scan_recv)
+    weigh = Weigh(place, lengths, decay_rate, chunk, True)
+    scan = Scan(place, weigh, states, inbox, totals, outbox, result, scan_send, scan_recv)
 
     def row_tiles(body):
         @pl.loop(0, rows // 128)
         def _(t):
             body(pl.ds(pl.multiple_of(t * 128, 128), 128))
 
-    def inner():
-        ready("dy", "wd", "p1", "p2")
-
-        @pl.loop(0, hidden_size // TILE)
+    def up():
+        ready("a2", "w1", "w2")
+
+        @pl.loop(hidden_size // 2 // TILE, hidden_size // TILE)
+        def _(t):
+            up_tile(dkp, w1, w2, s, p1, p2, t)
+
+    def mix():
+        ready("wd")
+
+        @pl.loop(0, width // TILE)
         def _(t):
             at = cols(t * TILE, TILE)
-            ds = kdot(dy[...], wd[pl.ds(pl.multiple_of(t * TILE, TILE), TILE), :], ((1,), (1,)))
-            first = p1[:, at].astype(F32)
-            p1[:, at] = (ds * p2[:, at].astype(F32)).astype(BF16)
-            p2[:, at] = (ds * first).astype(BF16)
-
+            dqp[:, at] = (hid[:, at] + kdot(s[...], wd[:, at])).astype(BF16)
+
+        load("mixed", dqp, mixed_o)
         load("wo", wo_i, wd.at[pl.ds(0, width)])
 
-    def middle():
-        ready("w1", "w2", "hid")
-
-        @pl.loop(0, width // TILE)
+    def middle(first, last):
+        @pl.loop(first, last)
         def _(t):
             r = pl.ds(pl.multiple_of(t * TILE, TILE), TILE)
             dh[:, cols(t * TILE, TILE)] = kdot(p1[...], w1[r, :], ((1,), (1,))) + kdot(
                 p2[...], w2[r, :], ((1,), (1,))
             )
 
+    def middle_rows():
+        ready("dy")
         load("wq", wm_i.at[:, pl.ds(0, 2 * width)], w1.at[:, pl.ds(0, 2 * width)])
         load("wv", wm_i.at[:, pl.ds(2 * width, 2 * width)], w2.at[:, pl.ds(0, 2 * width)])
 
@@ -1101,7 +1337,7 @@
         load("x", x_i, dy)
 
     def outer():
-        ready("wo", "ob", "u", "q")
+        ready("wo", "ob", "u")
 
         @pl.loop(0, width // TILE)
         def _(t):
@@ -1125,47 +1361,55 @@
             at = cols(h * DH, DH)
             for m in range(2):
                 r = slice(m * chunk, (m + 1) * chunk)
-                entering = edge(seg_col[r], marks[m], table[h], offset + 1.0)
+                entering = edge(seg_col[r], weigh.before[m], decay_rate[h], offset + 1.0)
                 left = (q[r, at].astype(F32) * entering).astype(BF16)
                 states[h, m] = kdot(left, ob[r, at], ((0,), (0,))).astype(BF16)
 
         scan.start()
 
-    def turn_back(grad, pre):
+    def slope(pre):
+        sig = lax.logistic(pre)
+        return sig * (1.0 + pre * (1.0 - sig))
+
+    def turned_back(grad, r, base, h):
         grad = grad.astype(BF16).astype(F32)
-        pre = pre.astype(F32)
-        return grad, pre
-
-    def attend(first, last):
+        back = grad * cosine[r, :] - pltpu.roll(grad, DH // 2, 1) * sine[r, :]
+        return (slope(s[r, cols(base + h * DH, DH)].astype(F32)) * back).astype(BF16)
+
+    def attend_queries(first, last):
         @pl.loop(first, last)
         def _(h):
             at = cols(h * DH, DH)
-            decay = decays(table[h], chunk)
+            decay = decays(decay_rate[h], chunk)
             for m in range(2):
                 r = slice(m * chunk, (m + 1) * chunk)
                 within = jnp.where(seg_col[r] == seg_row[m : m + 1], decay, 0.0)
-                entering = edge(seg_col[r], marks[m], table[h], offset + 1.0)
-                leaving = edge(seg_col[r], marks[2 + m], table[h], chunk - 1.0 - offset)
+                entering = edge(seg_col[r], weigh.before[m], decay_rate[h], offset + 1.0)
+                oh = ob[r, at]
+                grads = (kdot(oh, v[r, at], ((1,), (1,))) * within).astype(BF16)
+                dq = kdot(grads, k[r, at]) + entering * kdot(oh, state_in[h, m], ((1,), (1,)))
+                dqp[r, at] = turned_back(dq, r, 0, h)
+
+    def attend_keys(first, last):
+        @pl.loop(first, last)
+        def _(h):
+            at = cols(h * DH, DH)
+            decay = decays(decay_rate[h], chunk)
+            for m in range(2):
+                r = slice(m * chunk, (m + 1) * chunk)
+                within = jnp.where(seg_col[r] == seg_row[m : m + 1], decay, 0.0)
+                leaving = edge(seg_col[r], weigh.last[m], decay_rate[h], chunk - 1.0 - offset)
                 qh, kh, vh, oh = q[r, at], k[r, at], v[r, at], ob[r, at]
-                scores = (kdot(qh, kh, ((1,), (1,))) * within).astype(BF16)
                 grads = (kdot(oh, vh, ((1,), (1,))) * within).astype(BF16)
-                dq = kdot(grads, kh) + entering * kdot(oh, state_in[h, m], ((1,), (1,)))
                 dk = kdot(grads, qh, ((0,), (0,)))
                 dk = dk + leaving * kdot(vh, result[h, m], ((1,), (1,)))
+                scores = (kdot(qh, kh, ((1,), (1,))) * within).astype(BF16)
                 grad_v = kdot(scores, oh, ((0,), (0,))) + leaving * kdot(kh, result[h, m])
                 dv[r, at] = grad_v.astype(BF16)
-                for grad, base, low_out in ((dq, 0, dqp), (dk, width, dkp)):
-                    grad = grad.astype(BF16).astype(F32)
-                    back = grad * cosine[r, :] - pltpu.roll(grad, DH // 2, 1) * sine[r, :]
-                    pre = s[r, cols(base + h * DH, DH)].astype(F32)
-                    sig = lax.logistic(pre)
-                    slope = sig * (1.0 + pre * (1.0 - sig))
-                    low_out[r, at] = (slope * back).astype(BF16)
-
-    def inputs():
-        ready("wq", "wv", "x")
-
-        @pl.loop(0, width // TILE)
+                dkp[r, at] = turned_back(dk, r, width, h)
+
+    def inputs(first, last):
+        @pl.loop(first, last)
         def _(t):
             r = pl.ds(pl.multiple_of(t * TILE, TILE), TILE)
             acc = kdot(dqp[...], w1[r, 0:width], ((1,), (1,)))
@@ -1174,6 +1418,7 @@
             acc += kdot(u[...], w2[r, width : 2 * width], ((1,), (1,)))
             hid[:, cols(t * TILE, TILE)] = acc
 
+    def inputs_rows():
         def body(at):
             value = dy[at, :].astype(F32)
             scale = lax.rsqrt(jnp.mean(value * value, axis=-1, keepdims=True) + EPSILON)
@@ -1186,59 +1431,91 @@
         load("grad_x", dz, grad_x_o)
 
     def work(n):
-        if n == 1:
-            inner()
+        if n == 0:
+            weigh.tables(cosine, sine, seg_col, seg_row)
+            ready("a2t", "p1", "p2")
+        elif n == 1:
+            up()
         elif n == 2:
-            ready("a2t")
-            middle()
+            middle(0, 2)
         elif n == 3:
+            middle(2, 4)
+            ready("hid")
+            middle_rows()
+        elif n == 4:
+            mix()
+            ready("q")
+        elif n == 5:
             load("qp", qp_i, s.at[:, pl.ds(0, width)])
             load("kp", kp_i, s.at[:, pl.ds(width, width)])
             outer()
-        elif n == 4:
+        elif n == 6:
+            ready("k", "v", "state", "qp", "kp", "mixed")
+            attend_queries(0, H // 2)
+        elif n == 7:
             scan.totals_out()
-        elif n == 5:
+            attend_queries(H // 2, H)
+        elif n == 8:
             scan.forward()
-        elif n == 6:
+            ready("gt", "a1t")
+        elif n == 9:
             scan.results_out()
-            ready("gt", "k", "v", "state", "a1t", "qp", "kp")
-        elif n == 7:
+        elif n == 10:
             scan.finish()
-            attend(0, H // 2)
-        elif n == 8:
-            attend(H // 2, H)
+            attend_keys(0, H // 2)
         elif n == 11:
-            inputs()
+            attend_keys(H // 2, H)
+            ready("wq", "wv", "x")
+        elif n == 13:
+            inputs(0, 2)
+        elif n == 14:
+            inputs(2, 4)
+        elif n == 15:
+            inputs_rows()
 
     ready("dyt", "s")
-    for n in range(count + 5):
+    for n in range(max(level[-1] + 6, upright[-1] + 8)):
         if n < count:
             give_half(n)
-        if 0 <= n - 1 < count:
+        if n - 3 in upright:
+            z_halve(n - 3)
+        if n - 1 in range(count):
             merge(n - 1)
-        if 0 <= n - 2 < count:
+        if n - 2 in level:
             halve(n - 2)
-        if 0 <= n - 3 < count:
+        if n - 5 in upright:
+            z_quarter(n - 5)
+        if n - 3 in level:
             quarter(n - 3)
-        if 0 <= n - 4 < count:
+        if n - 6 in upright:
+            z_along(n - 6)
+        if n - 4 in level:
             along(n - 4)
-        if 0 <= n - 5 < count:
+        if n - 7 in upright:
+            z_end(n - 7)
+        if n - 5 in level:
             end(n - 5)
         work(n)
-    for n in (count - 2, count - 1):
-        for t in range(7):
+    sent(count - 2)
+    sent(count - 1)
+    for t in (0, 3, 4, 5, 6):
+        for n in order(t)[-2:]:
             move(n, t).wait_send()
+    for t in range(1, 6):
+        z_move(upright[-1], t).wait_send()
+    for n in level[-2:]:
         final_copy(n).wait()
+    z_copy(upright[-1]).wait()
     ready("grad_x")
 
 
-def run_backward(table, marks, cosine, sine, seg_col, seg_row, x, dy, kept):
+def run_backward(lengths, decay_rate, x, dy, kept):
     rows, width = x.shape
     hidden_size = kept[2].shape[1]
     part = width // 32
     row = jax.ShapeDtypeStruct((rows, width), BF16)
     outs = (
-        [row]
+        [row] * 2
         + [jax.ShapeDtypeStruct((part, width), F32)] * 5
         + [jax.ShapeDtypeStruct((part, hidden_size), F32)] * 3
     )
@@ -1251,116 +1528,103 @@
         [pltpu.VMEM((hidden_size, width), BF16), wv, wv, tv, tv, tv, rv, fv, fv]
         + [rv] * 9
         + [pltpu.VMEM((H, 2, DH, DH), BF16)]
+        + table_scratch(rows)
         + [pltpu.VMEM((width, rows), BF16)] * 4
         + scan_scratch()
         + [
             pltpu.VMEM((2, 512, n), BF16),
             pltpu.VMEM((2, 512, n), BF16),
-            pltpu.VMEM((2, 2, 2, 128, n), BF16),
-            pltpu.VMEM((2, 2, 128, n // 2), BF16),
-            pltpu.VMEM((2, 2, 128, n // 2), BF16),
-            pltpu.VMEM((2, 2, 128, n // 2), BF16),
-            pltpu.VMEM((2, 2, 128, n // 2), BF16),
-            pltpu.VMEM((2, 2, 128, n // 2), BF16),
+            pltpu.VMEM((2, 2, 2, 2, 2, 32, n), BF16),
+            pltpu.VMEM((2, 2, 2, 2, 32, n // 2), BF16),
+            pltpu.VMEM((2, 2, 2, 2, 32, n // 2), BF16),
+            pltpu.VMEM((2, 2, 2, 2, 32, n // 2), BF16),
+            pltpu.VMEM((2, 2, 2, 2, 32, n // 2), BF16),
+            pltpu.VMEM((2, 2, 2, 2, 32, n // 2), BF16),
             pltpu.VMEM((2, 2, 2, 32, n), BF16),
             pltpu.VMEM((2, 2, 32, n), BF16),
             pltpu.VMEM((2, 2, 32, n), BF16),
             pltpu.VMEM((2, 32, n), BF16),
             pltpu.VMEM((2, 32, n), F32),
+            pltpu.VMEM((2, 2, 2, 32, n), BF16),
+            pltpu.VMEM((2, 2, 2, 32, n), BF16),
+            pltpu.VMEM((2, 2, 32, n), BF16),
+            pltpu.VMEM((2, 2, 32, n), BF16),
+            pltpu.VMEM((2, 32, n // 2), BF16),
+            pltpu.VMEM((2, 32, n // 2), BF16),
+            pltpu.VMEM((2, 32, n // 2), BF16),
+            pltpu.VMEM((2, 32, n // 2), BF16),
+            pltpu.VMEM((2, 32, n // 2), BF16),
+            pltpu.VMEM((32, n), F32),
         ]
         + [pltpu.SemaphoreType.DMA((14,))] * 2
-        + [pltpu.SemaphoreType.REGULAR((7,)), pltpu.SemaphoreType.DMA((26,))]
-        + [pltpu.SemaphoreType.DMA((2,))]
+        + [pltpu.SemaphoreType.REGULAR((7,))]
+        + [pltpu.SemaphoreType.DMA((6,))] * 2
+        + [pltpu.SemaphoreType.REGULAR((6,))]
+        + [pltpu.SemaphoreType.DMA((28,)), pltpu.SemaphoreType.DMA((3,))]
         + [pltpu.SemaphoreType.DMA((13,))] * 2
     )
     return pl.pallas_call(
         backward_kernel,
         out_shape=outs,
-        in_specs=[SMEM, SMEM] + [VMEM] * 4 + [ANY] * (2 + len(kept)),
+        in_specs=[SMEM, SMEM] + [ANY] * (2 + len(kept)),
         out_specs=[ANY] * len(outs),
         scratch_shapes=scratch,
         compiler_params=pltpu.CompilerParams(
             collective_id=1, has_side_effects=True, vmem_limit_bytes=VMEM_BYTES
         ),
         name="backward",
-    )(table, marks, cosine, sine, seg_col, seg_row, x, dy, *kept)
-
-
-def factors(ends, rates, chunk, f, nf, nh, backward):
-    mb = ends.shape[0]
-    places = jnp.arange(nh)
-    groups = jnp.arange(nf)
-    at_group = lax.dynamic_slice_in_dim(ends, f * nh, nh, axis=1)
-    before_group = jnp.where(
-        f > 0, lax.dynamic_index_in_dim(ends, jnp.maximum(f * nh - 1, 0), 1, False), 0
-    )
-    before = jnp.concatenate([before_group[:, None], at_group[:, :-1]], axis=1)
-    last = at_group[:, -1]
-    group_last = ends.reshape(mb, nf, nh)[:, :, -1]
-    group_before = jnp.concatenate([jnp.zeros_like(group_last[:, :1]), group_last[:, :-1]], axis=1)
-
-    def factor(same, gap):
-        gap = jnp.maximum(gap, 0)
-        value = jnp.exp(-rates * (chunk * gap).astype(F32)[..., None])
-        return jnp.where(same[..., None], value, 0.0).reshape(-1)
-
-    rise = jnp.broadcast_to(places, (mb, nh))
-    fall = jnp.broadcast_to(nh - 1 - places, (mb, nh))
-    if backward:
-        to_total = factor(before == before_group[:, None], rise)
-        group_same = (last[:, None] == group_before) & (groups > f)
-        group_gap = jnp.broadcast_to((groups - 1 - f) * nh, (mb, nf))
-        to_place = factor(at_group == last[:, None], fall)
-        same = (at_group[:, :, None] == before[:, None, :]) & (places[None, :] > places[:, None])
-        gap = jnp.broadcast_to(places[None, :] - 1 - places[:, None], (mb, nh, nh))
-    else:
-        to_total = factor(at_group == last[:, None], fall)
-        group_same = (before_group[:, None] == group_last) & (groups < f)
-        group_gap = jnp.broadcast_to((f - 1 - groups) * nh, (mb, nf))
-        to_place = factor(before == before_group[:, None], rise)
-        same = (before[:, :, None] == at_group[:, None, :]) & (places[None, :] < places[:, None])
-        gap = jnp.broadcast_to(places[:, None] - 1 - places[None, :], (mb, nh, nh))
-    return jnp.concatenate([to_total, factor(group_same, group_gap), to_place, factor(same, gap)])
+    )(lengths, decay_rate, x, dy, *kept)
+
+
+def hand_over_kernel(*refs):
+    count = (len(refs) - 3) // 3
+    sources, targets, held = (refs[i * count : (i + 1) * count] for i in range(3))
+    turned, sems_in, sems_out = refs[3 * count :]
+    fetches = [
+        pltpu.make_async_copy(src, dst, sems_in.at[i])
+        for i, (src, dst) in enumerate(zip(sources, held))
+    ]
+    for fetch in fetches:
+        fetch.start()
+    stores = []
+    for i in reversed(range(count)):
+        fetches[i].wait()
+        src = held[i]
+        if i == count - 1:
+            for b in range(src.shape[1] // 128):
+                at = slice(b * 128, (b + 1) * 128)
+                turned[at, :] = src[:, at].T
+            src = turned
+        store = pltpu.make_async_copy(src, targets[i], sems_out.at[i])
+        store.start()
+        stores.append(store)
+    for store in stores:
+        store.wait()
+
+
+def hand_over(arrays):
+    outs = [jax.ShapeDtypeStruct(a.shape, a.dtype) for a in arrays]
+    last = arrays[-1]
+    outs[-1] = jax.ShapeDtypeStruct(last.shape[::-1], last.dtype)
+    return pl.pallas_call(
+        hand_over_kernel,
+        out_shape=outs,
+        in_specs=[ANY] * len(arrays),
+        out_specs=[ANY] * len(arrays),
+        scratch_shapes=[pltpu.VMEM(a.shape, a.dtype) for a in arrays]
+        + [pltpu.VMEM(last.shape[::-1], last.dtype)]
+        + [pltpu.SemaphoreType.DMA((len(arrays),))] * 2,
+        name="hand_over",
+    )(*arrays)
 
 
 def local_fast(tokens, cotangent, lengths, decay_rate, *weights):
-    wires = Wires()
     mb, chunk, width = tokens.shape
-    rows = mb * chunk
-    nf, nh = wires.nf, wires.nh
-    place = wires.f * nh + wires.h
-    positions = place * chunk + jnp.arange(chunk, dtype=jnp.int32)
-    cosine, sine_vals = rotation_tables(positions, DH)
-    cosine, sine_vals = cosine[:, 0], sine_vals[:, 0]
-    cos_table = jnp.tile(cosine, (mb, 2))
-    sin_table = jnp.tile(jnp.concatenate([-sine_vals, sine_vals], axis=1), (mb, 1))
-    seq_ends = jnp.cumsum(lengths, axis=1)
-    segs = jnp.sum((seq_ends[:, None, :] <= positions[None, :, None]).astype(jnp.int32), axis=2)
-    chunk_ends = (jnp.arange(nf * nh, dtype=jnp.int32) + 1) * chunk - 1
-    ends = jnp.sum((seq_ends[:, None, :] <= chunk_ends[None, :, None]).astype(jnp.int32), axis=2)
-    last = lax.dynamic_index_in_dim(ends, place, 1, False)
-    before = jnp.where(
-        place > 0, lax.dynamic_index_in_dim(ends, jnp.maximum(place - 1, 0), 1, False), 0
-    )
-    marks = jnp.concatenate([before, last])
-    mine = H // nh
-    rates = lax.dynamic_slice_in_dim(decay_rate, wires.h * mine, mine)
-    table = jnp.concatenate([decay_rate, factors(ends, rates, chunk, wires.f, nf, nh, False)])
-    back_table = jnp.concatenate([decay_rate, factors(ends, rates, chunk, wires.f, nf, nh, True)])
-    x = tokens.reshape(rows, width)
-    dy = cotangent.reshape(rows, width)
-    seg_col = segs.reshape(rows, 1)
-    around = (marks, cos_table, sin_table, seg_col, segs)
-    outs = run_forward(table, marks, x, dy, *around[1:], weights)
-    mixed = outs[17]
-    kept = outs[:17] + outs[18:]
-    grads = run_backward(back_table, *around, x, dy, kept)
-    return (
-        mixed.reshape(mb, chunk, width),
-        grads[0].reshape(mb, chunk, width),
-        *grads[1:8],
-        grads[8].T,
-    )
+    x = tokens.reshape(mb * chunk, width)
+    dy = cotangent.reshape(mb * chunk, width)
+    kept = run_forward(lengths, decay_rate, x, dy, weights)
+    mixed, grad_x, *grads = hand_over(run_backward(lengths, decay_rate, x, dy, kept))
+    return (mixed.reshape(tokens.shape), grad_x.reshape(tokens.shape), *grads)
 
 
 def solution(mesh):

time: 315 us -> 270 us (0.86)
  Pallas kernels: 293 us -> 266 us
  local copies, waits for them, and re-layouts: 16.5 us -> 2.51 us
  other arithmetic: 3.73 us -> 0 us
    pallas_call x1, Pallas kernels: 139 us -> 114 us  [run_forward(): pl.pallas_call(forward_kernel, out_shape=outs, in_specs=[SMEM, SMEM] + [V...]
    unnamed x31 -> x1, local copies, waits for them, and re-layouts: 11.1 us -> 2.51 us
    pallas_call x1, Pallas kernels: 154 us -> 147 us  [run_backward(): pl.pallas_call(backward_kernel, out_shape=outs, in_specs=[SMEM, SMEM] + [...]
    pallas_call x0 -> x1, Pallas kernels: none -> 4.89 us  [hand_over(): pl.pallas_call(hand_over_kernel, out_shape=outs, in_specs=[ANY] * len(arr...]
where the time goes in v4:
time: 270 us; the launch traced here: 269 us
  Pallas kernels  266 us (99%)
    pallas_call x1, Pallas kernels, run_backward(): pl.pallas_call(backward_kernel, out_shape=outs, in_specs=[SMEM, SMEM] + [...  147 us
    pallas_call x1, Pallas kernels, run_forward(): pl.pallas_call(forward_kernel, out_shape=outs, in_specs=[SMEM, SMEM] + [V...  114 us

profile of v4, /device:TPU:0, one launch (start us, length us, event | category | flops | bytes accessed | tf_op | source)
XLA Modules:
  0.0 269.5 jit_solution(8008944313032424099)
XLA Ops:
  0.6 114.0 %forward.1 = (bf16[1024,4096]{1,0:T(8,128)(2,1)}, bf16[1024,1024]{1,0:T(8,128)(2,1)}, bf16[1024,2816]{1,0:T(8,128)(2,1)}, bf16[1024,2816]{1,0:T(8,128)(2,1)}, bf...) custom-call(s32[2,8]{1,0:T(2,128)} %lengths.3, ...), custom_call_target="tpu_custom_call" | custom-call | tf_op jit(solution)/shard_map/forward/pallas_call | solution.py:955
  114.6 147.4 %backward.1 = (bf16[512,1024]{1,0:T(8,128)(2,1)}, bf16[512,1024]{1,0:T(8,128)(2,1)}, f32[32,1024]{1,0:T(8,128)}, f32[32,1024]{1,0:T(8,128)}, f32[32,1024]{1,0:T(...) custom-call(s32[2,8]{1,0:T(2,128)} %lengths.3, ...), custom_call_target="tpu_custom_call" | custom-call | tf_op jit(solution)/shard_map/backward/pallas_call | solution.py:1566
  262.1 4.9 %hand_over.1 = (bf16[512,1024]{1,0:T(8,128)(2,1)}, bf16[512,1024]{1,0:T(8,128)(2,1)}, f32[32,1024]{1,0:T(8,128)}, f32[32,1024]{1,0:T(8,128)}, f32[32,1024]{1,0:T...) custom-call(bf16[512,1024]{1,0:T(8,128)(2,1)} %get-tuple-element.74., ...), custom_call_target="tpu_custom_call" | custom-call | tf_op jit(solution)/shard_map/hand_over/pallas_call | solution.py:1609
  267.0 2.5 copy.22

commit v5 on v4

--- a/solution.py
+++ b/solution.py
@@ -984,7 +984,9 @@
     ]
 
 
-Z_FIRST = (10,)
+UPRIGHT = 256
+LAG = 2
+WITH_UPRIGHT = (0, 1, 2, 3, 10, 11, 12, 13)
 LAST = 1024
 
 
@@ -996,8 +998,8 @@
     wd, w1, w2, s, p1, p2, dy, hid, dh, dz, ob, u, q, k, v, dqp, dkp, dv, state_in,
     cosine, sine, seg_col, seg_row, a1t, a2t, gt, dyt, states, inbox, totals, outbox, result,
     give, take, merged, take_a, take_b, half_a, half_b, take2, mine, take3, pair, take4, final,
-    z_take, z_sum, z_take2, z_sum2, z_take_a, z_take_b, z_half_a, z_half_b, z_take3, z_final,
-    send, recv, free, z_send, z_recv, z_free, load_sem, out_sem, scan_send, scan_recv,
+    z_take, z_sum, z_take2, z_sum2, z_take_a, z_take_b, z_half_a, z_half_b, z_take3,
+    send, recv, free, load_sem, out_sem, scan_send, scan_recv,
 ):
     place = Place()
     rows, width = dy.shape
@@ -1035,94 +1037,76 @@
     for start in range(0, width, LAST):
         pieces.append((a1t, dv, gv_o, start, LAST))
     count = len(pieces)
-    level = [n for n in range(count) if n not in Z_FIRST]
-    upright = [n for n in range(count) if n in Z_FIRST]
+    steps = count + 1 + 4 * LAG
     low, high = place.z % 2, place.z // 2
     f = place.f
     at_c, at_x, at_y = (place.at(f=o) for o in (place.fc, place.fx, place.fy))
     at_z1, at_z2 = (place.at(z=place.zs[i]) for i in range(2))
     partner = [at_c, at_x, at_y, at_y, at_x, at_z1, at_z2]
-    z_partner = [at_z1, at_z2, at_x, at_y, at_y, at_x]
-
-    def turn(n, t):
-        return n if t == 0 else level.index(n)
+    partner += [at_z1, at_z2, at_x, at_y, at_y, at_x]
+    quarter_size = UPRIGHT // 2
+    lo, hi = pl.ds(0, quarter_size), pl.ds(quarter_size, quarter_size)
+
+    def upright(n):
+        return n in WITH_UPRIGHT
+
+    def half_of(n):
+        return (pieces[n][4] - UPRIGHT * upright(n)) // 2
+
+    def of(n, *which):
+        return [t for t in which if t < 7 or upright(n)]
 
     def move(n, t):
         size = pieces[n][4]
-        m, slot, half = n % 2, turn(n, t) % 2, size // 2
-        a, b, whole = pl.ds(0, half), pl.ds(half, half), pl.ds(0, size)
+        c, m, half = n % 2, n % 3, half_of(n)
+        a, b, ab, last = (pl.ds(*at) for at in ((0, half), (half, half), (0, 2 * half), (2 * half, UPRIGHT)))
         src, dst = [
-            lambda: (give.at[slot, :, whole], take.at[slot, :, whole]),
-            lambda: (merged.at[m, :, 1, :, :, :, a], take_a.at[slot, :, :, :, :, a]),
-            lambda: (merged.at[m, 1, :, :, :, :, b], take_b.at[slot, :, :, :, :, a]),
-            lambda: (half_a.at[slot, 1, :, :, :, a], take2.at[slot, 0, :, :, :, a]),
-            lambda: (half_b.at[slot, 1, :, :, :, a], take2.at[slot, 1, :, :, :, a]),
-            lambda: (mine.at[slot, :, 1 - low, :, whole], take3.at[slot, :, :, whole]),
-            lambda: (pair.at[slot, 1 - high, :, whole], take4.at[slot, :, whole]),
+            lambda: (give.at[c, :, pl.ds(0, size)], take.at[c, :, pl.ds(0, size)]),
+            lambda: (merged.at[m, :, 1, :, :, :, a], take_a.at[m, :, :, :, :, a]),
+            lambda: (merged.at[m, 1, :, :, :, :, b], take_b.at[m, :, :, :, :, a]),
+            lambda: (half_a.at[m, 1, :, :, :, a], take2.at[m, 0, :, :, :, a]),
+            lambda: (half_b.at[m, 1, :, :, :, a], take2.at[m, 1, :, :, :, a]),
+            lambda: (mine.at[m, :, 1 - low, :, ab], take3.at[m, :, :, ab]),
+            lambda: (pair.at[m, 1 - high, :, ab], take4.at[m, :, ab]),
+            lambda: (merged.at[m, :, :, :, 1 - low, :, last], z_take.at[m]),
+            lambda: (z_sum.at[m, :, :, 1 - high], z_take2.at[m]),
+            lambda: (z_sum2.at[m, :, 1, :, lo], z_take_a.at[m]),
+            lambda: (z_sum2.at[m, 1, :, :, hi], z_take_b.at[m]),
+            lambda: (z_half_a.at[m, 1], z_take3.at[m, 0]),
+            lambda: (z_half_b.at[m, 1], z_take3.at[m, 1]),
         ][t]()
         return pltpu.make_async_remote_copy(
             src_ref=src,
             dst_ref=dst,
-            send_sem=send.at[2 * t + slot],
-            recv_sem=recv.at[2 * t + slot],
+            send_sem=send.at[3 * t + m],
+            recv_sem=recv.at[3 * t + m],
             device_id=partner[t],
             device_id_type=MESH,
         )
 
-    def z_move(n, t):
-        size = pieces[n][4]
-        half = size // 2
-        a, b, whole = pl.ds(0, half), pl.ds(half, half), pl.ds(0, size)
-        src, dst = [
-            lambda: (merged.at[n % 2, :, :, :, 1 - low, :, whole], z_take.at[:, :, :, :, whole]),
-            lambda: (z_sum.at[:, :, 1 - high, :, whole], z_take2.at[:, :, :, whole]),
-            lambda: (z_sum2.at[:, 1, :, a], z_take_a.at[:, :, a]),
-            lambda: (z_sum2.at[1, :, :, b], z_take_b.at[:, :, a]),
-            lambda: (z_half_a.at[1, :, a], z_take3.at[0, :, a]),
-            lambda: (z_half_b.at[1, :, a], z_take3.at[1, :, a]),
-        ][t]()
-        return pltpu.make_async_remote_copy(
-            src_ref=src,
-            dst_ref=dst,
-            send_sem=z_send.at[t],
-            recv_sem=z_recv.at[t],
-            device_id=z_partner[t],
-            device_id_type=MESH,
-        )
-
-    def order(t):
-        return list(range(count)) if t == 0 else level
-
     def go(n, t):
-        if turn(n, t) >= 2:
-            pl.semaphore_wait(free.at[t], 1)
         move(n, t).start()
 
-    def reuse(n, t):
-        i = turn(n, t)
-        if i >= 2:
-            move(order(t)[i - 2], t).wait_send()
+    def reuse(n, *which):
+        for t in which:
+            earlier = n - (2 if t == 0 else 3)
+            if earlier >= 0 and of(earlier, t):
+                move(earlier, t).wait_send()
 
     def got(n, t):
         move(n, t).wait_recv()
 
-    def used(n, t):
-        if turn(n, t) + 2 < len(order(t)):
-            pl.semaphore_signal(free.at[t], 1, device_id=partner[t], device_id_type=MESH)
-
-    def z_go(n, t):
-        if n != upright[0]:
-            pl.semaphore_wait(z_free.at[t], 1)
-        z_move(n, t).start()
-
-    def z_reuse(n, t):
-        i = upright.index(n)
-        if i >= 1:
-            z_move(upright[i - 1], t).wait_send()
-
-    def z_used(n, t):
-        if n != upright[-1]:
-            pl.semaphore_signal(z_free.at[t], 1, device_id=z_partner[t], device_id_type=MESH)
+    near = (at_c, at_x, at_y, at_z1, at_z2)
+
+    def freed(n):
+        if n < steps - 1:
+            for i, where in enumerate(near):
+                pl.semaphore_signal(free.at[i], 1, device_id=where, device_id_type=MESH)
+
+    def allowed(n):
+        if n >= 1:
+            for i in range(len(near)):
+                pl.semaphore_wait(free.at[i], 1)
 
     def give_half(n):
         left, right, _, start, size = pieces[n]
@@ -1134,21 +1118,12 @@
             value = kdot(left[rows : 2 * rows, :], right[:, cols(start + t * TILE, TILE)])
             give[slot, :, cols(t * TILE, TILE)] = value.astype(BF16)
 
-        go(n, 0)
-
-    def sent(n):
-        if n in level:
-            move(n, 1).wait_send()
-            move(n, 2).wait_send()
-        else:
-            z_move(n, 0).wait_send()
 
     def merge(n):
         left, right, _, start, size = pieces[n]
-        slot = n % 2
+        slot, m = n % 2, n % 3
         got(n, 0)
-        if n >= 2:
-            sent(n - 2)
+        reuse(n, 1, 2, 7)
 
         @pl.loop(0, size // TILE)
         def _(t):
@@ -1157,131 +1132,91 @@
             value = (value + take[slot, :, at].astype(F32)).astype(BF16)
             for i in range(16):
                 r = i * 32
-                merged[slot, i // 8, i // 4 % 2, i // 2 % 2, i % 2, :, at] = value[r : r + 32]
-
-        used(n, 0)
-        if n in level:
-            go(n, 1)
-            go(n, 2)
-        else:
-            z_go(n, 0)
+                merged[m, i // 8, i // 4 % 2, i // 2 % 2, i % 2, :, at] = value[r : r + 32]
+
+        for t in of(n, 1, 2, 7):
+            go(n, t)
 
     def add(a, b):
         return a.astype(F32) + b.astype(F32)
 
     def halve(n):
-        size = pieces[n][4]
-        m, slot, half = n % 2, turn(n, 1) % 2, size // 2
+        m, half = n % 3, half_of(n)
+        reuse(n, 8)
+        if upright(n):
+            got(n, 7)
+            c = slice(2 * half, 2 * half + UPRIGHT)
+            for y in range(2):
+                z_sum[m, y] = add(merged[m, y, :, :, low, :, c], z_take[m, y]).astype(BF16)
+            go(n, 8)
         got(n, 1)
         reuse(n, 3)
         for i in (1, 0):
-            half_a[slot, i, :, :, :, :half] = add(
-                merged[m, i, 0, :, :, :, :half], take_a[slot, i, :, :, :, :half]
+            half_a[m, i, :, :, :, :half] = add(
+                merged[m, i, 0, :, :, :, :half], take_a[m, i, :, :, :, :half]
             ).astype(BF16)
-        used(n, 1)
         go(n, 3)
         got(n, 2)
         reuse(n, 4)
         for i in (1, 0):
-            half_b[slot, i, :, :, :, :half] = add(
-                merged[m, 0, i, :, :, :, half:size], take_b[slot, i, :, :, :, :half]
+            half_b[m, i, :, :, :, :half] = add(
+                merged[m, 0, i, :, :, :, half : 2 * half], take_b[m, i, :, :, :, :half]
             ).astype(BF16)
-        used(n, 2)
         go(n, 4)
 
     def quarter(n):
-        size = pieces[n][4]
-        slot, half = turn(n, 1) % 2, size // 2
+        m, half = n % 3, half_of(n)
+        reuse(n, 9, 10)
+        if upright(n):
+            got(n, 8)
+            z_sum2[m] = add(z_sum[m, :, :, high], z_take2[m]).astype(BF16)
+            go(n, 9)
+            go(n, 10)
         reuse(n, 5)
-        for t, kept, at in ((3, half_a, slice(0, half)), (4, half_b, slice(half, size))):
+        for t, kept, at in ((3, half_a, slice(0, half)), (4, half_b, slice(half, 2 * half))):
             got(n, t)
-            mine[slot, :, :, :, at] = add(
-                kept[slot, 0, :, :, :, :half], take2[slot, t - 3, :, :, :, :half]
+            mine[m, :, :, :, at] = add(
+                kept[m, 0, :, :, :, :half], take2[m, t - 3, :, :, :, :half]
             ).astype(BF16)
-            used(n, t)
         go(n, 5)
 
     def along(n):
-        size = pieces[n][4]
-        slot = turn(n, 1) % 2
+        m, whole = n % 3, 2 * half_of(n)
+        reuse(n, 11, 12)
+        if upright(n):
+            got(n, 9)
+            z_half_a[m] = add(z_sum2[m, :, 0, :, :quarter_size], z_take_a[m]).astype(BF16)
+            go(n, 11)
+            got(n, 10)
+            z_half_b[m] = add(z_sum2[m, 0, :, :, quarter_size:], z_take_b[m]).astype(BF16)
+            go(n, 12)
         got(n, 5)
         reuse(n, 6)
         for i in range(2):
-            pair[slot, i, :, :size] = add(
-                mine[slot, i, low, :, :size], take3[slot, i, :, :size]
+            pair[m, i, :, :whole] = add(
+                mine[m, i, low, :, :whole], take3[m, i, :, :whole]
             ).astype(BF16)
-        used(n, 5)
         go(n, 6)
 
-    def result_copy(n, src, sem):
+    def final_copy(n):
         _, _, out, start, size = pieces[n]
-        return pltpu.make_async_copy(src.at[:, pl.ds(0, size)], out.at[:, pl.ds(start, size)], sem)
-
-    def final_copy(n):
-        slot = turn(n, 1) % 2
-        return result_copy(n, final.at[slot], out_sem.at[slot])
+        m = n % 3
+        return pltpu.make_async_copy(
+            final.at[m, :, pl.ds(0, size)], out.at[:, pl.ds(start, size)], out_sem.at[m]
+        )
 
     def end(n):
-        size = pieces[n][4]
-        i = turn(n, 1)
-        slot = i % 2
+        m, whole = n % 3, 2 * half_of(n)
+        if n >= 3:
+            final_copy(n - 3).wait()
+        for t in of(n, 11, 12):
+            i, kept = t - 11, (z_half_a, z_half_b)[t - 11]
+            got(n, t)
+            at = slice(whole + i * quarter_size, whole + (i + 1) * quarter_size)
+            final[m, :, at] = add(kept[m, 0], z_take3[m, i])
         got(n, 6)
-        if i >= 2:
-            final_copy(level[i - 2]).wait()
-        final[slot, :, :size] = add(pair[slot, high, :, :size], take4[slot, :, :size])
-        used(n, 6)
+        final[m, :, :whole] = add(pair[m, high, :, :whole], take4[m, :, :whole])
         final_copy(n).start()
-
-    def z_halve(n):
-        size = pieces[n][4]
-        z_move(n, 0).wait_recv()
-        z_reuse(n, 1)
-        for y in range(2):
-            z_sum[y, :, :, :, :size] = add(
-                merged[n % 2, y, :, :, low, :, :size], z_take[y, :, :, :, :size]
-            ).astype(BF16)
-        z_used(n, 0)
-        z_go(n, 1)
-
-    def z_quarter(n):
-        size = pieces[n][4]
-        z_move(n, 1).wait_recv()
-        z_reuse(n, 2)
-        z_reuse(n, 3)
-        z_sum2[:, :, :, :size] = add(
-            z_sum[:, :, high, :, :size], z_take2[:, :, :, :size]
-        ).astype(BF16)
-        z_used(n, 1)
-        z_go(n, 2)
-        z_go(n, 3)
-
-    def z_along(n):
-        size = pieces[n][4]
-        half = size // 2
-        z_move(n, 2).wait_recv()
-        z_reuse(n, 4)
-        z_half_a[:, :, :half] = add(z_sum2[:, 0, :, :half], z_take_a[:, :, :half]).astype(BF16)
-        z_used(n, 2)
-        z_go(n, 4)
-        z_move(n, 3).wait_recv()
-        z_reuse(n, 5)
-        z_half_b[:, :, :half] = add(z_sum2[0, :, :, half:size], z_take_b[:, :, :half]).astype(BF16)
-        z_used(n, 3)
-        z_go(n, 5)
-
-    def z_copy(n):
-        return result_copy(n, z_final, out_sem.at[2])
-
-    def z_end(n):
-        size = pieces[n][4]
-        half = size // 2
-        if n != upright[0]:
-            z_copy(upright[upright.index(n) - 1]).wait()
-        for t, kept, at in ((4, z_half_a, slice(0, half)), (5, z_half_b, slice(half, size))):
-            z_move(n, t).wait_recv()
-            z_final[:, at] = add(kept[0, :, :half], z_take3[t - 4, :, :half])
-            z_used(n, t)
-        z_copy(n).start()
 
     offset = lax.broadcasted_iota(jnp.int32, (chunk, 1), 0).astype(F32)
     weigh = Weigh(place, lengths, decay_rate, chunk, True)
@@ -1453,17 +1388,16 @@
             ready("k", "v", "state", "qp", "kp", "mixed")
             attend_queries(0, H // 2)
         elif n == 7:
+            attend_queries(H // 2, H)
             scan.totals_out()
-            attend_queries(H // 2, H)
         elif n == 8:
-            scan.forward()
             ready("gt", "a1t")
         elif n == 9:
+            scan.forward()
             scan.results_out()
-        elif n == 10:
+        elif n == 11:
             scan.finish()
             attend_keys(0, H // 2)
-        elif n == 11:
             attend_keys(H // 2, H)
             ready("wq", "wv", "x")
         elif n == 13:
@@ -1474,38 +1408,29 @@
             inputs_rows()
 
     ready("dyt", "s")
-    for n in range(max(level[-1] + 6, upright[-1] + 8)):
+    for n in range(steps):
         if n < count:
             give_half(n)
-        if n - 3 in upright:
-            z_halve(n - 3)
-        if n - 1 in range(count):
+        allowed(n)
+        if n < count:
+            go(n, 0)
+        if 0 <= n - 1 < count:
             merge(n - 1)
-        if n - 2 in level:
-            halve(n - 2)
-        if n - 5 in upright:
-            z_quarter(n - 5)
-        if n - 3 in level:
-            quarter(n - 3)
-        if n - 6 in upright:
-            z_along(n - 6)
-        if n - 4 in level:
-            along(n - 4)
-        if n - 7 in upright:
-            z_end(n - 7)
-        if n - 5 in level:
-            end(n - 5)
+        if n - 1 - 1 * LAG in range(count):
+            halve(n - 1 - 1 * LAG)
+        if n - 1 - 2 * LAG in range(count):
+            quarter(n - 1 - 2 * LAG)
+        if n - 1 - 3 * LAG in range(count):
+            along(n - 1 - 3 * LAG)
+        if n - 1 - 4 * LAG in range(count):
+            end(n - 1 - 4 * LAG)
+        freed(n)
         work(n)
-    sent(count - 2)
-    sent(count - 1)
-    for t in (0, 3, 4, 5, 6):
-        for n in order(t)[-2:]:
-            move(n, t).wait_send()
-    for t in range(1, 6):
-        z_move(upright[-1], t).wait_send()
-    for n in level[-2:]:
+    for n in range(count - 3, count):
+        for t in range(13):
+            if of(n, t) and (t > 0 or n > count - 3):
+                move(n, t).wait_send()
         final_copy(n).wait()
-    z_copy(upright[-1]).wait()
     ready("grad_x")
 
 
@@ -1524,6 +1449,7 @@
     tv = pltpu.VMEM((rows, hidden_size), BF16)
     wv = pltpu.VMEM((width, hidden_size), BF16)
     n = 1024
+    h = n // 2
     scratch = (
         [pltpu.VMEM((hidden_size, width), BF16), wv, wv, tv, tv, tv, rv, fv, fv]
         + [rv] * 9
@@ -1534,32 +1460,29 @@
         + [
             pltpu.VMEM((2, 512, n), BF16),
             pltpu.VMEM((2, 512, n), BF16),
-            pltpu.VMEM((2, 2, 2, 2, 2, 32, n), BF16),
-            pltpu.VMEM((2, 2, 2, 2, 32, n // 2), BF16),
-            pltpu.VMEM((2, 2, 2, 2, 32, n // 2), BF16),
-            pltpu.VMEM((2, 2, 2, 2, 32, n // 2), BF16),
-            pltpu.VMEM((2, 2, 2, 2, 32, n // 2), BF16),
-            pltpu.VMEM((2, 2, 2, 2, 32, n // 2), BF16),
-            pltpu.VMEM((2, 2, 2, 32, n), BF16),
-            pltpu.VMEM((2, 2, 32, n), BF16),
-            pltpu.VMEM((2, 2, 32, n), BF16),
-            pltpu.VMEM((2, 32, n), BF16),
-            pltpu.VMEM((2, 32, n), F32),
-            pltpu.VMEM((2, 2, 2, 32, n), BF16),
-            pltpu.VMEM((2, 2, 2, 32, n), BF16),
-            pltpu.VMEM((2, 2, 32, n), BF16),
-            pltpu.VMEM((2, 2, 32, n), BF16),
-            pltpu.VMEM((2, 32, n // 2), BF16),
-            pltpu.VMEM((2, 32, n // 2), BF16),
-            pltpu.VMEM((2, 32, n // 2), BF16),
-            pltpu.VMEM((2, 32, n // 2), BF16),
-            pltpu.VMEM((2, 32, n // 2), BF16),
-            pltpu.VMEM((32, n), F32),
+            pltpu.VMEM((3, 2, 2, 2, 2, 32, n), BF16),
+            pltpu.VMEM((3, 2, 2, 2, 32, h), BF16),
+            pltpu.VMEM((3, 2, 2, 2, 32, h), BF16),
+            pltpu.VMEM((3, 2, 2, 2, 32, h), BF16),
+            pltpu.VMEM((3, 2, 2, 2, 32, h), BF16),
+            pltpu.VMEM((3, 2, 2, 2, 32, h), BF16),
+            pltpu.VMEM((3, 2, 2, 32, 2 * h), BF16),
+            pltpu.VMEM((3, 2, 32, 2 * h), BF16),
+            pltpu.VMEM((3, 2, 32, 2 * h), BF16),
+            pltpu.VMEM((3, 32, 2 * h), BF16),
+            pltpu.VMEM((3, 32, n), F32),
+            pltpu.VMEM((3, 2, 2, 2, 32, UPRIGHT), BF16),
+            pltpu.VMEM((3, 2, 2, 2, 32, UPRIGHT), BF16),
+            pltpu.VMEM((3, 2, 2, 32, UPRIGHT), BF16),
+            pltpu.VMEM((3, 2, 2, 32, UPRIGHT), BF16),
+            pltpu.VMEM((3, 2, 32, UPRIGHT // 2), BF16),
+            pltpu.VMEM((3, 2, 32, UPRIGHT // 2), BF16),
+            pltpu.VMEM((3, 2, 32, UPRIGHT // 2), BF16),
+            pltpu.VMEM((3, 2, 32, UPRIGHT // 2), BF16),
+            pltpu.VMEM((3, 2, 32, UPRIGHT // 2), BF16),
         ]
-        + [pltpu.SemaphoreType.DMA((14,))] * 2
-        + [pltpu.SemaphoreType.REGULAR((7,))]
-        + [pltpu.SemaphoreType.DMA((6,))] * 2
-        + [pltpu.SemaphoreType.REGULAR((6,))]
+        + [pltpu.SemaphoreType.DMA((39,))] * 2
+        + [pltpu.SemaphoreType.REGULAR((5,))]
         + [pltpu.SemaphoreType.DMA((28,)), pltpu.SemaphoreType.DMA((3,))]
         + [pltpu.SemaphoreType.DMA((13,))] * 2
     )
@@ -1577,9 +1500,9 @@
 
 
 def hand_over_kernel(*refs):
-    count = (len(refs) - 3) // 3
+    count = (len(refs) - 2) // 3
     sources, targets, held = (refs[i * count : (i + 1) * count] for i in range(3))
-    turned, sems_in, sems_out = refs[3 * count :]
+    sems_in, sems_out = refs[3 * count :]
     fetches = [
         pltpu.make_async_copy(src, dst, sems_in.at[i])
         for i, (src, dst) in enumerate(zip(sources, held))
@@ -1587,15 +1510,9 @@
     for fetch in fetches:
         fetch.start()
     stores = []
-    for i in reversed(range(count)):
+    for i in range(count):
         fetches[i].wait()
-        src = held[i]
-        if i == count - 1:
-            for b in range(src.shape[1] // 128):
-                at = slice(b * 128, (b + 1) * 128)
-                turned[at, :] = src[:, at].T
-            src = turned
-        store = pltpu.make_async_copy(src, targets[i], sems_out.at[i])
+        store = pltpu.make_async_copy(held[i], targets[i], sems_out.at[i])
         store.start()
         stores.append(store)
     for store in stores:
@@ -1603,16 +1520,12 @@
 
 
 def hand_over(arrays):
-    outs = [jax.ShapeDtypeStruct(a.shape, a.dtype) for a in arrays]
-    last = arrays[-1]
-    outs[-1] = jax.ShapeDtypeStruct(last.shape[::-1], last.dtype)
     return pl.pallas_call(
         hand_over_kernel,
-        out_shape=outs,
+        out_shape=[jax.ShapeDtypeStruct(a.shape, a.dtype) for a in arrays],
         in_specs=[ANY] * len(arrays),
         out_specs=[ANY] * len(arrays),
         scratch_shapes=[pltpu.VMEM(a.shape, a.dtype) for a in arrays]
-        + [pltpu.VMEM(last.shape[::-1], last.dtype)]
         + [pltpu.SemaphoreType.DMA((len(arrays),))] * 2,
         name="hand_over",
     )(*arrays)
@@ -1624,7 +1537,7 @@
     dy = cotangent.reshape(mb * chunk, width)
     kept = run_forward(lengths, decay_rate, x, dy, weights)
     mixed, grad_x, *grads = hand_over(run_backward(lengths, decay_rate, x, dy, kept))
-    return (mixed.reshape(tokens.shape), grad_x.reshape(tokens.shape), *grads)
+    return (mixed.reshape(tokens.shape), grad_x.reshape(tokens.shape), *grads[:-1], grads[-1].T)
 
 
 def solution(mesh):

time: 270 us -> 258 us (0.956)
  Pallas kernels: 266 us -> 257 us
    pallas_call x1, Pallas kernels: 147 us -> 140 us  [run_backward(): pl.pallas_call(backward_kernel, out_shape=outs, in_specs=[SMEM, SMEM] + [...]
where the time goes in v5:
time: 258 us
  Pallas kernels  257 us (100%)
    pallas_call x1, Pallas kernels, run_backward(): pl.pallas_call(backward_kernel, out_shape=outs, in_specs=[SMEM, SMEM] + [...  140 us
    pallas_call x1, Pallas kernels, run_forward(): pl.pallas_call(forward_kernel, out_shape=outs, in_specs=[SMEM, SMEM] + [V...  114 us

profile of v5, /device:TPU:0, one launch (start us, length us, event | category | flops | bytes accessed | tf_op | source)
XLA Modules:
  0.0 258.1 jit_solution(10973960634824852441)
XLA Ops:
  0.6 114.0 %forward.1 = (bf16[1024,4096]{1,0:T(8,128)(2,1)}, bf16[1024,1024]{1,0:T(8,128)(2,1)}, bf16[1024,2816]{1,0:T(8,128)(2,1)}, bf16[1024,2816]{1,0:T(8,128)(2,1)}, bf...) custom-call(s32[2,8]{1,0:T(2,128)} %lengths.3, ...), custom_call_target="tpu_custom_call" | custom-call | tf_op jit(solution)/shard_map/forward/pallas_call | solution.py:955
  114.6 139.9 %backward.1 = (bf16[512,1024]{1,0:T(8,128)(2,1)}, bf16[512,1024]{1,0:T(8,128)(2,1)}, f32[32,1024]{1,0:T(8,128)}, f32[32,1024]{1,0:T(8,128)}, f32[32,1024]{1,0:T(...) custom-call(s32[2,8]{1,0:T(2,128)} %lengths.3, ...), custom_call_target="tpu_custom_call" | custom-call | tf_op jit(solution)/shard_map/backward/pallas_call | solution.py:1489
  254.6 3.3 %hand_over.1 = (bf16[512,1024]{1,0:T(8,128)(2,1)}, bf16[512,1024]{1,0:T(8,128)(2,1)}, f32[32,1024]{1,0:T(8,128)}, f32[32,1024]{1,0:T(8,128)}, f32[32,1024]{1,0:T...) custom-call(bf16[512,1024]{1,0:T(8,128)(2,1)} %get-tuple-element.74., ...), custom_call_target="tpu_custom_call" | custom-call | tf_op jit(solution)/shard_map/hand_over/pallas_call | solution.py:1523

commit v6 on v5

--- a/solution.py
+++ b/solution.py
@@ -627,6 +627,10 @@
         for w, full in ((w1, f1), (w2, f2)):
             at = part * half_hidden
             pieces.append((w, full, (0, 128), (at, half_hidden), at))
+    w, full, _, (at, size), _ = pieces.pop()
+    first = (size // 2 + 127) // 128 * 128
+    pieces.append((w, full, (0, 128), (at, first), at))
+    pieces.append((w, full, (0, 128), (at + first, size - first), at + first))
     count = len(pieces)
     parity = place.z % 2
 
@@ -948,8 +952,8 @@
         + table_scratch(rows)
         + [pltpu.VMEM((width, rows), BF16)] * 4
         + scan_scratch()
-        + [pltpu.SemaphoreType.DMA((121,))] * 2
-        + [pltpu.SemaphoreType.DMA((11,)), pltpu.SemaphoreType.DMA((28,))]
+        + [pltpu.SemaphoreType.DMA((132,))] * 2
+        + [pltpu.SemaphoreType.DMA((12,)), pltpu.SemaphoreType.DMA((29,))]
         + [pltpu.SemaphoreType.DMA((13,))] * 2
     )
     return pl.pallas_call(
@@ -986,7 +990,7 @@
 
 UPRIGHT = 256
 LAG = 2
-WITH_UPRIGHT = (0, 1, 2, 3, 10, 11, 12, 13)
+WITH_UPRIGHT = (0, 1, 2, 3, 4, 8, 9, 10, 11, 12, 13)
 LAST = 1024
 
 

time: 258 us -> 255 us (0.988)
  Pallas kernels: 257 us -> 254 us
where the time goes in v6:
time: 255 us
  Pallas kernels  254 us (100%)
    pallas_call x1, Pallas kernels, run_backward(): pl.pallas_call(backward_kernel, out_shape=outs, in_specs=[SMEM, SMEM] + [...  138 us
    pallas_call x1, Pallas kernels, run_forward(): pl.pallas_call(forward_kernel, out_shape=outs, in_specs=[SMEM, SMEM] + [V...  114 us

profile of v6, /device:TPU:0, one launch (start us, length us, event | category | flops | bytes accessed | tf_op | source)
XLA Modules:
  0.0 255.3 jit_solution(1403166252668344586)
XLA Ops:
  0.6 113.6 %forward.1 = (bf16[1024,4096]{1,0:T(8,128)(2,1)}, bf16[1024,1024]{1,0:T(8,128)(2,1)}, bf16[1024,2816]{1,0:T(8,128)(2,1)}, bf16[1024,2816]{1,0:T(8,128)(2,1)}, bf...) custom-call(s32[2,8]{1,0:T(2,128)} %lengths.3, ...), custom_call_target="tpu_custom_call" | custom-call | tf_op jit(solution)/shard_map/forward/pallas_call | solution.py:959
  114.3 137.5 %backward.1 = (bf16[512,1024]{1,0:T(8,128)(2,1)}, bf16[512,1024]{1,0:T(8,128)(2,1)}, f32[32,1024]{1,0:T(8,128)}, f32[32,1024]{1,0:T(8,128)}, f32[32,1024]{1,0:T(...) custom-call(s32[2,8]{1,0:T(2,128)} %lengths.3, ...), custom_call_target="tpu_custom_call" | custom-call | tf_op jit(solution)/shard_map/backward/pallas_call | solution.py:1493
  251.8 3.3 %hand_over.1 = (bf16[512,1024]{1,0:T(8,128)(2,1)}, bf16[512,1024]{1,0:T(8,128)(2,1)}, f32[32,1024]{1,0:T(8,128)}, f32[32,1024]{1,0:T(8,128)}, f32[32,1024]{1,0:T...) custom-call(bf16[512,1024]{1,0:T(8,128)(2,1)} %get-tuple-element.74., ...), custom_call_target="tpu_custom_call" | custom-call | tf_op jit(solution)/shard_map/hand_over/pallas_call | solution.py:1527

commit v7 on v6

--- a/solution.py
+++ b/solution.py
@@ -1138,7 +1138,7 @@
                 r = i * 32
                 merged[m, i // 8, i // 4 % 2, i // 2 % 2, i % 2, :, at] = value[r : r + 32]
 
-        for t in of(n, 1, 2, 7):
+        for t in of(n, 7, 1, 2):
             go(n, t)
 
     def add(a, b):

time: 255 us -> 255 us (level)
  no operation moved by 1% of the time
where the time goes in v7:
time: 255 us
  Pallas kernels  254 us (100%)
    pallas_call x1, Pallas kernels, run_backward(): pl.pallas_call(backward_kernel, out_shape=outs, in_specs=[SMEM, SMEM] + [...  137 us
    pallas_call x1, Pallas kernels, run_forward(): pl.pallas_call(forward_kernel, out_shape=outs, in_specs=[SMEM, SMEM] + [V...  114 us

profile of v7, /device:TPU:0, one launch (start us, length us, event | category | flops | bytes accessed | tf_op | source)
XLA Modules:
  0.0 254.9 jit_solution(11758543203442322405)
XLA Ops:
  0.6 113.6 %forward.1 = (bf16[1024,4096]{1,0:T(8,128)(2,1)}, bf16[1024,1024]{1,0:T(8,128)(2,1)}, bf16[1024,2816]{1,0:T(8,128)(2,1)}, bf16[1024,2816]{1,0:T(8,128)(2,1)}, bf...) custom-call(s32[2,8]{1,0:T(2,128)} %lengths.3, ...), custom_call_target="tpu_custom_call" | custom-call | tf_op jit(solution)/shard_map/forward/pallas_call | solution.py:959
  114.3 137.2 %backward.1 = (bf16[512,1024]{1,0:T(8,128)(2,1)}, bf16[512,1024]{1,0:T(8,128)(2,1)}, f32[32,1024]{1,0:T(8,128)}, f32[32,1024]{1,0:T(8,128)}, f32[32,1024]{1,0:T(...) custom-call(s32[2,8]{1,0:T(2,128)} %lengths.3, ...), custom_call_target="tpu_custom_call" | custom-call | tf_op jit(solution)/shard_map/backward/pallas_call | solution.py:1493
  251.5 3.3 %hand_over.1 = (bf16[512,1024]{1,0:T(8,128)(2,1)}, bf16[512,1024]{1,0:T(8,128)(2,1)}, f32[32,1024]{1,0:T(8,128)}, f32[32,1024]{1,0:T(8,128)}, f32[32,1024]{1,0:T...) custom-call(bf16[512,1024]{1,0:T(8,128)(2,1)} %get-tuple-element.74., ...), custom_call_target="tpu_custom_call" | custom-call | tf_op jit(solution)/shard_map/hand_over/pallas_call | solution.py:1527
